TPU v7x, 128 devices: a whole 4x4x4 slice. The times are simulated.
128 devices in a mesh: rep: 16 (over y_hi, x, core), shard: 8 (over y_lo, z).
Axes of the slice: x: 4, y: 4 (y_hi: 2, y_lo: 2; y = y_hi * 2 + y_lo), z: 4, core: 2. Of those that a mesh axis runs over, the one named last changes fastest.
Arguments:
- tokens: bfloat16 [16384, 2048], P(('rep', 'shard')), may hold values from -6 to 6
- cotangent: float32 [16384, 2048], P(('rep', 'shard')), may hold values from -6 to 6
- lengths: int32 [16, 3], P('rep'), may hold values from 1 to 1022, as said below
- attn_gain: bfloat16 [2048], P('shard'), may hold values from 0.5 to 1.5
- mlp_gain: bfloat16 [2048], P('shard'), may hold values from 0.5 to 1.5
- query_gain: bfloat16 [128], replicated, may hold values from 0.796875 to 1.59375
- key_gain: bfloat16 [128], replicated, may hold values from 0.796875 to 1.59375
- w_query: bfloat16 [2048, 2048], P('shard'), may hold values from -0.125 to 0.125
- w_key: bfloat16 [2048, 1024], P('shard'), may hold values from -0.125 to 0.125
- w_value: bfloat16 [2048, 1024], P('shard'), may hold values from -0.125 to 0.125
- w_out: bfloat16 [2048, 2048], P('shard'), may hold values from -1 to 1
- w_gate: bfloat16 [6144, 2048], P('shard'), may hold values from -0.125 to 0.125
- w_up: bfloat16 [6144, 2048], P('shard'), may hold values from -0.125 to 0.125
- w_down: bfloat16 [6144, 2048], P('shard'), may hold values from -0.078125 to 0.078125
Outputs:
- result: float32 [16384, 2048], P(('rep', 'shard'))
- grad_tokens: float32 [16384, 2048], P(('rep', 'shard'))
- grad_w_query: float32 [2048, 2048], P('shard')
- grad_w_key: float32 [2048, 1024], P('shard')
- grad_w_value: float32 [2048, 1024], P('shard')
- grad_w_out: float32 [2048, 2048], P('shard')
- grad_w_gate: float32 [6144, 2048], P('shard')
- grad_w_up: float32 [6144, 2048], P('shard')
- grad_w_down: float32 [6144, 2048], P('shard')
- grad_attn_gain: float32 [2048], P('shard')
- grad_mlp_gain: float32 [2048], P('shard')
- grad_query_gain: float32 [128], P('shard')
- grad_key_gain: float32 [128], P('shard')
Inputs may be any that keep to these rules, and one draw needn't show every extreme that they name: Row r holds, in order, the lengths of the three sequences of replica r; they sum to 1024, and the first and the last are each at most 127.
All inputs are finite; a program needn't handle non-finite values.
Results may differ from a plain program's by a relative error of at most 0.025.
Values may be sent and summed in bfloat16 or wider, within the bound.
A program may use at most 512 MiB of HBM per device.

v0:
```python
import math

import jax
import jax.numpy as jnp
from jax import lax
from jax.sharding import PartitionSpec as P

HEADS = 16
KV_HEADS = 8
HEAD_DIM = 128


epsilon = 1e-06
theta_base = 1000000.0
masked_value = -1e30


def rms_scale(values, gain):
    return values * lax.rsqrt(jnp.mean(values * values, axis=-1, keepdims=True) + epsilon) * gain


def rotate(values, positions):
    half_dim = values.shape[-1] // 2
    frequency = theta_base ** (-jnp.arange(half_dim, dtype=jnp.float32) * (2.0 / values.shape[-1]))
    angles = positions.astype(jnp.float32)[:, None] * frequency[None, :]
    cosine = jnp.cos(angles)[:, None, :]
    sine = jnp.sin(angles)[:, None, :]
    first_half = values[..., :half_dim]
    second_half = values[..., half_dim:]
    return jnp.concatenate(
        [first_half * cosine - second_half * sine, second_half * cosine + first_half * sine],
        axis=-1,
    )


def segment_info(lengths_row, indices):
    start_one = lengths_row[0]
    start_two = lengths_row[0] + lengths_row[1]
    segment = (indices >= start_one).astype(jnp.int32) + (indices >= start_two).astype(jnp.int32)
    begin = jnp.where(segment == 0, 0, jnp.where(segment == 1, start_one, start_two))
    return (segment, indices - begin)


def contract_rows(left, right):
    return lax.dot_general(
        left, right, (((1,), (1,)), ((), ())), preferred_element_type=jnp.float32
    )


def contract_first(left, right):
    return lax.dot_general(
        left, right, (((0,), (0,)), ((), ())), preferred_element_type=jnp.float32
    )


def per_device(
    tokens,
    cotangent,
    lengths,
    attn_gain,
    mlp_gain,
    query_gain,
    key_gain,
    w_query,
    w_key,
    w_value,
    w_out,
    w_gate,
    w_up,
    w_down,
):
    tok_rows = tokens.shape[0]
    shards = lax.axis_size("shard")
    group_rows = tok_rows * shards
    width = tokens.shape[1]
    q_width = w_query.shape[1]
    kv_width = w_key.shape[1]
    head_dim = HEAD_DIM
    head_count = HEADS
    kv_count = KV_HEADS
    group_size = head_count // kv_count
    scale = 1.0 / math.sqrt(head_dim)
    my_shard = lax.axis_index("shard")
    query_index = my_shard * tok_rows + jnp.arange(tok_rows, dtype=jnp.int32)
    key_index = jnp.arange(group_rows, dtype=jnp.int32)
    query_segment, query_position = segment_info(lengths[0], query_index)
    key_segment = segment_info(lengths[0], key_index)[0]
    visible = (query_segment[:, None] == key_segment[None, :]) & (
        key_index[None, :] <= query_index[:, None]
    )
    inputs = tokens.astype(jnp.float32)
    normed = inputs * lax.rsqrt(jnp.mean(inputs * inputs, axis=-1, keepdims=True) + epsilon)
    piece_one = lax.all_gather(attn_gain, "shard", axis=0, tiled=True)
    piece_two = lax.all_gather(mlp_gain, "shard", axis=0, tiled=True)
    query_part = lax.all_gather(w_query, "shard", axis=0, tiled=True)
    key_part = lax.all_gather(w_key, "shard", axis=0, tiled=True)
    value_part = lax.all_gather(w_value, "shard", axis=0, tiled=True)
    out_part = lax.all_gather(w_out, "shard", axis=0, tiled=True)
    count = query_part.shape[0]
    columns = (normed * piece_one.astype(jnp.float32)).astype(jnp.bfloat16)
    q_sum = jnp.dot(columns, query_part, preferred_element_type=jnp.float32)
    k_sum = jnp.dot(columns, key_part, preferred_element_type=jnp.float32)
    v_sum = jnp.dot(columns, value_part, preferred_element_type=jnp.float32)

    def prepare(projected, gain, count):
        return rotate(rms_scale(projected.reshape(tok_rows, count, head_dim), gain), query_position)

    q_rot, query_back = jax.vjp(
        lambda projected, gain: prepare(projected, gain, head_count),
        q_sum,
        query_gain.astype(jnp.float32),
    )
    k_rot, key_back = jax.vjp(
        lambda projected, gain: prepare(projected, gain, kv_count),
        k_sum,
        key_gain.astype(jnp.float32),
    )
    query_low = q_rot.astype(jnp.bfloat16).reshape(tok_rows, kv_count, group_size, head_dim)
    key_low = k_rot.astype(jnp.bfloat16).reshape(tok_rows, kv_width)
    value_low = v_sum.astype(jnp.bfloat16)
    keys_all, values_all = (
        lax.all_gather(key_low, "shard", axis=0, tiled=True),
        lax.all_gather(value_low, "shard", axis=0, tiled=True),
    )
    key_heads = keys_all.reshape(group_rows, kv_count, head_dim)
    value_heads = values_all.reshape(group_rows, kv_count, head_dim)
    scores = (
        jnp.einsum("tkgd,skd->kgts", query_low, key_heads, preferred_element_type=jnp.float32)
        * scale
    )
    masked = jnp.where(visible[None, None], scores, masked_value)
    top = jnp.max(masked, axis=-1, keepdims=True)
    total = jnp.log(jnp.sum(jnp.exp(masked - top), axis=-1, keepdims=True)) + top
    probs = jnp.exp(masked - total).astype(jnp.bfloat16)
    mixed = jnp.einsum("kgts,skd->tkgd", probs, value_heads, preferred_element_type=jnp.float32)
    attended = mixed.reshape(tok_rows, q_width).astype(jnp.bfloat16)
    resid = inputs + contract_rows(attended, out_part)
    second_value, second_back = jax.vjp(rms_scale, resid, piece_two.astype(jnp.float32))
    second_low = second_value.astype(jnp.bfloat16)
    grad_low = cotangent.astype(jnp.bfloat16)
    gate_part = lax.all_gather(w_gate, "shard", axis=0, tiled=True)
    up_part = lax.all_gather(w_up, "shard", axis=0, tiled=True)
    down_part = lax.all_gather(w_down, "shard", axis=0, tiled=True)
    gate_cols = contract_rows(second_low, gate_part)
    up_cols = contract_rows(second_low, up_part)
    hidden_cols = (jax.nn.silu(gate_cols) * up_cols).astype(jnp.bfloat16)
    out_sum = jnp.dot(hidden_cols, down_part, preferred_element_type=jnp.float32)
    take_gate_all = gate_cols
    take_up_all = up_cols
    gate_part = lax.all_gather(w_gate, "shard", axis=0, tiled=True)
    up_part = lax.all_gather(w_up, "shard", axis=0, tiled=True)
    down_part = lax.all_gather(w_down, "shard", axis=0, tiled=True)
    count = gate_part.shape[0]
    dhidden = contract_rows(grad_low, down_part)
    gate_cols = take_gate_all
    up_cols = take_up_all
    sigma = jax.nn.sigmoid(gate_cols)
    dgate_cols = (dhidden * up_cols * sigma * (1.0 + gate_cols * (1.0 - sigma))).astype(
        jnp.bfloat16
    )
    dup_cols = (dhidden * gate_cols * sigma).astype(jnp.bfloat16)
    dsecond = jnp.dot(dgate_cols, gate_part, preferred_element_type=jnp.float32)
    dsecond = dsecond + jnp.dot(dup_cols, up_part, preferred_element_type=jnp.float32)
    ffn_grads = lax.psum_scatter(
        jnp.concatenate(
            [
                contract_first(dgate_cols, second_low),
                contract_first(dup_cols, second_low),
                contract_first(hidden_cols, grad_low),
            ],
            axis=1,
        ).astype(jnp.bfloat16),
        "shard",
        scatter_dimension=0,
        tiled=True,
    ).astype(jnp.float32)
    grad_gate = ffn_grads[:, :width]
    grad_up = ffn_grads[:, width : 2 * width]
    grad_down = ffn_grads[:, 2 * width :]
    result = resid + out_sum
    grad_resid_part, grad_second_gain = second_back(dsecond)
    grad_resid = cotangent + grad_resid_part
    grad_branch = grad_resid.astype(jnp.bfloat16)
    query_full, key_full, value_full, out_again = (
        lax.all_gather(w_query, "shard", axis=0, tiled=True),
        lax.all_gather(w_key, "shard", axis=0, tiled=True),
        lax.all_gather(w_value, "shard", axis=0, tiled=True),
        lax.all_gather(w_out, "shard", axis=0, tiled=True),
    )
    grad_att = jnp.dot(grad_branch, out_again, preferred_element_type=jnp.float32).astype(
        jnp.bfloat16
    )
    grad_heads = grad_att.reshape(tok_rows, kv_count, group_size, head_dim)
    scores_again = (
        jnp.einsum("tkgd,skd->kgts", query_low, key_heads, preferred_element_type=jnp.float32)
        * scale
    )
    weights_again = jnp.exp(jnp.where(visible[None, None], scores_again, masked_value) - total)
    dprobs = jnp.einsum(
        "tkgd,skd->kgts", grad_heads, value_heads, preferred_element_type=jnp.float32
    )
    inner = jnp.sum(weights_again * dprobs, axis=-1, keepdims=True)
    dscores = (weights_again * (dprobs - inner)).astype(jnp.bfloat16)
    dquery = (
        jnp.einsum("kgts,skd->tkgd", dscores, key_heads, preferred_element_type=jnp.float32) * scale
    )
    dkeys_all = (
        jnp.einsum("kgts,tkgd->skd", dscores, query_low, preferred_element_type=jnp.float32) * scale
    )
    dvalues_all = jnp.einsum(
        "kgts,tkgd->skd",
        weights_again.astype(jnp.bfloat16),
        grad_heads,
        preferred_element_type=jnp.float32,
    )
    dkeys_own, dvalues_own = (
        lax.psum_scatter(
            dkeys_all.reshape(group_rows, kv_width).astype(jnp.bfloat16),
            "shard",
            scatter_dimension=0,
            tiled=True,
        ).astype(jnp.float32),
        lax.psum_scatter(
            dvalues_all.reshape(group_rows, kv_width).astype(jnp.bfloat16),
            "shard",
            scatter_dimension=0,
            tiled=True,
        ).astype(jnp.float32),
    )
    dq_proj, grad_query_part = query_back(dquery.reshape(tok_rows, head_count, head_dim))
    dk_proj, grad_key_part = key_back(dkeys_own.reshape(tok_rows, kv_count, head_dim))
    dq_low = dq_proj.astype(jnp.bfloat16)
    dk_low = dk_proj.astype(jnp.bfloat16)
    dv_low = dvalues_own.astype(jnp.bfloat16)
    grad_first = (
        contract_rows(dq_low, query_full)
        + contract_rows(dk_low, key_full)
        + contract_rows(dv_low, value_full)
    )
    attn_grads = lax.psum_scatter(
        jnp.concatenate(
            [
                contract_first(columns, dq_low),
                contract_first(columns, dk_low),
                contract_first(columns, dv_low),
                contract_first(grad_branch, attended),
            ],
            axis=1,
        ).astype(jnp.bfloat16),
        "shard",
        scatter_dimension=0,
        tiled=True,
    ).astype(jnp.float32)
    grad_query = attn_grads[:, :q_width]
    grad_key = attn_grads[:, q_width : q_width + kv_width]
    grad_value = attn_grads[:, q_width + kv_width : q_width + 2 * kv_width]
    grad_out = attn_grads[:, q_width + 2 * kv_width :]
    first_back = jax.vjp(rms_scale, inputs, piece_one.astype(jnp.float32))[1]
    grad_input_part, grad_first_gain = first_back(grad_first)
    grad_tokens = grad_resid + grad_input_part
    gains_first, gains_second, gains_query, gains_key = lax.psum(
        (grad_first_gain, grad_second_gain, grad_query_part, grad_key_part), ("rep", "shard")
    )
    width_piece = width // shards
    head_piece = head_dim // shards
    gains_first = lax.dynamic_slice_in_dim(gains_first, my_shard * width_piece, width_piece, 0)
    gains_second = lax.dynamic_slice_in_dim(gains_second, my_shard * width_piece, width_piece, 0)
    gains_query = lax.dynamic_slice_in_dim(gains_query, my_shard * head_piece, head_piece, 0)
    gains_key = lax.dynamic_slice_in_dim(gains_key, my_shard * head_piece, head_piece, 0)
    summed = (
        lax.psum(grad_query.astype(jnp.bfloat16), "rep").astype(jnp.float32),
        lax.psum(grad_key.astype(jnp.bfloat16), "rep").astype(jnp.float32),
        lax.psum(grad_value.astype(jnp.bfloat16), "rep").astype(jnp.float32),
        lax.psum(grad_out.astype(jnp.bfloat16), "rep").astype(jnp.float32),
        lax.psum(grad_gate.astype(jnp.bfloat16), "rep").astype(jnp.float32),
        lax.psum(grad_up.astype(jnp.bfloat16), "rep").astype(jnp.float32),
        lax.psum(grad_down.astype(jnp.bfloat16), "rep").astype(jnp.float32),
    )
    return (
        result,
        grad_tokens,
        summed[0],
        summed[1],
        summed[2],
        summed[3],
        summed[4],
        summed[5],
        summed[6],
        gains_first,
        gains_second,
        gains_query,
        gains_key,
    )


def solution(mesh):
    placed = (
        P(("rep", "shard"), None),
        P(("rep", "shard"), None),
        P("rep", None),
        P("shard"),
        P("shard"),
        P(),
        P(),
        P("shard", None),
        P("shard", None),
        P("shard", None),
        P("shard", None),
        P("shard", None),
        P("shard", None),
        P("shard", None),
    )
    return jax.shard_map(
        per_device,
        mesh=mesh,
        in_specs=placed,
        out_specs=(
            P(("rep", "shard"), None),
            P(("rep", "shard"), None),
            P("shard", None),
            P("shard", None),
            P("shard", None),
            P("shard", None),
            P("shard", None),
            P("shard", None),
            P("shard", None),
            P("shard"),
            P("shard"),
            P("shard"),
            P("shard"),
        ),
        check_vma=False,
    )
```

profile of v0, /device:TPU:1, one launch (start us, length us, event | category | flops | bytes accessed | tf_op | source)
XLA Modules:
  0.0 2500.2 jit_solution(160606535998352789)
XLA Ops:
  9.4 17.6 all-gather
  28.3 37.5 %all-gather.12.cloned.1.call-done = bf16[2048,1024]{1,0:T(8,128)(2,1)} async-done(((bf16[256,1024]{1,0:T(8,128)(2,1)}), bf16[2048,1024]{1,0:T(8,128)(2,1)}) %all-gather.12.cloned.1.call-update) | async-done | bytes 4194320 | tf_op jit(solution)/shard_map/all_gather | solution.py:97
  65.7 3.8 convolution_convert_fusion.8
  74.5 44.3 %all-gather.16.cloned.1.call-done = bf16[2048,1024]{1,0:T(8,128)(2,1)} async-done(((bf16[256,1024]{1,0:T(8,128)(2,1)}), bf16[2048,1024]{1,0:T(8,128)(2,1)}) %all-gather.16.cloned.1.call-update) | async-done | bytes 4194320 | tf_op jit(solution)/shard_map/all_gather | solution.py:96
  127.3 13.8 all-gather.1
  142.7 13.2 all-gather.14.cloned.1.call-done
  155.8 3.5 copy.182
  159.4 94.9 %all-gather.20.cloned.1.call-done = bf16[2048,2048]{1,0:T(8,128)(2,1)} async-done(((bf16[256,2048]{1,0:T(8,128)(2,1)}), bf16[2048,2048]{1,0:T(8,128)(2,1)}) %all-gather.20.cloned.1.call-update) | async-done | bytes 8388624 | tf_op jit(solution)/shard_map/all_gather | solution.py:95
  254.3 4.7 convolution_bitcast_fusion
  262.0 34.1 %all-gather.18.cloned.1.call-done = bf16[1024,1024]{0,1:T(8,128)(2,1)} async-done(((bf16[128,1024]{0,1:T(8,128)(2,1)}), bf16[1024,1024]{0,1:T(8,128)(2,1)}) %all-gather.18.cloned.1.call-update) | async-done | bytes 2097168 | tf_op jit(solution)/shard_map/all_gather | solution.py:122
  296.1 3.6 fusion.4
  306.1 89.0 %all-gather.22.cloned.1.call-done = bf16[2048,2048]{1,0:T(8,128)(2,1)} async-done(((bf16[256,2048]{1,0:T(8,128)(2,1)}), bf16[2048,2048]{1,0:T(8,128)(2,1)}) %all-gather.22.cloned.1.call-update) | async-done | bytes 8388624 | tf_op jit(solution)/shard_map/all_gather | solution.py:98
  395.1 6.5 multiply_reduce_fusion.4
  403.7 241.2 %all-gather.26.cloned.1.call-done = bf16[6144,2048]{1,0:T(8,128)(2,1)} async-done(((bf16[768,2048]{1,0:T(8,128)(2,1)}), bf16[6144,2048]{1,0:T(8,128)(2,1)}) %all-gather.26.cloned.1.call-update) | async-done | bytes 25165840 | tf_op jit(solution)/shard_map/all_gather | solution.py:142
  644.8 14.5 fusion.67
  659.3 235.2 %all-gather.24.cloned.1.call-done = bf16[6144,2048]{1,0:T(8,128)(2,1)} async-done(((bf16[768,2048]{1,0:T(8,128)(2,1)}), bf16[6144,2048]{1,0:T(8,128)(2,1)}) %all-gather.24.cloned.1.call-update) | async-done | bytes 25165840 | tf_op jit(solution)/shard_map/all_gather | solution.py:141
  894.6 14.3 fusion.66
  908.9 235.4 %all-gather.28.cloned.1.call-done = bf16[6144,2048]{1,0:T(8,128)(2,1)} async-done(((bf16[768,2048]{1,0:T(8,128)(2,1)}), bf16[6144,2048]{1,0:T(8,128)(2,1)}) %all-gather.28.cloned.1.call-update) | async-done | bytes 25165840 | tf_op jit(solution)/shard_map/all_gather | solution.py:143
  1144.3 15.8 multiply_convert_fusion
  1160.1 11.1 fusion.68
  1171.3 11.2 multiply_reduce_fusion.1
  1185.5 6.0 fusion
  1191.5 5.1 fusion.2
  1198.6 3.1 fusion.5
  1201.7 3.9 copy.173
  1205.7 7.1 bitcast_convert_fusion
  1212.8 4.0 copy.175
  1217.3 3.6 convolution_multiply_fusion
  1233.5 5.7 convolution_convert_fusion.4
  1239.3 5.6 convolution_convert_fusion.3
  1251.1 3.4 convolution_convert_fusion.6
  1254.4 32.0 %reduce-scatter.15.cloned.1.call-done = bf16[128,1024]{1,0:T(8,128)(2,1)} async-done(((bf16[1024,1024]{1,0:T(8,128)(2,1)}), bf16[128,1024]{1,0:T(8,128)(2,1)}) %reduce-scatter.15.cloned.1.call-update) | async-done | bytes 262160
  1286.4 4.3 convolution_convert_fusion.5
  1290.7 18.0 pad_maximum_fusion.1
  1309.8 14.0 convolution_convert_fusion.1
  1323.8 13.3 convolution_convert_fusion.2
  1337.0 13.4 convolution_convert_fusion
  1350.5 51.6 %pad_maximum_fusion = bf16[6144,6144]{0,1:T(8,128)(2,1)} fusion(bf16[6144,2048]{0,1:T(8,128)(2,1)} %convolution_convert_fusion, bf16[6144,2048]{0,1:T(8,128)(2,1)} %convolution_convert_fusion.1, bf16[6144,2048]{0,1:T(8,128)(2,1)} %convolution_convert_fusion.2), kind=kLoop, calls=%fused_computation | loop fusion | flops 226492416 | bytes 150994944 | tf_op jit(solution)/shard_map/concatenate | solution.py:165
  1402.4 161.0 %reduce-scatter.9.cloned.1.call-done = bf16[256,6144]{0,1:T(8,128)(2,1)} async-done(((bf16[2048,6144]{0,1:T(8,128)(2,1)}), bf16[256,6144]{0,1:T(8,128)(2,1)}) %reduce-scatter.9.cloned.1.call-update) | async-done | bytes 3145744 | tf_op jit(solution)/shard_map/reduce_scatter | solution.py:240
  1568.6 718.1 %reduce-scatter.11.cloned.1.call-done = bf16[768,6144]{0,1:T(8,128)(2,1)} async-done(((bf16[6144,6144]{0,1:T(8,128)(2,1)}), bf16[768,6144]{0,1:T(8,128)(2,1)}) %reduce-scatter.11.cloned.1.call-update) | async-done | bytes 9437200 | tf_op jit(solution)/shard_map/reduce_scatter | solution.py:164
  2286.7 6.7 fusion.60
  2294.4 6.4 fusion.24
  2300.8 11.7 convolution_add_fusion.3
  2316.7 71.3 %all-reduce.4 = (f32[2048]{0:T(1024)S(1)}, f32[2048]{0:T(1024)S(1)}, f32[128]{0:T(128)S(1)}, f32[128]{0:T(128)S(1)}) all-reduce(f32[2048]{0:T(1024)S(1)} %get-tuple-element.82, f32[2048]{0:T(1024)S(1)} %copy-done.35, f32[128]{0:T(128)S(1)} %copy-done.41, f32[128]{0:T(128)S(1)} %copy-done.42), channel_id=1, replica_groups=mesh['rep'=16,'shard'=8] {'rep','shard'}, use_global_device_ids=true, to_apply=%region_23.24 | all-reduce | flops 4352 | bytes 34816 | tf_op jit(solution)/shard_map/psum | solution.py:261
  2393.0 76.4 %all-reduce.8.cloned.1.call-done = (bf16[256,2048]{0,1:T(8,128)(2,1)}, bf16[256,1024]{0,1:T(8,128)(2,1)}, bf16[256,1024]{0,1:T(8,128)(2,1)}, bf16[256,2048]{0,1:...) async-done(((bf16[256,2048]{0,1:T(8,128)(2,1)}, bf16[256,1024]{0,1:T(8,128)(2,1)}, bf16[256,1024]{0,1:T(8,128)(2,1)}, ...) | async-done | bytes 12582928 | tf_op jit(solution)/shard_map/psum | solution.py:271
  2479.0 5.5 copy.153
  2484.5 5.4 copy.154
  2489.9 3.6 copy.155
  (208 shorter events, 78.5 us)
Async XLA Ops:
  7.2 111.7 %copy-start.1 = (bf16[128,2048]{1,0:T(8,128)(2,1)S(1)}, bf16[128,2048]{1,0:T(8,128)(2,1)}, u32[]{:S(2)}) copy-start(bf16[128,2048]{1,0:T(8,128)(2,1)} %param.14) | copy-start | bytes 1572868
  7.2 58.6 %all-gather.12.cloned.1.call-start = ((), (), s32[]{:S(2)}) async-start(), calls=%async_computation.4 | async-start | bytes 4718592 | tf_op jit(solution)/shard_map/all_gather | solution.py:97
  7.9 110.9 %all-gather.16.cloned.1.call-start = ((), (), s32[]{:S(2)}) async-start(), calls=%async_computation.6 | async-start | bytes 4718592 | tf_op jit(solution)/shard_map/all_gather | solution.py:96
  8.7 147.1 %all-gather.14.cloned.1.call-start = ((), (), s32[]{:S(2)}) async-start(), calls=%async_computation.5 | async-start | bytes 2359296 | tf_op jit(solution)/shard_map/all_gather | solution.py:123
  28.2 46.3 %copy-start.43 = (f32[128]{0:T(128)}, f32[128]{0:T(128)S(1)}, u32[]{:S(2)}) copy-start(f32[128]{0:T(128)S(1)} %fusion.20) | copy-start | bytes 1540
  28.2 226.0 %copy-start.31 = (f32[128]{0:T(128)}, f32[128]{0:T(128)S(1)}, u32[]{:S(2)}) copy-start(f32[128]{0:T(128)S(1)} %fusion.46) | copy-start | bytes 1540
  69.6 184.7 %all-gather.20.cloned.1.call-start = ((), (), s32[]{:S(2)}) async-start(), calls=%async_computation.8 | async-start | bytes 9437184 | tf_op jit(solution)/shard_map/all_gather | solution.py:95
  70.2 226.0 %all-gather.18.cloned.1.call-start = ((), (), s32[]{:S(2)}) async-start(), calls=%async_computation.7 | async-start | bytes 2359296 | tf_op jit(solution)/shard_map/all_gather | solution.py:122
  70.9 55.1 %copy-start.39 = (f32[128]{0:T(128)}, f32[128]{0:T(128)S(1)}, u32[]{:S(2)}) copy-start(f32[128]{0:T(128)S(1)} %convert_element_type.181) | copy-start | bytes 1540
  121.8 5.5 copy-start.48
  122.2 20.3 copy-start.33
  123.9 271.2 %all-gather.22.cloned.1.call-start = ((), (), s32[]{:S(2)}) async-start(), calls=%async_computation.9 | async-start | bytes 9437184 | tf_op jit(solution)/shard_map/all_gather | solution.py:98
  124.5 520.4 %all-gather.26.cloned.1.call-start = ((), (), s32[]{:S(2)}) async-start(), calls=%async_computation.11 | async-start | bytes 28311552 | tf_op jit(solution)/shard_map/all_gather | solution.py:142
  125.2 769.3 %all-gather.24.cloned.1.call-start = ((), (), s32[]{:S(2)}) async-start(), calls=%async_computation.10 | async-start | bytes 28311552 | tf_op jit(solution)/shard_map/all_gather | solution.py:141
  126.0 1018.3 %all-gather.28.cloned.1.call-start = ((), (), s32[]{:S(2)}) async-start(), calls=%async_computation.12 | async-start | bytes 28311552 | tf_op jit(solution)/shard_map/all_gather | solution.py:143
  126.7 1118.2 %reduce-scatter.13.cloned.1.call-start = ((), (), s32[]{:S(2)}) async-start(), calls=%async_computation.15 | async-start | bytes 2359296
  261.9 39.6 %copy-start.16 = (bf16[128,16,64]{2,0,1:T(8,128)(2,1)}, bf16[128,16,64]{2,0,1:T(8,128)(2,1)S(1)}, u32[]{:S(2)}) copy-start(bf16[128,16,64]{2,0,1:T(8,128)(2,1)S(1)} %copy.129) | copy-start | bytes 786436
  262.0 39.5 %copy-start.18 = (bf16[128,16,64]{2,0,1:T(8,128)(2,1)}, bf16[128,16,64]{2,0,1:T(8,128)(2,1)S(1)}, u32[]{:S(2)}) copy-start(bf16[128,16,64]{2,0,1:T(8,128)(2,1)S(1)} %copy.130) | copy-start | bytes 786436
  296.1 6.9 copy-start.10
  401.7 780.9 %copy-start.3 = (f32[128,2048]{1,0:T(8,128)}, f32[128,2048]{1,0:T(8,128)S(1)}, u32[]{:S(2)}) copy-start(f32[128,2048]{1,0:T(8,128)S(1)} %get-tuple-element.126) | copy-start | bytes 3145732
  1160.1 11.2 copy-start.12
  1160.1 11.2 copy-start.13
  1160.1 11.2 copy-start.38
  1160.1 23.7 slice-start
  1171.3 11.2 copy-start.46
  1171.3 11.3 copy-start.22
  1171.3 12.5 slice-start.1
  1185.4 6.0 copy-start.24
  1191.5 7.1 copy-start.17
  1191.5 7.1 copy-start.19
  1205.6 80.8 %reduce-scatter.15.cloned.1.call-start = ((), (), s32[]{:S(2)}) async-start(), calls=%async_computation.16 | async-start | bytes 2359296
  1216.8 11.8 copy-start.36
  1216.8 346.6 %reduce-scatter.9.cloned.1.call-start = ((), (), s32[]{:S(2)}) async-start(), calls=%async_computation.13 | async-start | bytes 28311552 | tf_op jit(solution)/shard_map/reduce_scatter | solution.py:240
  1220.9 9.3 copy-start.30
  1222.0 11.6 copy-start.32
  1230.1 9.1 copy-start.6
  1230.3 8.9 copy-start.23
  1239.3 10.1 copy-start.40
  1239.3 11.2 copy-start.34
  1308.8 977.9 %reduce-scatter.11.cloned.1.call-start = ((), (), s32[]{:S(2)}) async-start(), calls=%async_computation.14 | async-start | bytes 84934656 | tf_op jit(solution)/shard_map/reduce_scatter | solution.py:164
  1402.1 1067.3 %all-reduce.8.cloned.1.call-start = ((), (), s32[]{:S(2)}) async-start(), calls=%async_computation.17 | async-start | bytes 25165824 | tf_op jit(solution)/shard_map/psum | solution.py:271
  2293.4 7.4 copy-start.4
  2294.4 6.4 copy-start.11
  2300.8 11.7 copy-start.8
  2300.8 13.2 copy-start.7
  2300.8 13.2 copy-start.26
  2312.5 78.0 %copy-start.44 = (f32[128]{0:T(128)S(1)}, f32[128]{0:T(128)}, u32[]{:S(2)}) copy-start(f32[128]{0:T(128)} %copy-done.43) | copy-start | bytes 1540
  2479.0 10.9 copy-start.25
  (17 other events, 37.6 us)
Sparse Core Ops, SparseCore 0:
  9.7 56.0 all-gather.11
  67.4 51.4 all-gather.15
  121.1 34.7 all-gather.13
  157.3 96.9 all-gather.19
  256.3 39.8 all-gather.17
  297.6 97.4 all-gather.21
  396.8 248.0 all-gather.25
  646.5 248.0 all-gather.23
  896.2 248.0 all-gather.27
  1205.8 36.1 reduce-scatter.12
  1245.0 41.3 reduce-scatter.14
  1308.9 254.4 reduce-scatter.8
  1565.9 720.7 reduce-scatter.10
  2293.5 175.8 all-reduce.7
where the time goes:
time: 2510 us; the launch traced here: 2500 us
  waiting for transfers between devices  2020 us (80%)
  matrix products  195 us (8%)
  blocking collectives  103 us (4%)
  other arithmetic  96.3 us (4%)
  local copies, waits for them, and re-layouts  72.1 us (3%)
    reduce_scatter x1, waiting for transfers between devices, per_device(): lax.psum_scatter(jnp.concatenate([contract_first(dgate_cols, second_low),...  718 us
    all_gather x1, waiting for transfers between devices, per_device(): up_part = lax.all_gather(w_up, 'shard', axis=0, tiled=True)  241 us
    all_gather x1, waiting for transfers between devices, per_device(): down_part = lax.all_gather(w_down, 'shard', axis=0, tiled=True)  235 us
    all_gather x1, waiting for transfers between devices, per_device(): gate_part = lax.all_gather(w_gate, 'shard', axis=0, tiled=True)  235 us
    reduce_scatter x1, waiting for transfers between devices, per_device(): lax.psum_scatter(jnp.concatenate([contract_first(columns, dq_low), contra...  161 us
    all_gather x1, waiting for transfers between devices, per_device(): query_part = lax.all_gather(w_query, 'shard', axis=0, tiled=True)  94.9 us
    all_gather x1, waiting for transfers between devices, per_device(): out_part = lax.all_gather(w_out, 'shard', axis=0, tiled=True)  89 us
    psum x1, waiting for transfers between devices, per_device(): lax.psum(grad_query.astype(jnp.bfloat16), 'rep').astype(jnp.float32)  76.4 us
  transfers between devices with their start and end apart: 14, of which 13 were waited for; matrix products, arithmetic and copies ran while one was open for 10% of the time, Pallas kernels for 0%

commit v1 on v0

v1 whole, which is shorter than its diff:
```python
import math

import jax
import jax.numpy as jnp
from jax import lax
from jax.sharding import PartitionSpec as P

HEADS = 16
KV_HEADS = 8
HEAD_DIM = 128

epsilon = 1e-06
theta_base = 1000000.0
masked_value = -1e30


def rms_scale(values, gain):
    return values * lax.rsqrt(jnp.mean(values * values, axis=-1, keepdims=True) + epsilon) * gain


def rotate(values, positions):
    half_dim = values.shape[-1] // 2
    frequency = theta_base ** (-jnp.arange(half_dim, dtype=jnp.float32) * (2.0 / values.shape[-1]))
    angles = positions.astype(jnp.float32)[:, None] * frequency[None, :]
    cosine = jnp.cos(angles)[:, None, :]
    sine = jnp.sin(angles)[:, None, :]
    first_half = values[..., :half_dim]
    second_half = values[..., half_dim:]
    return jnp.concatenate(
        [first_half * cosine - second_half * sine, second_half * cosine + first_half * sine],
        axis=-1,
    )


def segment_info(lengths_row, indices):
    start_one = lengths_row[0]
    start_two = lengths_row[0] + lengths_row[1]
    segment = (indices >= start_one).astype(jnp.int32) + (indices >= start_two).astype(jnp.int32)
    begin = jnp.where(segment == 0, 0, jnp.where(segment == 1, start_one, start_two))
    return (segment, indices - begin)


def dot(left, right):
    return jnp.dot(left, right, preferred_element_type=jnp.float32)


def contract_rows(left, right):
    return lax.dot_general(
        left, right, (((1,), (1,)), ((), ())), preferred_element_type=jnp.float32
    )


def contract_first(left, right):
    return lax.dot_general(
        left, right, (((0,), (0,)), ((), ())), preferred_element_type=jnp.float32
    )


def gather(x):
    return lax.all_gather(x, "shard", axis=0, tiled=True)


def scatter_sum(x):
    return lax.psum_scatter(
        x.astype(jnp.bfloat16), "shard", scatter_dimension=0, tiled=True
    ).astype(jnp.float32)


def per_device(
    tokens,
    cotangent,
    lengths,
    attn_gain,
    mlp_gain,
    query_gain,
    key_gain,
    w_query,
    w_key,
    w_value,
    w_out,
    w_gate,
    w_up,
    w_down,
):
    low = jnp.bfloat16
    tok_rows, width = tokens.shape
    shards = lax.axis_size("shard")
    rows = tok_rows * shards
    group = HEADS // KV_HEADS
    feat = width // shards
    scale = 1.0 / math.sqrt(HEAD_DIM)
    my_shard = lax.axis_index("shard")
    index = jnp.arange(rows, dtype=jnp.int32)
    segment, position = segment_info(lengths[0], index)
    visible = (segment[:, None] == segment[None, :]) & (index[None, :] <= index[:, None])

    q_cols = w_query.shape[1] // shards
    k_cols = w_key.shape[1] // shards
    packed = jnp.concatenate(
        [
            w_query.reshape(feat, shards, q_cols),
            w_key.reshape(feat, shards, k_cols),
            w_value.reshape(feat, shards, k_cols),
            w_out.reshape(feat, shards, q_cols),
        ],
        axis=2,
    )
    mine = lax.all_to_all(packed, "shard", split_axis=1, concat_axis=0, tiled=True).reshape(
        width, -1
    )
    qkv_cols = q_cols + 2 * k_cols
    w_qkv = mine[:, :qkv_cols]
    w_o = mine[:, qkv_cols:]

    gains_rows = jnp.concatenate(
        [attn_gain, mlp_gain, jnp.zeros((width - 2 * feat,), low)]
    ).reshape(1, width)
    gathered = gather(
        jnp.concatenate([tokens, jnp.broadcast_to(gains_rows, (16, width))], axis=0)
    ).reshape(shards, tok_rows + 16, width)
    tokens_all = gathered[:, :tok_rows].reshape(rows, width)
    gain_one = gathered[:, tok_rows, :feat].reshape(width).astype(jnp.float32)
    gain_two = gathered[:, tok_rows, feat : 2 * feat].reshape(width).astype(jnp.float32)

    inputs = tokens.astype(jnp.float32)
    first = rms_scale(tokens_all.astype(jnp.float32), gain_one).astype(low)
    proj = dot(first, w_qkv)

    def prepare(projected, gain, count):
        return rotate(rms_scale(projected.reshape(rows, count, HEAD_DIM), gain), position)

    q_rot, query_back = jax.vjp(
        lambda p, g: prepare(p, g, group), proj[:, :q_cols], query_gain.astype(jnp.float32)
    )
    k_rot, key_back = jax.vjp(
        lambda p, g: prepare(p, g, 1), proj[:, q_cols : q_cols + k_cols], key_gain.astype(jnp.float32)
    )
    query = q_rot.astype(low)
    key = k_rot.astype(low)[:, 0]
    value = proj[:, q_cols + k_cols :].astype(low)
    scores = jnp.einsum("tgd,sd->gts", query, key, preferred_element_type=jnp.float32) * scale
    masked = jnp.where(visible[None], scores, masked_value)
    top = jnp.max(masked, axis=-1, keepdims=True)
    total = jnp.log(jnp.sum(jnp.exp(masked - top), axis=-1, keepdims=True)) + top
    weights = jnp.exp(masked - total)
    probs = weights.astype(low)
    attended = (
        jnp.einsum("gts,sd->tgd", probs, value, preferred_element_type=jnp.float32)
        .reshape(rows, q_cols)
        .astype(low)
    )
    resid = inputs + scatter_sum(contract_rows(attended, w_o))
    second_value, second_back = jax.vjp(rms_scale, resid, gain_two)
    second = gather(second_value.astype(low))
    grad_low = gather(cotangent.astype(low))
    gate = contract_rows(second, w_gate)
    up = contract_rows(second, w_up)
    sigma = jax.nn.sigmoid(gate)
    hidden = (gate * sigma * up).astype(low)
    result = resid + scatter_sum(dot(hidden, w_down))
    dhidden = contract_rows(grad_low, w_down)
    dgate = (dhidden * up * sigma * (1.0 + gate * (1.0 - sigma))).astype(low)
    dup = (dhidden * gate * sigma).astype(low)
    dsecond = scatter_sum(dot(dgate, w_gate) + dot(dup, w_up))
    ffn_grads = lax.psum(
        tuple(
            g.astype(low)
            for g in (
                contract_first(dgate, second),
                contract_first(dup, second),
                contract_first(hidden, grad_low),
            )
        ),
        "rep",
    )
    grad_resid_part, grad_second_gain = second_back(dsecond)
    grad_resid = cotangent + grad_resid_part
    branch = gather(grad_resid.astype(low))
    grad_att = dot(branch, w_o).astype(low)
    grad_heads = grad_att.reshape(rows, group, HEAD_DIM)
    dprobs = jnp.einsum("tgd,sd->gts", grad_heads, value, preferred_element_type=jnp.float32)
    inner = jnp.sum(weights * dprobs, axis=-1, keepdims=True)
    dscores = (weights * (dprobs - inner)).astype(low)
    dquery = jnp.einsum("gts,sd->tgd", dscores, key, preferred_element_type=jnp.float32) * scale
    dkey = jnp.einsum("gts,tgd->sd", dscores, query, preferred_element_type=jnp.float32) * scale
    dvalue = jnp.einsum("gts,tgd->sd", probs, grad_heads, preferred_element_type=jnp.float32)
    dq_proj, grad_query_part = query_back(dquery)
    dk_proj, grad_key_part = key_back(dkey[:, None])
    d_qkv = jnp.concatenate(
        [dq_proj.astype(low), dk_proj.astype(low), dvalue.astype(low)], axis=1
    )
    grad_first = scatter_sum(contract_rows(d_qkv, w_qkv))
    attn_grads = lax.psum(
        jnp.concatenate(
            [contract_first(first, d_qkv), contract_first(branch, attended)], axis=1
        ).astype(low),
        "rep",
    )
    attn_grads = lax.all_to_all(
        attn_grads.reshape(shards, feat, -1), "shard", split_axis=0, concat_axis=1, tiled=True
    ).reshape(shards, feat, -1).transpose(1, 0, 2).astype(jnp.float32)
    grad_query = attn_grads[:, :, :q_cols].reshape(feat, -1)
    grad_key = attn_grads[:, :, q_cols : q_cols + k_cols].reshape(feat, -1)
    grad_value = attn_grads[:, :, q_cols + k_cols : qkv_cols].reshape(feat, -1)
    grad_out = attn_grads[:, :, qkv_cols:].reshape(feat, -1)
    first_back = jax.vjp(rms_scale, inputs, gain_one)[1]
    grad_input_part, grad_first_gain = first_back(grad_first)
    grad_tokens = grad_resid + grad_input_part
    gains = lax.psum(
        jnp.concatenate([grad_first_gain, grad_second_gain, grad_query_part, grad_key_part]),
        ("rep", "shard"),
    )
    head_piece = HEAD_DIM // shards
    gains_first = lax.dynamic_slice_in_dim(gains, my_shard * feat, feat, 0)
    gains_second = lax.dynamic_slice_in_dim(gains, width + my_shard * feat, feat, 0)
    gains_query = lax.dynamic_slice_in_dim(gains, 2 * width + my_shard * head_piece, head_piece, 0)
    gains_key = lax.dynamic_slice_in_dim(
        gains, 2 * width + HEAD_DIM + my_shard * head_piece, head_piece, 0
    )
    return (
        result,
        grad_tokens,
        grad_query,
        grad_key,
        grad_value,
        grad_out,
        ffn_grads[0].astype(jnp.float32),
        ffn_grads[1].astype(jnp.float32),
        ffn_grads[2].astype(jnp.float32),
        gains_first,
        gains_second,
        gains_query,
        gains_key,
    )


def solution(mesh):
    spread = P(("rep", "shard"), None)
    rowed = P("shard", None)
    return jax.shard_map(
        per_device,
        mesh=mesh,
        in_specs=(spread, spread, P("rep", None), P("shard"), P("shard"), P(), P()) + (rowed,) * 7,
        out_specs=(spread, spread) + (rowed,) * 7 + (P("shard"),) * 4,
        check_vma=False,
    )
```

time: 2510 us -> 891 us (0.35)
  waiting for transfers between devices: 2020 us -> 539 us
  matrix products: 195 us -> 110 us
  other arithmetic: 96.3 us -> 63.7 us
  local copies, waits for them, and re-layouts: 72.1 us -> 41.1 us
    all_gather x9 -> x4, waiting for transfers between devices: 1020 us -> 128 us  [gather(): return lax.all_gather(x, 'shard', axis=0, tiled=True)]
    reduce_scatter x2 -> x4, waiting for transfers between devices: 879 us -> 186 us  [scatter_sum(): lax.psum_scatter(x.astype(jnp.bfloat16), 'shard', scatter_dimension=0, ti...]
    psum x1, waiting for transfers between devices: 76.4 us -> 161 us  [per_device(): lax.psum(jnp.concatenate([contract_first(first, d_qkv), contract_first(br...]
    all_to_all x0 -> x2, waiting for transfers between devices: none -> 64.4 us  [the longest x1 64.4 us: per_device(): lax.all_to_all(packed, 'shard', split_axis=1, concat_axis=0, tiled=True)]
    concatenate x2 -> x5, other arithmetic: 69.7 us -> 6.34 us  [the longest x1 3.12 us: per_device(): jnp.concatenate([w_query.reshape(feat, shards, q_cols), w_key.reshape(fea...]
    unnamed x16 -> x9, waiting for transfers between devices: 36.6 us -> 0.15 us
    dot_general x7 -> x5, matrix products: 59.7 us -> 23.9 us  [contract_first(): lax.dot_general(left, right, (((0,), (0,)), ((), ())), preferred_element_...]
    all_gather x2 -> x0, blocking collectives: 31.4 us -> none  [the longest x1 17.6 us: per_device(): piece_one = lax.all_gather(attn_gain, 'shard', axis=0, tiled=True)]
  transfers between devices with their start and end apart: 14 -> 11, of which waited for: 13 -> 9; matrix products, arithmetic and copies ran while one was open for 10% -> 10% of each run, Pallas kernels for 0% -> 0%
where the time goes in v1:
time: 891 us; the launch traced here: 881 us
  waiting for transfers between devices  539 us (60%)
  matrix products  110 us (12%)
  blocking collectives  98.3 us (11%)
  other arithmetic  63.7 us (7%)
  local copies, waits for them, and re-layouts  41.1 us (5%)
  between operations  16.2 us (2%)
  starting transfers between devices  11.9 us (1%)
    reduce_scatter x4, waiting for transfers between devices, scatter_sum(): lax.psum_scatter(x.astype(jnp.bfloat16), 'shard', scatter_dimension=0, ti...  186 us
    psum x1, waiting for transfers between devices, per_device(): lax.psum(jnp.concatenate([contract_first(first, d_qkv), contract_first(br...  161 us
    all_gather x4, waiting for transfers between devices, gather(): return lax.all_gather(x, 'shard', axis=0, tiled=True)  128 us
    psum x1, blocking collectives, per_device(): lax.psum(jnp.concatenate([grad_first_gain, grad_second_gain, grad_query_p...  98.3 us
    all_to_all x1, waiting for transfers between devices, per_device(): lax.all_to_all(packed, 'shard', split_axis=1, concat_axis=0, tiled=True)  64.4 us
    dot_general x5, matrix products, contract_rows(): lax.dot_general(left, right, (((1,), (1,)), ((), ())), preferred_element_...  34.1 us
    dot_general x5, matrix products, dot(): return jnp.dot(left, right, preferred_element_type=jnp.float32)  33.1 us
    dot_general x5, matrix products, contract_first(): lax.dot_general(left, right, (((0,), (0,)), ((), ())), preferred_element_...  23.9 us
  transfers between devices with their start and end apart: 11, of which 9 were waited for; matrix products, arithmetic and copies ran while one was open for 10% of the time, Pallas kernels for 0%

profile of v1, /device:TPU:1, one launch (start us, length us, event | category | flops | bytes accessed | tf_op | source)
XLA Modules:
  0.0 880.7 jit_solution(18401693859321994216)
XLA Ops:
  14.2 2.3 copy.84
  18.7 3.1 pad_maximum_fusion
  21.8 7.0 all-to-all-start
  31.5 3.0 multiply_cosine_fusion
  36.1 64.4 %all-to-all-done = bf16[256,8,768]{0,2,1:T(8,128)(2,1)} async-done(((bf16[256,8,768]{0,2,1:T(8,128)(2,1)}), bf16[256,8,768]{0,2,1:T(8,128)(2,1)}, u32[]{:S(2)}, u32[]{:S(2)}) %all-to-all-start) | async-done | bytes 3145760 | tf_op jit(solution)/shard_map/all_to_all | solution.py:108
  100.5 4.6 copy.88
  105.2 4.8 all-gather.5.cloned.1.call-done
  110.0 3.1 multiply_reduce_fusion
  113.8 3.2 slice_convert_fusion
  119.3 2.4 fusion.9
  124.7 2.5 copy.89
  136.0 3.7 convolution_convert_fusion.8
  140.5 4.6 convolution_convert_fusion.1
  145.1 53.7 %reduce-scatter.5.cloned.1.call-done = bf16[128,2048]{1,0:T(8,128)(2,1)} async-done(((bf16[1024,2048]{1,0:T(8,128)(2,1)}), bf16[128,2048]{1,0:T(8,128)(2,1)}) %reduce-scatter.5.cloned.1.call-update) | async-done | bytes 524304 | tf_op jit(solution)/shard_map/reduce_scatter | solution.py:64
  204.7 49.4 %all-gather.7.cloned.1.call-done = bf16[1024,2048]{1,0:T(8,128)(2,1)} async-done(((bf16[128,2048]{1,0:T(8,128)(2,1)}), bf16[1024,2048]{1,0:T(8,128)(2,1)}) %all-gather.7.cloned.1.call-update) | async-done | bytes 4194320 | tf_op jit(solution)/shard_map/all_gather | solution.py:60
  254.1 8.4 fusion.71
  262.5 5.1 fusion.70
  267.6 40.0 %all-gather.9.cloned.1.call-done = bf16[1024,2048]{1,0:T(8,128)(2,1)} async-done(((bf16[128,2048]{1,0:T(8,128)(2,1)}), bf16[1024,2048]{1,0:T(8,128)(2,1)}) %all-gather.9.cloned.1.call-update) | async-done | bytes 4194320 | tf_op jit(solution)/shard_map/all_gather | solution.py:60
  307.6 9.7 %multiply_convert_fusion = (bf16[1024,768]{1,0:T(8,128)(2,1)S(1)}, bf16[1024,768]{1,0:T(8,128)(2,1)S(1)}, bf16[1024,768]{1,0:T(8,128)(2,1)}) fusion(f32[1024,768]{1,0:T(8,128)} %fusion.70, f32[1024,768]{1,0:T(8,128)} %fusion.71, bf16[1024,2048]{1,0:T(8,128)(2,1)} %all-gather.9.cloned.1.call-done, bf16[768,2048]{1,0:T(8,128)(2,1)S(1)} %copy-done), kind=kOutput, calls=%fused_computation.28 | convolution fusion | flops 3233808384 | bytes 18350080 | tf_op jit(solution)/shard_map/dot_general | solution.py:48
  317.4 3.4 fusion.72
  320.9 16.5 %add_convert_fusion = bf16[1024,2048]{1,0:T(8,128)(2,1)} fusion(f32[1024,2048]{1,0:T(8,128)S(1)} %fusion.72, bf16[1024,768]{1,0:T(8,128)(2,1)S(1)} %get-tuple-element.43, bf16[768,2048]{1,0:T(8,128)(2,1)S(1)} %copy-done.27), kind=kOutput, calls=%fused_computation.9 | convolution fusion | flops 3225419776 | bytes 17301504 | tf_op jit(solution)/shard_map/dot_general | solution.py:44
  337.4 52.1 %reduce-scatter.9.cloned.1.call-done = bf16[128,2048]{1,0:T(8,128)(2,1)} async-done(((bf16[1024,2048]{1,0:T(8,128)(2,1)}), bf16[128,2048]{1,0:T(8,128)(2,1)}) %reduce-scatter.9.cloned.1.call-update) | async-done | bytes 524304 | tf_op jit(solution)/shard_map/reduce_scatter | solution.py:64
  391.5 2.9 fusion.62
  394.4 8.0 convolution_convert_fusion.4
  402.4 4.9 convolution_convert_fusion.5
  407.3 4.9 convolution_convert_fusion.3
  412.2 33.8 %all-gather.11.cloned.1.call-done = bf16[1024,2048]{1,0:T(8,128)(2,1)} async-done(((bf16[128,2048]{1,0:T(8,128)(2,1)}), bf16[1024,2048]{1,0:T(8,128)(2,1)}) %all-gather.11.cloned.1.call-update) | async-done | bytes 4194320 | tf_op jit(solution)/shard_map/all_gather | solution.py:60
  445.9 3.9 convolution_convert_fusion.9
  449.9 6.8 fusion.17
  456.7 3.0 fusion
  459.7 2.9 fusion.2
  472.9 4.9 convolution_convert_fusion.6
  481.6 6.3 convolution_convert_fusion
  487.9 6.9 convolution_convert_fusion.2
  494.9 161.1 %all-reduce.7.cloned.1.call-done = (bf16[8,256,768]{1,2,0:T(8,128)(2,1)}, bf16[768,2048]{1,0:T(8,128)(2,1)}, bf16[768,2048]{1,0:T(8,128)(2,1)}, bf16[768,2048]{1,0:T(8,128)(2,1)}) async-done(((bf16[8,256,768]{1,2,0:T(8,128)(2,1)}, bf16[768,2048]{1,0:T(8,128)(2,1)}, bf16[768,2048]{1,0:T(8,128)(2,1)}, bf16[768,2048]{1,0:T(8,128)(2,1)}), (bf16[8,256,768]{1,2,0:T(8,128)(2,1)}, bf16[768,2048]{1,0:T(8,128)(2,1)}, ...) | async-done | bytes 12582928 | tf_op jit(solution)/shard_map/psum | solution.py:193
  655.9 4.5 all-to-all-start.1
  660.4 79.9 %reduce-scatter.11.cloned.1.call-done = bf16[128,2048]{1,0:T(8,128)(2,1)} async-done(((bf16[1024,2048]{1,0:T(8,128)(2,1)}), bf16[128,2048]{1,0:T(8,128)(2,1)}) %reduce-scatter.11.cloned.1.call-update) | async-done | bytes 524304 | tf_op jit(solution)/shard_map/reduce_scatter | solution.py:64
  742.1 98.3 %psum.39 = f32[4352]{0:T(1024)S(1)} all-reduce(f32[4352]{0:T(1024)S(1)} %pad_maximum_fusion.9), channel_id=1, replica_groups=mesh['rep'=16,'shard'=8] {'rep','shard'}, use_global_device_ids=true, to_apply=%region_24.25 | all-reduce | flops 4352 | bytes 34816 | tf_op jit(solution)/shard_map/psum | solution.py:209
  841.7 4.2 fusion.23
  845.9 3.6 convert_element_type.225
  849.4 3.6 convert_element_type.227
  853.0 3.6 convert_element_type.229
  856.5 2.4 convert_bitcast_fusion
  860.5 2.4 fusion.65
  862.9 2.9 copy.106
  865.8 2.9 copy.103
  868.7 2.5 copy.105
  871.2 2.5 copy.104
  (148 shorter events, 54.0 us)
Async XLA Ops:
  7.2 300.5 %copy-start = (bf16[768,2048]{1,0:T(8,128)(2,1)S(1)}, bf16[768,2048]{1,0:T(8,128)(2,1)}, u32[]{:S(2)}) copy-start(bf16[768,2048]{1,0:T(8,128)(2,1)} %param.27) | copy-start | bytes 9437188
  7.2 102.8 %all-gather.5.cloned.1.call-start = ((), (), s32[]{:S(2)}) async-start(), calls=%async_computation.6 | async-start | bytes 5308416 | tf_op jit(solution)/shard_map/all_gather | solution.py:60
  21.8 7.1 copy-start.28
  21.8 7.1 copy-start.29
  21.8 7.1 copy-start.20
  21.8 78.7 %all-to-all-start = ((bf16[256,8,768]{0,2,1:T(8,128)(2,1)}), bf16[256,8,768]{0,2,1:T(8,128)(2,1)}, u32[]{:S(2)}, u32[]{:S(2)}) async-start(bf16[256,8,768]{0,2,1:T(8,128)(2,1)} %pad_maximum_fusion), calls=%async_computation | async-start | bytes 6291456 | tf_op jit(solution)/shard_map/all_to_all | solution.py:108
  28.8 170.0 %reduce-scatter.5.cloned.1.call-start = ((), (), s32[]{:S(2)}) async-start(), calls=%async_computation.7 | async-start | bytes 4718592 | tf_op jit(solution)/shard_map/reduce_scatter | solution.py:64
  117.1 2.2 copy-start.7
  117.9 3.8 copy-start.10
  121.7 1.7 copy-start.5
  127.2 3.3 copy-start.2
  130.5 2.2 copy-start.14
  130.5 2.2 copy-start.16
  132.7 3.3 copy-start.1
  139.7 0.8 copy-start.18
  145.1 109.0 %all-gather.7.cloned.1.call-start = ((), (), s32[]{:S(2)}) async-start(), calls=%async_computation.8 | async-start | bytes 4718592 | tf_op jit(solution)/shard_map/all_gather | solution.py:60
  202.5 105.1 %all-gather.9.cloned.1.call-start = ((), (), s32[]{:S(2)}) async-start(), calls=%async_computation.10 | async-start | bytes 4718592 | tf_op jit(solution)/shard_map/all_gather | solution.py:60
  204.7 184.8 %reduce-scatter.9.cloned.1.call-start = ((), (), s32[]{:S(2)}) async-start(), calls=%async_computation.11 | async-start | bytes 4718592 | tf_op jit(solution)/shard_map/reduce_scatter | solution.py:64
  254.1 8.4 copy-start.22
  254.1 8.4 copy-start.25
  307.6 9.8 %copy-start.26 = (bf16[768,2048]{1,0:T(8,128)(2,1)S(1)}, bf16[768,2048]{1,0:T(8,128)(2,1)}, u32[]{:S(2)}) copy-start(bf16[768,2048]{1,0:T(8,128)(2,1)} %param.25) | copy-start | bytes 9437188
  317.4 3.4 copy-start.31
  317.4 3.4 copy-start.33
  317.4 3.5 copy-start.27
  337.4 108.6 %all-gather.11.cloned.1.call-start = ((), (), s32[]{:S(2)}) async-start(), calls=%async_computation.12 | async-start | bytes 4718592 | tf_op jit(solution)/shard_map/all_gather | solution.py:60
  394.3 261.6 %all-reduce.7.cloned.1.call-start = ((), (), s32[]{:S(2)}) async-start(), calls=%async_computation.14 | async-start | bytes 25165824 | tf_op jit(solution)/shard_map/psum | solution.py:193
  394.4 8.0 copy-start.23
  394.4 8.0 copy-start.32
  402.4 4.9 copy-start.24
  402.4 4.9 copy-start.30
  445.9 3.9 copy-start.3
  445.9 10.8 %slice-start = ((s8[8388608]{0:T(1024)(128)(4,1)}), s8[4194304]{0:T(1024)(128)(4,1)S(1)}, s32[]{:S(2)}) async-start(s8[8388608]{0:T(1024)(128)(4,1)} %bitcast.137), calls=%async_computation.15 | async-start | bytes 8388608
  449.9 6.8 slice-start.1
  449.9 6.8 copy-start.6
  459.7 3.0 copy-start.15
  459.7 3.0 copy-start.17
  464.3 3.1 copy-start.8
  464.3 3.1 copy-start.9
  466.2 2.0 copy-start.4
  472.9 4.9 copy-start.19
  472.9 4.9 copy-start.21
  481.5 258.8 %reduce-scatter.11.cloned.1.call-start = ((), (), s32[]{:S(2)}) async-start(), calls=%async_computation.13 | async-start | bytes 4718592 | tf_op jit(solution)/shard_map/reduce_scatter | solution.py:64
  487.9 353.8 %reduce-scatter.7.cloned.1.call-start = ((), (), s32[]{:S(2)}) async-start(), calls=%async_computation.9 | async-start | bytes 4718592 | tf_op jit(solution)/shard_map/reduce_scatter | solution.py:64
  655.9 200.6 %all-to-all-start.1 = ((bf16[8,256,768]{1,2,0:T(8,128)(2,1)}), bf16[8,256,768]{1,2,0:T(8,128)(2,1)}, u32[]{:S(2)}, u32[]{:S(2)}) async-start(bf16[8,256,768]{1,2,0:T(8,128)(2,1)} %get-tuple-element.35), calls=%async_computation.5 | async-start | bytes 6291456 | tf_op jit(solution)/shard_map/all_to_all | solution.py:199
  841.7 4.2 copy-start.13
  845.8 3.6 copy-start.12
  849.4 3.6 copy-start.11
Sparse Core Ops, SparseCore 0:
  10.2 99.6 all-gather.4
  145.2 53.5 reduce-scatter.4
  202.7 51.3 all-gather.6
  256.2 51.4 all-gather.8
  337.5 51.9 reduce-scatter.8
  394.5 51.3 all-gather.10
  481.6 174.2 all-reduce.6
  658.9 81.4 reduce-scatter.10
  743.3 51.5 reduce-scatter.6

commit v2 on v1

--- a/solution.py
+++ b/solution.py
@@ -1,8 +1,11 @@
+import functools
 import math
 
 import jax
 import jax.numpy as jnp
 from jax import lax
+from jax.experimental import pallas as pl
+from jax.experimental.pallas import tpu as pltpu
 from jax.sharding import PartitionSpec as P
 
 HEADS = 16
@@ -12,6 +15,639 @@
 epsilon = 1e-06
 theta_base = 1000000.0
 masked_value = -1e30
+
+
+MESH = pl.DeviceIdType.MESH
+BLOCK = 128
+HALF = 64
+LINE = 512
+low = jnp.bfloat16
+f32 = jnp.float32
+
+
+def mm(left, right):
+    return lax.dot_general(left, right, (((1,), (0,)), ((), ())), preferred_element_type=f32)
+
+
+def mm_nt(left, right):
+    return lax.dot_general(left, right, (((1,), (1,)), ((), ())), preferred_element_type=f32)
+
+
+def mm_tn(left, right):
+    return lax.dot_general(left, right, (((0,), (0,)), ((), ())), preferred_element_type=f32)
+
+
+class Place:
+    def __init__(self):
+        self.rep = lax.axis_index("rep")
+        shard = lax.axis_index("shard")
+        self.yl, self.z = shard // 4, shard % 4
+
+    def block(self, dy, dz):
+        return ((self.yl + dy + 2) % 2) * 4 + (self.z + dz + 8) % 4
+
+    def dev(self, dy, dz):
+        return (self.rep, self.block(dy, dz))
+
+    def rows(self, dy, dz, start=0, count=BLOCK):
+        return pl.ds(pl.multiple_of(self.block(dy, dz) * BLOCK + start, 32), count)
+
+    def line(self, dy):
+        return pl.multiple_of(((self.yl + dy + 2) % 2) * LINE, LINE)
+
+    def greet(self):
+        barrier = pltpu.get_barrier_semaphore()
+        for peer in ((1, 0), (0, 1), (0, 3)):
+            pl.semaphore_signal(barrier, inc=1, device_id=self.dev(*peer), device_id_type=MESH)
+        pl.semaphore_wait(barrier, 3)
+
+
+class Net:
+    def __init__(self, send_sems, recv_sems):
+        self.send_sems, self.recv_sems = send_sems, recv_sems
+        self.started, self.coming = [], {}
+
+    def send(self, tag, src, dst, dev, here):
+        k = len(self.started)
+        copy = pltpu.make_async_remote_copy(
+            src_ref=src,
+            dst_ref=dst,
+            send_sem=self.send_sems.at[k],
+            recv_sem=self.recv_sems.at[k],
+            device_id=dev,
+            device_id_type=MESH,
+        )
+        copy.start()
+        self.started.append(copy)
+        self.coming[tag] = (k, here, dev)
+
+    def wait(self, tag):
+        k, here, dev = self.coming.pop(tag)
+        pltpu.make_async_remote_copy(
+            src_ref=here,
+            dst_ref=here,
+            send_sem=self.send_sems.at[k],
+            recv_sem=self.recv_sems.at[k],
+            device_id=dev,
+            device_id_type=MESH,
+        ).wait_recv()
+
+    def finish(self):
+        for tag in list(self.coming):
+            self.wait(tag)
+        for copy in self.started:
+            copy.wait_send()
+
+
+class Gather:
+    COPIES = 18
+
+    def __init__(self, place, buf, send_sems, recv_sems):
+        self.place, self.buf = place, buf
+        self.net = Net(send_sems, recv_sems)
+
+    def send(self, tag, block, start, count, to):
+        rows = self.place.rows(*block, start, count)
+        here = self.place.rows(block[0] - to[0], block[1] - to[1], start, count)
+        self.net.send(
+            tag, self.buf.at[rows], self.buf.at[rows], self.place.dev(*to), self.buf.at[here]
+        )
+
+    def start(self):
+        self.send("y_up", (0, 0), 0, HALF, (1, 0))
+        for d in (1, 3):
+            self.send(f"z_low{d}", (0, 0), HALF, HALF, (0, d))
+        self.send("y_low", (0, 0), HALF, HALF, (1, 0))
+
+    def step_one(self):
+        self.net.wait("y_up")
+        for d in (1, 3):
+            self.send(f"p_up{d}", (1, 0), 0, HALF, (0, d))
+
+    def step_two(self):
+        for e, d in enumerate((1, 3)):
+            self.net.wait(f"z_low{d}")
+            self.send(f"f_low{d}", (0, -d), HALF + 32 * e, 32, (0, d))
+            self.send(f"q_low{d}", (0, -d), HALF, HALF, (1, 0))
+        for d in (1, 3):
+            self.send(f"z_up{d}", (0, 0), 0, HALF, (0, d))
+
+    def step_three(self):
+        for e, d in enumerate((1, 3)):
+            self.net.wait(f"p_up{d}")
+            self.send(f"f_p{d}", (1, -d), 32 * e, 32, (0, d))
+        for e, d in enumerate((1, 3)):
+            self.net.wait(f"f_low{d}")
+            self.send(f"q_far{d}", (0, -2 * d), HALF + 32 * e, 32, (1, 0))
+
+    def step_four(self):
+        for e, d in enumerate((1, 3)):
+            self.net.wait(f"z_up{d}")
+            self.send(f"f_up{d}", (0, -d), 32 * e, 32, (0, d))
+
+    def own_line(self):
+        for d in (1, 3):
+            self.net.wait(f"f_up{d}")
+
+    def other_line(self):
+        for tag in list(self.net.coming):
+            self.net.wait(tag)
+
+    def steps(self):
+        return [self.start, self.step_one, self.step_two, self.step_three, self.step_four]
+
+    def finish(self):
+        self.net.finish()
+
+
+class Scatter:
+    COPIES = 17
+
+    @staticmethod
+    def scratch(columns):
+        return [
+            pltpu.VMEM((4, HALF, columns), low),
+            pltpu.VMEM((3, 2, 32, columns), low),
+            pltpu.VMEM((3, 2, HALF, columns), low),
+            pltpu.VMEM((HALF, columns), low),
+        ]
+
+    def __init__(self, place, part, across, near, far, last, send_sems, recv_sems):
+        self.place, self.part = place, part
+        self.across, self.near, self.far, self.last = across, near, far, last
+        self.net = Net(send_sems, recv_sems)
+
+    def add(self, rows, *refs):
+        total = self.part[rows, :].astype(f32)
+        for ref in refs:
+            total = total + ref[...].astype(f32)
+        self.part[rows, :] = total.astype(low)
+
+    def first(self, kind):
+        dy, start = ((1, 0), (0, 0), (0, HALF))[kind]
+        for e, d in enumerate((1, 3)):
+            src = self.part.at[self.place.rows(dy, 2, start + 32 * e, 32)]
+            dst = self.near.at[kind, e]
+            self.net.send(f"near{kind}{e}", src, dst, self.place.dev(0, d), dst)
+
+    def second(self, kind):
+        dy, start = ((1, 0), (0, 0), (0, HALF))[kind]
+        for e, d in enumerate((1, 3)):
+            self.net.wait(f"near{kind}{e}")
+            self.add(self.place.rows(dy, d, start + 32 * e, 32), self.near.at[kind, e])
+            src = self.part.at[self.place.rows(dy, d, start, HALF)]
+            dst = self.far.at[kind, e]
+            self.net.send(f"far{kind}{e}", src, dst, self.place.dev(0, d), dst)
+
+    def send_other(self):
+        for d in (2, 1, 3, 0):
+            src = self.part.at[self.place.rows(1, d, HALF, HALF)]
+            dst = self.across.at[d]
+            self.net.send(f"across{d}", src, dst, self.place.dev(1, 0), dst)
+        self.first(0)
+
+    def send_own(self):
+        self.first(1)
+
+    def step_one(self):
+        self.net.wait("across2")
+        self.add(self.place.rows(0, 2, HALF, HALF), self.across.at[2])
+        self.first(2)
+        self.second(0)
+        self.second(1)
+
+    def step_two(self):
+        for d in (1, 3):
+            self.net.wait(f"across{d}")
+            self.add(self.place.rows(0, d, HALF, HALF), self.across.at[d])
+        self.second(2)
+
+    def step_three(self):
+        for e in range(2):
+            self.net.wait(f"far0{e}")
+        rows = self.place.rows(1, 0, 0, HALF)
+        self.add(rows, self.far.at[0, 0], self.far.at[0, 1])
+        self.net.send("last", self.part.at[rows], self.last, self.place.dev(1, 0), self.last)
+
+    def total(self, half):
+        if half == 0:
+            tags, extra, kind = ("far10", "far11", "last"), self.last, 1
+        else:
+            tags, extra, kind = ("far20", "far21", "across0"), self.across.at[0], 2
+        for tag in tags:
+            self.net.wait(tag)
+        out = self.part[self.place.rows(0, 0, half * HALF, HALF), :].astype(f32)
+        for ref in (self.far.at[kind, 0], self.far.at[kind, 1], extra):
+            out = out + ref[...].astype(f32)
+        return out
+
+    def finish(self):
+        self.net.finish()
+
+
+def rms_backward(value, gain, upstream):
+    root = lax.rsqrt(jnp.mean(value * value, axis=-1, keepdims=True) + epsilon)
+    pulled = upstream * gain
+    back = root * pulled - value * (root * root * root) * jnp.mean(
+        pulled * value, axis=-1, keepdims=True
+    )
+    return back, upstream * (value * root)
+
+
+def swap_halves(value):
+    return pltpu.roll(value, HEAD_DIM // 2, 1)
+
+
+def late_kernel(
+    scale,
+    lengths,
+    resid,
+    cotangent,
+    tokens,
+    gain_one,
+    gain_two,
+    query_gain,
+    key_gain,
+    proj,
+    cosine,
+    sine,
+    w_attn_hbm,
+    heads_hbm,
+    first_hbm,
+    w_gate_hbm,
+    w_up_hbm,
+    w_down_hbm,
+    result,
+    grad_tokens,
+    gains,
+    attn_grads,
+    ffn_grads,
+    second,
+    cot_all,
+    branch,
+    w_gate,
+    w_up,
+    w_down,
+    hidden,
+    d_gate,
+    d_up,
+    part_out,
+    part_back,
+    d_att,
+    d_key,
+    d_value,
+    d_qkv,
+    staged,
+    o_across,
+    o_near,
+    o_far,
+    o_last,
+    b_across,
+    b_near,
+    b_far,
+    b_last,
+    local_sems,
+    stage_sems,
+    send_sems,
+    recv_sems,
+):
+    place = Place()
+    rows_all = 8 * BLOCK
+    hid = w_gate.shape[0]
+    width = second.shape[1]
+
+    loads = [
+        pltpu.make_async_copy(src, dst, local_sems.at[i])
+        for i, (src, dst) in enumerate(
+            ((w_gate_hbm, w_gate), (w_up_hbm, w_up), (w_down_hbm, w_down))
+        )
+    ]
+    for load in loads:
+        load.start()
+
+    used = [0]
+
+    def sems(count):
+        at = used[0]
+        used[0] += count
+        return send_sems.at[pl.ds(at, count)], recv_sems.at[pl.ds(at, count)]
+
+    own = place.rows(0, 0)
+    root = lax.rsqrt(jnp.mean(resid[...] * resid[...], axis=-1, keepdims=True) + epsilon)
+    second[own, :] = (resid[...] * root * gain_two[...]).astype(low)
+    cot_all[own, :] = cotangent[...].astype(low)
+    place.greet()
+    gather_second = Gather(place, second, *sems(Gather.COPIES))
+    gather_cot = Gather(place, cot_all, *sems(Gather.COPIES))
+    gather_branch = Gather(place, branch, *sems(Gather.COPIES))
+    scatter_out = Scatter(
+        place, part_out, o_across, o_near, o_far, o_last, *sems(Scatter.COPIES)
+    )
+    scatter_back = Scatter(
+        place, part_back, b_across, b_near, b_far, b_last, *sems(Scatter.COPIES)
+    )
+
+    def feed_forward(dy):
+        rows = pl.ds(place.line(dy), LINE)
+
+        @pl.loop(0, hid // 256)
+        def _(i):
+            cols = pl.ds(pl.multiple_of(i * 256, 256), 256)
+            gate = mm_nt(second[rows, :], w_gate[cols, :])
+            up = mm_nt(second[rows, :], w_up[cols, :])
+            sigma = 1.0 / (1.0 + jnp.exp(-gate))
+            silu = gate * sigma
+            hidden[rows, cols] = (silu * up).astype(low)
+            d_gate[rows, cols] = (up * sigma * (1.0 + gate * (1.0 - sigma))).astype(low)
+            d_up[rows, cols] = silu.astype(low)
+
+    def project_out(dy):
+        rows = pl.ds(place.line(dy), LINE)
+
+        @pl.loop(0, width // 512)
+        def _(i):
+            cols = pl.ds(pl.multiple_of(i * 512, 512), 512)
+            part_out[rows, cols] = mm(hidden[rows, :], w_down[:, cols]).astype(low)
+
+    def feed_backward(dy):
+        rows = pl.ds(place.line(dy), LINE)
+
+        @pl.loop(0, hid // 256)
+        def _(i):
+            cols = pl.ds(pl.multiple_of(i * 256, 256), 256)
+            d_hidden = mm_nt(cot_all[rows, :], w_down[cols, :])
+            d_gate[rows, cols] = (d_hidden * d_gate[rows, cols].astype(f32)).astype(low)
+            d_up[rows, cols] = (d_hidden * d_up[rows, cols].astype(f32)).astype(low)
+
+        @pl.loop(0, width // 512)
+        def _(i):
+            cols = pl.ds(pl.multiple_of(i * 512, 512), 512)
+            part_back[rows, cols] = (
+                mm(d_gate[rows, :], w_gate[:, cols]) + mm(d_up[rows, :], w_up[:, cols])
+            ).astype(low)
+
+    stores = [None, None]
+
+    def weight_grad(which, left, right):
+        for i in range(hid // 256):
+            slot = (which * (hid // 256) + i) % 2
+            if stores[slot] is not None:
+                stores[slot].wait()
+            staged[slot] = mm_tn(left[:, pl.ds(i * 256, 256)], right[...]).astype(low)
+            stores[slot] = pltpu.make_async_copy(
+                staged.at[slot], ffn_grads.at[which, pl.ds(i * 256, 256)], stage_sems.at[slot]
+            )
+            stores[slot].start()
+
+    for step in gather_second.steps():
+        step()
+    gather_second.own_line()
+    gather_cot.start()
+    for load in loads:
+        load.wait()
+    feed_forward(0)
+    gather_cot.step_one()
+    gather_cot.step_two()
+    gather_second.other_line()
+    feed_forward(1)
+    gather_cot.step_three()
+    gather_cot.step_four()
+    project_out(1)
+    project_out(0)
+    gather_cot.own_line()
+    gather_cot.other_line()
+    feed_backward(1)
+    scatter_back.send_other()
+    feed_backward(0)
+    scatter_back.send_own()
+    weight_grad(0, d_gate, second)
+    scatter_back.step_one()
+    weight_grad(1, d_up, second)
+    scatter_back.step_two()
+    weight_grad(2, hidden, cot_all)
+    gather_second.finish()
+    gather_cot.finish()
+    heads = d_up
+    q_cols = 2 * HEAD_DIM
+    query = heads.at[:, pl.ds(0, q_cols)]
+    key = heads.at[:, pl.ds(q_cols, HEAD_DIM)]
+    value = heads.at[:, pl.ds(q_cols + HEAD_DIM, HEAD_DIM)]
+    attended = heads.at[:, pl.ds(q_cols + 2 * HEAD_DIM, q_cols)]
+    w_attn = cot_all
+    attn_cols = heads.shape[1]
+    loads = [
+        pltpu.make_async_copy(heads_hbm, heads, local_sems.at[0]),
+        pltpu.make_async_copy(
+            w_attn_hbm.at[pl.ds(0, rows_all)],
+            w_attn.at[:, pl.ds(0, attn_cols)],
+            local_sems.at[1],
+        ),
+        pltpu.make_async_copy(
+            w_attn_hbm.at[pl.ds(rows_all, rows_all)],
+            w_attn.at[:, pl.ds(attn_cols, attn_cols)],
+            local_sems.at[2],
+        ),
+    ]
+    for load in loads:
+        load.start()
+    scatter_back.step_three()
+    gain_rows = None
+    for half in (1, 0):
+        rows = pl.ds(half * HALF, HALF)
+        d_second = scatter_back.total(half)
+        back, gain_part = rms_backward(resid[rows, :], gain_two[...], d_second)
+        grad_tokens[rows, :] = cotangent[rows, :] + back
+        gain_part = jnp.sum(gain_part, axis=0, keepdims=True)
+        gain_rows = gain_part if gain_rows is None else gain_rows + gain_part
+    gains[...] = jnp.zeros_like(gains)
+    gains[0:1, :] = gain_rows
+    branch[own, :] = grad_tokens[...].astype(low)
+    gather_branch.start()
+    scatter_out.send_other()
+    scatter_out.send_own()
+    gather_branch.step_one()
+    gather_branch.step_two()
+    gather_branch.step_three()
+    gather_branch.step_four()
+    gather_branch.own_line()
+    for load in loads:
+        load.wait()
+
+    def into_attention(dy):
+        rows = pl.ds(place.line(dy), LINE)
+        d_att[rows, :] = (
+            mm(branch[rows, 0:rows_all], w_attn[:, 4 * HEAD_DIM : attn_cols])
+            + mm(branch[rows, rows_all:], w_attn[:, attn_cols + 4 * HEAD_DIM : 2 * attn_cols])
+        ).astype(low)
+
+    into_attention(0)
+    gather_branch.other_line()
+    into_attention(1)
+
+    def unrotate(rows, upstream, projected, gain):
+        turned = upstream * cosine[rows, :] - swap_halves(upstream) * sine[rows, :]
+        return rms_backward(projected, gain, turned)
+
+    gain_rows = jnp.zeros((1, HEAD_DIM), f32)
+    start_one = lengths[0, 0]
+    start_two = lengths[0, 0] + lengths[0, 1]
+    d_key[...] = jnp.zeros_like(d_key)
+    d_value[...] = jnp.zeros_like(d_value)
+    chunk = 256
+    scatter_out.step_one()
+    for part in range(rows_all // chunk):
+        rows = pl.ds(part * chunk, chunk)
+        seen = (part + 1) * chunk
+        token = part * chunk + lax.broadcasted_iota(jnp.int32, (chunk, 1), 0)
+        source = lax.broadcasted_iota(jnp.int32, (1, seen), 1)
+        begin = jnp.where(
+            token >= start_two, start_two, jnp.where(token >= start_one, start_one, 0)
+        )
+        visible = (source >= begin) & (source <= token)
+        for g in range(2):
+            lanes = pl.ds(g * HEAD_DIM, HEAD_DIM)
+            scores = mm_nt(query[rows, lanes], key[0:seen, :]) * scale
+            weights = jnp.where(visible, jnp.exp(scores - proj[rows, 3 * HEAD_DIM + g : 3 * HEAD_DIM + g + 1]), 0.0)
+            d_probs = mm_nt(d_att[rows, lanes], value[0:seen, :])
+            inner = jnp.sum(weights * d_probs, axis=-1, keepdims=True)
+            d_scores = (weights * (d_probs - inner)).astype(low)
+            back, gain_part = unrotate(
+                rows, mm(d_scores, key[0:seen, :]) * scale, proj[rows, lanes], query_gain[...]
+            )
+            d_qkv[rows, lanes] = back.astype(low)
+            gain_rows = gain_rows + jnp.sum(gain_part, axis=0, keepdims=True)
+            d_key[0:seen, :] += mm_tn(d_scores, query[rows, lanes])
+            d_value[0:seen, :] += mm_tn(weights.astype(low), d_att[rows, lanes])
+        if part == 1:
+            scatter_out.step_two()
+        if part == 2:
+            scatter_out.step_three()
+    d_qkv[:, 3 * HEAD_DIM :] = d_value[...].astype(low)
+
+    gains[2:3, 0:HEAD_DIM] = gain_rows
+    lanes = pl.ds(2 * HEAD_DIM, HEAD_DIM)
+    back, gain_part = unrotate(pl.ds(0, rows_all), d_key[...] * scale, proj[:, lanes], key_gain[...])
+    d_qkv[:, lanes] = back.astype(low)
+    gains[2:3, HEAD_DIM : 2 * HEAD_DIM] = jnp.sum(gain_part, axis=0, keepdims=True)
+
+    scatter_back.finish()
+    scatter_first = Scatter(
+        place, part_back, b_across, b_near, b_far, b_last, *sems(Scatter.COPIES)
+    )
+    for half in (0, 1):
+        rows = pl.ds(half * HALF, HALF)
+        result[rows, :] = resid[rows, :] + scatter_out.total(half)
+    scatter_out.finish()
+    load = pltpu.make_async_copy(first_hbm, second, local_sems.at[0])
+    load.start()
+
+    def into_first(dy):
+        rows = pl.ds(place.line(dy), LINE)
+
+        for side in range(2):
+
+            @pl.loop(0, rows_all // 256)
+            def _(i):
+                feats = pl.ds(pl.multiple_of(i * 256, 256), 256)
+                cols = pl.ds(pl.multiple_of(side * rows_all + i * 256, 256), 256)
+                part_back[rows, cols] = mm_nt(
+                    d_qkv[rows, :], w_attn[feats, pl.ds(side * attn_cols, 4 * HEAD_DIM)]
+                ).astype(low)
+
+    into_first(1)
+    scatter_first.send_other()
+    into_first(0)
+    scatter_first.send_own()
+    load.wait()
+
+    def attention_grad(index, store):
+        @pl.loop(0, 4)
+        def _(i):
+            cols = pl.ds(pl.multiple_of(index * rows_all + i * 256, 256), 256)
+            rows = pl.ds(pl.multiple_of(i * 256, 256), 256)
+            store[rows, 0 : 4 * HEAD_DIM] = mm_tn(second[:, cols], d_qkv[...]).astype(low)
+            store[rows, 4 * HEAD_DIM :] = mm_tn(branch[:, cols], attended[...]).astype(low)
+
+        copy = pltpu.make_async_copy(
+            store, attn_grads.at[pl.ds(index * rows_all, rows_all)], local_sems.at[1 + index]
+        )
+        copy.start()
+        stores.append(copy)
+
+    attention_grad(0, hidden)
+    scatter_first.step_one()
+    attention_grad(1, d_gate)
+    scatter_first.step_two()
+    scatter_first.step_three()
+    gain_rows = None
+    for half in (1, 0):
+        rows = pl.ds(half * HALF, HALF)
+        d_first = scatter_first.total(half)
+        back, gain_part = rms_backward(tokens[rows, :].astype(f32), gain_one[...], d_first)
+        grad_tokens[rows, :] += back
+        gain_part = jnp.sum(gain_part, axis=0, keepdims=True)
+        gain_rows = gain_part if gain_rows is None else gain_rows + gain_part
+    gains[1:2, :] = gain_rows
+
+    for store in stores:
+        store.wait()
+    gather_branch.finish()
+    scatter_first.finish()
+
+
+def late_call(lengths, *args):
+    width = args[0].shape[1]
+    hid = args[-1].shape[0]
+    rows = 8 * BLOCK
+    vmem = pl.BlockSpec(memory_space=pltpu.VMEM)
+    smem = pl.BlockSpec(memory_space=pltpu.SMEM)
+    anywhere = pl.BlockSpec(memory_space=pl.ANY)
+    copies = 3 * Gather.COPIES + 3 * Scatter.COPIES
+    return pl.pallas_call(
+        functools.partial(late_kernel, 1.0 / math.sqrt(HEAD_DIM)),
+        name="late",
+        out_shape=[
+            jax.ShapeDtypeStruct((BLOCK, width), f32),
+            jax.ShapeDtypeStruct((BLOCK, width), f32),
+            jax.ShapeDtypeStruct((8, width), f32),
+            jax.ShapeDtypeStruct((width, 6 * HEAD_DIM), low),
+            jax.ShapeDtypeStruct((3, hid, width), low),
+        ],
+        in_specs=[smem] + [vmem] * (len(args) - 6) + [anywhere] * 6,
+        out_specs=[vmem] * 3 + [anywhere] * 2,
+        scratch_shapes=[
+            pltpu.VMEM((rows, width), low),
+            pltpu.VMEM((rows, width), low),
+            pltpu.VMEM((rows, width), low),
+            pltpu.VMEM((hid, width), low),
+            pltpu.VMEM((hid, width), low),
+            pltpu.VMEM((hid, width), low),
+            pltpu.VMEM((rows, hid), low),
+            pltpu.VMEM((rows, hid), low),
+            pltpu.VMEM((rows, hid), low),
+            pltpu.VMEM((rows, width), low),
+            pltpu.VMEM((rows, width), low),
+            pltpu.VMEM((rows, 2 * HEAD_DIM), low),
+            pltpu.VMEM((rows, HEAD_DIM), f32),
+            pltpu.VMEM((rows, HEAD_DIM), f32),
+            pltpu.VMEM((rows, 4 * HEAD_DIM), low),
+            pltpu.VMEM((2, 256, width), low),
+        ]
+        + Scatter.scratch(width)
+        + Scatter.scratch(width)
+        + [
+            pltpu.SemaphoreType.DMA((3,)),
+            pltpu.SemaphoreType.DMA((2,)),
+            pltpu.SemaphoreType.DMA((copies,)),
+            pltpu.SemaphoreType.DMA((copies,)),
+        ],
+        compiler_params=pltpu.CompilerParams(
+            collective_id=1, has_side_effects=True, vmem_limit_bytes=60 << 20
+        ),
+        cost_estimate=pl.CostEstimate(
+            flops=36_000_000_000, bytes_accessed=60_000_000, transcendentals=4_000_000
+        ),
+    )(lengths, *args)
 
 
 def rms_scale(values, gain):
@@ -82,7 +718,6 @@
     w_up,
     w_down,
 ):
-    low = jnp.bfloat16
     tok_rows, width = tokens.shape
     shards = lax.axis_size("shard")
     rows = tok_rows * shards
@@ -129,12 +764,8 @@
     def prepare(projected, gain, count):
         return rotate(rms_scale(projected.reshape(rows, count, HEAD_DIM), gain), position)
 
-    q_rot, query_back = jax.vjp(
-        lambda p, g: prepare(p, g, group), proj[:, :q_cols], query_gain.astype(jnp.float32)
-    )
-    k_rot, key_back = jax.vjp(
-        lambda p, g: prepare(p, g, 1), proj[:, q_cols : q_cols + k_cols], key_gain.astype(jnp.float32)
-    )
+    q_rot = prepare(proj[:, :q_cols], query_gain.astype(f32), group)
+    k_rot = prepare(proj[:, q_cols : q_cols + k_cols], key_gain.astype(f32), 1)
     query = q_rot.astype(low)
     key = k_rot.astype(low)[:, 0]
     value = proj[:, q_cols + k_cols :].astype(low)
@@ -150,64 +781,50 @@
         .astype(low)
     )
     resid = inputs + scatter_sum(contract_rows(attended, w_o))
-    second_value, second_back = jax.vjp(rms_scale, resid, gain_two)
-    second = gather(second_value.astype(low))
-    grad_low = gather(cotangent.astype(low))
-    gate = contract_rows(second, w_gate)
-    up = contract_rows(second, w_up)
-    sigma = jax.nn.sigmoid(gate)
-    hidden = (gate * sigma * up).astype(low)
-    result = resid + scatter_sum(dot(hidden, w_down))
-    dhidden = contract_rows(grad_low, w_down)
-    dgate = (dhidden * up * sigma * (1.0 + gate * (1.0 - sigma))).astype(low)
-    dup = (dhidden * gate * sigma).astype(low)
-    dsecond = scatter_sum(dot(dgate, w_gate) + dot(dup, w_up))
-    ffn_grads = lax.psum(
-        tuple(
-            g.astype(low)
-            for g in (
-                contract_first(dgate, second),
-                contract_first(dup, second),
-                contract_first(hidden, grad_low),
-            )
-        ),
-        "rep",
-    )
-    grad_resid_part, grad_second_gain = second_back(dsecond)
-    grad_resid = cotangent + grad_resid_part
-    branch = gather(grad_resid.astype(low))
-    grad_att = dot(branch, w_o).astype(low)
-    grad_heads = grad_att.reshape(rows, group, HEAD_DIM)
-    dprobs = jnp.einsum("tgd,sd->gts", grad_heads, value, preferred_element_type=jnp.float32)
-    inner = jnp.sum(weights * dprobs, axis=-1, keepdims=True)
-    dscores = (weights * (dprobs - inner)).astype(low)
-    dquery = jnp.einsum("gts,sd->tgd", dscores, key, preferred_element_type=jnp.float32) * scale
-    dkey = jnp.einsum("gts,tgd->sd", dscores, query, preferred_element_type=jnp.float32) * scale
-    dvalue = jnp.einsum("gts,tgd->sd", probs, grad_heads, preferred_element_type=jnp.float32)
-    dq_proj, grad_query_part = query_back(dquery)
-    dk_proj, grad_key_part = key_back(dkey[:, None])
-    d_qkv = jnp.concatenate(
-        [dq_proj.astype(low), dk_proj.astype(low), dvalue.astype(low)], axis=1
-    )
-    grad_first = scatter_sum(contract_rows(d_qkv, w_qkv))
-    attn_grads = lax.psum(
-        jnp.concatenate(
-            [contract_first(first, d_qkv), contract_first(branch, attended)], axis=1
-        ).astype(low),
-        "rep",
-    )
+    half = HEAD_DIM // 2
+    frequency = theta_base ** (-jnp.arange(half, dtype=f32) * (2.0 / HEAD_DIM))
+    angles = position.astype(f32)[:, None] * frequency[None, :]
+    cosine = jnp.concatenate([jnp.cos(angles)] * 2, axis=1)
+    sine = jnp.concatenate([-jnp.sin(angles), jnp.sin(angles)], axis=1)
+    kept = jnp.concatenate(
+        [
+            proj[:, : q_cols + k_cols],
+            total[0],
+            total[1],
+            jnp.zeros((rows, HEAD_DIM - 2), f32),
+        ],
+        axis=1,
+    )
+    result, grad_tokens, gain_parts, attn_grads, ffn_grads = late_call(
+        lengths,
+        resid,
+        cotangent,
+        tokens,
+        gain_one[None],
+        gain_two[None],
+        query_gain.astype(f32)[None],
+        key_gain.astype(f32)[None],
+        kept,
+        cosine,
+        sine,
+        mine,
+        jnp.concatenate([query.reshape(rows, q_cols), key, value, attended], axis=1),
+        first,
+        w_gate,
+        w_up,
+        w_down,
+    )
+    ffn_grads = lax.psum(ffn_grads, "rep").astype(f32)
+    attn_grads = lax.psum(attn_grads, "rep")
     attn_grads = lax.all_to_all(
         attn_grads.reshape(shards, feat, -1), "shard", split_axis=0, concat_axis=1, tiled=True
-    ).reshape(shards, feat, -1).transpose(1, 0, 2).astype(jnp.float32)
+    ).reshape(shards, feat, -1).transpose(1, 0, 2).astype(f32)
     grad_query = attn_grads[:, :, :q_cols].reshape(feat, -1)
     grad_key = attn_grads[:, :, q_cols : q_cols + k_cols].reshape(feat, -1)
     grad_value = attn_grads[:, :, q_cols + k_cols : qkv_cols].reshape(feat, -1)
     grad_out = attn_grads[:, :, qkv_cols:].reshape(feat, -1)
-    first_back = jax.vjp(rms_scale, inputs, gain_one)[1]
-    grad_input_part, grad_first_gain = first_back(grad_first)
-    grad_tokens = grad_resid + grad_input_part
     gains = lax.psum(
-        jnp.concatenate([grad_first_gain, grad_second_gain, grad_query_part, grad_key_part]),
+        jnp.concatenate([gain_parts[1], gain_parts[0], gain_parts[2, : 2 * HEAD_DIM]]),
         ("rep", "shard"),
     )
     head_piece = HEAD_DIM // shards
@@ -224,9 +841,9 @@
         grad_key,
         grad_value,
         grad_out,
-        ffn_grads[0].astype(jnp.float32),
-        ffn_grads[1].astype(jnp.float32),
-        ffn_grads[2].astype(jnp.float32),
+        ffn_grads[0],
+        ffn_grads[1],
+        ffn_grads[2],
         gains_first,
         gains_second,
         gains_query,

time: 891 us -> 735 us (0.82)
  waiting for transfers between devices: 539 us -> 301 us
  Pallas kernels: 0 us -> 192 us
  matrix products: 110 us -> 18.2 us
  other arithmetic: 63.7 us -> 53.1 us
    pallas_call x0 -> x1, Pallas kernels: none -> 192 us  [late_call(): pl.pallas_call(functools.partial(late_kernel, 1.0 / math.sqrt(HEAD_DIM)),...]
    reduce_scatter x4 -> x1, waiting for transfers between devices: 186 us -> 37.5 us  [scatter_sum(): lax.psum_scatter(x.astype(jnp.bfloat16), 'shard', scatter_dimension=0, ti...]
    all_to_all x1, waiting for transfers between devices: 64.4 us -> 0.01 us  [per_device(): lax.all_to_all(packed, 'shard', split_axis=1, concat_axis=0, tiled=True)]
    all_gather x4 -> x1, waiting for transfers between devices: 128 us -> 79.7 us  [gather(): return lax.all_gather(x, 'shard', axis=0, tiled=True)]
    dot_general x9 -> x0, matrix products: 37.2 us -> none  [the longest x5 23.9 us: contract_first(): lax.dot_general(left, right, (((0,), (0,)), ((), ())), preferred_element_...]
    dot_general x5 -> x1, matrix products: 34.1 us -> 4.55 us  [contract_rows(): lax.dot_general(left, right, (((1,), (1,)), ((), ())), preferred_element_...]
    dot_general x5 -> x1, matrix products: 33.1 us -> 5.24 us  [dot(): return jnp.dot(left, right, preferred_element_type=jnp.float32)]
    psum x1, waiting for transfers between devices: 161 us -> 184 us  [per_device(): attn_grads = lax.psum(attn_grads, 'rep')]
  transfers between devices with their start and end apart: 11 -> 5, of which waited for: 9 -> 3; matrix products, arithmetic and copies ran while one was open for 10% -> 9% of each run, Pallas kernels for 0% -> 0%
where the time goes in v2:
time: 735 us; the launch traced here: 726 us
  waiting for transfers between devices  301 us (41%)
  Pallas kernels  192 us (26%)
  blocking collectives  91.4 us (12%)
  other arithmetic  53.1 us (7%)
  local copies, waits for them, and re-layouts  42.6 us (6%)
  matrix products  18.2 us (2%)
  between operations  16 us (2%)
  starting transfers between devices  11.6 us (2%)
    pallas_call x1, Pallas kernels, late_call(): pl.pallas_call(functools.partial(late_kernel, 1.0 / math.sqrt(HEAD_DIM)),...  192 us
    psum x1, waiting for transfers between devices, per_device(): attn_grads = lax.psum(attn_grads, 'rep')  184 us
    psum x1, blocking collectives, per_device(): lax.psum(jnp.concatenate([gain_parts[1], gain_parts[0], gain_parts[2, :2...  91.4 us
    all_gather x1, waiting for transfers between devices, gather(): return lax.all_gather(x, 'shard', axis=0, tiled=True)  79.7 us
    reduce_scatter x1, waiting for transfers between devices, scatter_sum(): lax.psum_scatter(x.astype(jnp.bfloat16), 'shard', scatter_dimension=0, ti...  37.5 us
  transfers between devices with their start and end apart: 5, of which 3 were waited for; matrix products, arithmetic and copies ran while one was open for 9% of the time, Pallas kernels for 0%

profile of v2, /device:TPU:1, one launch (start us, length us, event | category | flops | bytes accessed | tf_op | source)
XLA Modules:
  0.0 725.6 jit_solution(13775703435995359200)
XLA Ops:
  7.3 0.8 pad_maximum_fusion.5
  8.1 1.9 pad_maximum_fusion.1
  10.1 1.3 copy_bitcast_fusion.5
  11.6 1.8 pad_maximum_fusion
  13.4 7.0 all-to-all-start
  23.0 3.2 fusion.24
  26.7 1.6 fusion.4
  28.3 79.7 %all-gather.2.cloned.1.call-done = bf16[1152,2048]{1,0:T(8,128)(2,1)} async-done(((bf16[144,2048]{1,0:T(8,128)(2,1)}), bf16[1152,2048]{1,0:T(8,128)(2,1)}) %all-gather.2.cloned.1.call-update) | async-done | bytes 4718608 | tf_op jit(solution)/shard_map/all_gather | solution.py:696
  108.0 3.1 multiply_reduce_fusion
  111.1 0.8 fusion.28
  111.9 3.2 slice_convert_fusion
  115.1 2.8 fusion.1.first_hbm
  117.9 5.2 fusion.6
  123.1 1.0 slice.121
  124.3 2.5 copy.49
  127.5 2.4 fusion.23
  130.0 1.7 multiply_multiply_fusion
  131.7 1.7 multiply_subtract_fusion
  133.4 2.1 fusion.2
  135.6 2.5 exponential_reduce_fusion
  138.1 0.8 copy-done.2
  139.1 6.3 fusion.8
  146.2 4.6 convolution_convert_fusion
  150.9 0.9 copy-done.4
  151.8 1.0 pad_maximum_fusion.2.cosine
  152.8 2.0 pad_maximum_fusion.3.sine
  154.8 2.0 copy.64
  156.8 1.2 slice.126
  158.6 1.9 copy.67
  161.0 1.5 copy_bitcast_fusion.4
  162.6 3.7 concatenate.49.heads_hbm
  166.3 1.7 maximum_maximum_fusion.proj
  167.9 37.5 %reduce-scatter.2.cloned.1.call-done = bf16[128,2048]{1,0:T(8,128)(2,1)} async-done(((bf16[1024,2048]{1,0:T(8,128)(2,1)}), bf16[128,2048]{1,0:T(8,128)(2,1)}) %reduce-scatter.2.cloned.1.call-update) | async-done | bytes 524304 | tf_op jit(solution)/shard_map/reduce_scatter | solution.py:700
  205.4 2.1 convert_add_fusion.resid
  207.6 191.8 %late.1 = (f32[128,2048]{1,0:T(8,128)}, f32[128,2048]{1,0:T(8,128)}, f32[8,2048]{1,0:T(8,128)}, bf16[2048,768]{1,0:T(8,128)(2,1)}, bf16[3,768,2048]{2,1,0:T(8,128)(2,1)}) custom-call(s32[1,3]{1,0:T(1,128)} %lengths.1, f32[128,2048]{1,0:T(8,128)} %convert_add_fusion.resid, f32[128,2048]{1,0:T(8,128)} %cotangent.1, bf16[128,2048]{1,0:T(8,128)(2,1)} %tokens.1, ...), custom_call_target="tpu_custom_call" | custom-call | flops 35999997952 | bytes 60000000 | tf_op jit(solution)/shard_map/late/pallas_call | solution.py:606
  399.4 183.7 %all-reduce.3.cloned.1.call-done = (bf16[8,256,768]{2,1,0:T(8,128)(2,1)}, bf16[3,768,2048]{2,1,0:T(8,128)(2,1)}) async-done(((bf16[8,256,768]{2,1,0:T(8,128)(2,1)}, bf16[3,768,2048]{2,1,0:T(8,128)(2,1)}), (bf16[8,256,768]{2,1,0:T(8,128)(2,1)}, bf16[3,768,2048]{2,1,0:T(8,128)(2,1)})) %all-reduce.3.cloned.1.call-update) | async-done | bytes 12582928 | tf_op jit(solution)/shard_map/psum | solution.py:818
  583.2 4.5 all-to-all-start.1
  588.4 0.9 fusion.29
  589.3 91.4 %psum.23 = f32[4352]{0:T(1024)S(1)} all-reduce(f32[4352]{0:T(1024)S(1)} %pad_maximum_fusion.4), channel_id=1, replica_groups=mesh['rep'=16,'shard'=8] {'rep','shard'}, use_global_device_ids=true, to_apply=%region_8.9 | all-reduce | flops 4352 | bytes 34816 | tf_op jit(solution)/shard_map/psum | solution.py:826
  681.9 12.5 %convert_element_type.157 = f32[3,768,2048]{2,1,0:T(8,128)} convert(bf16[3,768,2048]{2,1,0:T(8,128)(2,1)} %get-tuple-element.24) | non-fusion elementwise | flops 4718592 | bytes 28311552 | tf_op jit(solution)/shard_map/convert_element_type | solution.py:817
  694.5 13.7 %slice_bitcast_fusion = (f32[768,2048]{1,0:T(8,128)}, f32[768,2048]{1,0:T(8,128)}, f32[768,2048]{1,0:T(8,128)}) fusion(f32[3,768,2048]{2,1,0:T(8,128)} %convert_element_type.157), kind=kLoop, calls=%fused_computation.8 | loop fusion | bytes 37748736 | tf_op jit(solution)/shard_map/squeeze | solution.py:846
  708.2 2.4 convert_bitcast_fusion
  711.3 1.6 copy.73
  712.9 1.6 copy.76
  714.5 1.1 copy.84
  715.6 1.1 copy.85
  716.7 1.0 copy.90
  717.7 1.0 copy.91
  (80 shorter events, 7.7 us)
Async XLA Ops:
  7.2 2.9 copy-start
  7.2 4.2 copy-start.13
  7.2 4.2 copy-start.12
  7.2 100.8 %all-gather.2.cloned.1.call-start = ((), (), s32[]{:S(2)}) async-start(), calls=%async_computation.3 | async-start | bytes 5308416 | tf_op jit(solution)/shard_map/all_gather | solution.py:696
  13.4 7.1 copy-start.19
  13.4 12.8 %copy-start.20 = (bf16[128]{0:T(256)(128)(2,1)S(1)}, bf16[128]{0:T(256)(128)(2,1)}, u32[]{:S(2)}) copy-start(bf16[128]{0:T(256)(128)(2,1)} %param.19) | copy-start | bytes 772
  13.4 12.8 %copy-start.21 = (bf16[128]{0:T(256)(128)(2,1)S(1)}, bf16[128]{0:T(256)(128)(2,1)}, u32[]{:S(2)}) copy-start(bf16[128]{0:T(256)(128)(2,1)} %param.20) | copy-start | bytes 772
  13.4 104.5 %all-to-all-start = ((bf16[256,8,768]{2,0,1:T(8,128)(2,1)}), bf16[256,8,768]{2,0,1:T(8,128)(2,1)}, u32[]{:S(2)}, u32[]{:S(2)}) async-start(bf16[256,8,768]{2,0,1:T(8,128)(2,1)} %pad_maximum_fusion), calls=%async_computation | async-start | bytes 6291456 | tf_op jit(solution)/shard_map/all_to_all | solution.py:743
  20.4 185.0 %reduce-scatter.2.cloned.1.call-start = ((), (), s32[]{:S(2)}) async-start(), calls=%async_computation.4 | async-start | bytes 4718592 | tf_op jit(solution)/shard_map/reduce_scatter | solution.py:700
  111.8 3.3 copy-start.18
  127.5 5.9 copy-start.5
  130.0 5.6 copy-start.16
  130.0 5.6 copy-start.17
  133.4 2.2 copy-start.8
  133.4 2.2 copy-start.9
  135.6 3.3 copy-start.2
  139.1 6.3 copy-start.14
  145.4 0.8 copy-start.6
  150.7 1.0 copy-start.4
  150.7 2.0 copy-start.3
  150.7 432.4 %all-reduce.3.cloned.1.call-start = ((), (), s32[]{:S(2)}) async-start(), calls=%async_computation.5 | async-start | bytes 25165824 | tf_op jit(solution)/shard_map/psum | solution.py:818
  156.8 5.7 copy-start.15
  166.2 39.2 %copy-start.7 = (bf16[128,2048]{1,0:T(8,128)(2,1)S(1)}, bf16[128,2048]{1,0:T(8,128)(2,1)}, u32[]{:S(2)}) copy-start(bf16[128,2048]{1,0:T(8,128)(2,1)} %tokens.1) | copy-start | bytes 1572868
  583.2 125.0 %all-to-all-start.1 = ((bf16[8,256,768]{2,1,0:T(8,128)(2,1)}), bf16[8,256,768]{2,1,0:T(8,128)(2,1)}, u32[]{:S(2)}, u32[]{:S(2)}) async-start(bf16[8,256,768]{2,1,0:T(8,128)(2,1)} %get-tuple-element.23), calls=%async_computation.2 | async-start | bytes 6291456 | tf_op jit(solution)/shard_map/all_to_all | solution.py:819
  712.9 3.8 copy-start.11
  714.5 3.2 copy-start.10
  714.5 4.1 copy-start.1
Sparse Core Ops, SparseCore 0:
  10.3 97.6 all-gather.1
  150.9 54.5 reduce-scatter.1
  399.6 183.5 all-reduce.2

commit v3 on v2

--- a/solution.py
+++ b/solution.py
@@ -40,8 +40,9 @@
 class Place:
     def __init__(self):
         self.rep = lax.axis_index("rep")
-        shard = lax.axis_index("shard")
-        self.yl, self.z = shard // 4, shard % 4
+        self.shard = lax.axis_index("shard")
+        self.yl, self.z = self.shard // 4, self.shard % 4
+        self.yh, self.x, self.core = self.rep // 8, (self.rep // 2) % 4, self.rep % 2
 
     def block(self, dy, dz):
         return ((self.yl + dy + 2) % 2) * 4 + (self.z + dz + 8) % 4
@@ -49,17 +50,33 @@
     def dev(self, dy, dz):
         return (self.rep, self.block(dy, dz))
 
+    def x_at(self, dx):
+        return (self.x + dx + 8) % 4
+
+    def rep_dev(self, dyh, dx, dcore):
+        rep = ((self.yh + dyh) % 2) * 8 + self.x_at(dx) * 2 + (self.core + dcore) % 2
+        return (rep, self.shard)
+
     def rows(self, dy, dz, start=0, count=BLOCK):
         return pl.ds(pl.multiple_of(self.block(dy, dz) * BLOCK + start, 32), count)
 
     def line(self, dy):
         return pl.multiple_of(((self.yl + dy + 2) % 2) * LINE, LINE)
 
+    def shard_peers(self):
+        return [self.dev(dy, dz) for dy in range(2) for dz in range(4) if dy or dz]
+
+    def rep_peers(self):
+        return [
+            self.rep_dev(*by) for by in ((0, 0, 1), (0, 1, 0), (0, 2, 0), (0, 3, 0), (1, 0, 0))
+        ]
+
     def greet(self):
         barrier = pltpu.get_barrier_semaphore()
-        for peer in ((1, 0), (0, 1), (0, 3)):
-            pl.semaphore_signal(barrier, inc=1, device_id=self.dev(*peer), device_id_type=MESH)
-        pl.semaphore_wait(barrier, 3)
+        peers = self.shard_peers() + self.rep_peers()
+        for peer in peers:
+            pl.semaphore_signal(barrier, inc=1, device_id=peer, device_id_type=MESH)
+        pl.semaphore_wait(barrier, len(peers))
 
 
 class Net:
@@ -240,6 +257,111 @@
         for ref in (self.far.at[kind, 0], self.far.at[kind, 1], extra):
             out = out + ref[...].astype(f32)
         return out
+
+    def finish(self):
+        self.net.finish()
+
+
+def add_rows(into, start, count, *refs):
+    step = 64 if count % 64 == 0 else 48
+
+    @pl.loop(0, count // step)
+    def _(i):
+        at = pl.multiple_of(i * step, 16)
+        rows = pl.ds(pl.multiple_of(start + at, 16), step)
+        total = into[rows, :].astype(f32)
+        for ref in refs:
+            total = total + ref[pl.ds(at, step), :].astype(f32)
+        into[rows, :] = total.astype(low)
+
+
+class RepSum:
+    COPIES = 15
+
+    def __init__(self, place, sems, own, other, landed, near, far, cross, out, unit, out_unit):
+        self.place, self.net = place, Net(*sems)
+        self.own, self.other, self.landed = own, other, landed
+        self.near, self.far, self.cross = near, far, cross
+        self.out, self.unit, self.out_unit = out, unit, out_unit
+
+    def chunk(self, dx, start=0, count=None):
+        at = self.place.x_at(dx) * 2 * self.unit + start
+        return pl.ds(pl.multiple_of(at, 16), 2 * self.unit if count is None else count)
+
+    def out_rows(self, dcore, dx, start=0, count=None):
+        core = (self.place.core + dcore) % 2
+        at = (core * 8 + self.place.x_at(dx) * 2 + start) * self.out_unit
+        count = (2 if count is None else count) * self.out_unit
+        return self.out.at[pl.ds(pl.multiple_of(at, 16), count)]
+
+    def core_send(self):
+        self.net.send("core", self.other, self.landed, self.place.rep_dev(0, 0, 1), self.landed)
+
+    def x_first(self, load=None):
+        self.net.wait("core")
+        add_rows(self.own, 0, 8 * self.unit, self.landed if load is None else load())
+        for e, d in enumerate((1, 3)):
+            src = self.own.at[self.chunk(2, e * self.unit, self.unit)]
+            dst = self.near[e]
+            self.net.send(f"near{e}", src, dst, self.place.rep_dev(0, d, 0), dst)
+
+    def x_second(self):
+        for e, d in enumerate((1, 3)):
+            self.net.wait(f"near{e}")
+            add_rows(self.own, self.place.x_at(d) * 2 * self.unit + e * self.unit, self.unit, self.near[e])
+            dst = self.far[e]
+            self.net.send(
+                f"far{e}", self.own.at[self.chunk(d)], dst, self.place.rep_dev(0, d, 0), dst
+            )
+
+    def y_send(self):
+        for e in range(2):
+            self.net.wait(f"far{e}")
+        add_rows(self.own, self.place.x * 2 * self.unit, 2 * self.unit, *self.far)
+        src = self.own.at[self.chunk(0, (1 - self.place.yh) * self.unit, self.unit)]
+        self.net.send("cross", src, self.cross, self.place.rep_dev(1, 0, 0), self.cross)
+
+    def piece(self):
+        self.net.wait("cross")
+        at = (self.place.x * 2 + self.place.yh) * self.unit
+        add_rows(self.own, at, self.unit, self.cross)
+        return self.own.at[pl.ds(pl.multiple_of(at, 16), self.unit)]
+
+    def y_gather(self, piece, sem):
+        mine = self.out_rows(0, 0, self.place.yh, 1)
+        copy = pltpu.make_async_copy(piece, mine, sem)
+        copy.start()
+        self.net.send(
+            "y", piece, mine, self.place.rep_dev(1, 0, 0), self.out_rows(0, 0, 1 - self.place.yh, 1)
+        )
+        copy.wait()
+
+    def to_core(self, dx):
+        rows = self.out_rows(0, dx)
+        self.net.send(
+            f"core{dx}", rows, rows, self.place.rep_dev(0, 0, 1), self.out_rows(1, dx)
+        )
+
+    def x_gather(self):
+        self.net.wait("y")
+        rows = self.out_rows(0, 0)
+        for d in (1, 3):
+            self.net.send(f"x{d}", rows, rows, self.place.rep_dev(0, d, 0), self.out_rows(0, -d))
+        self.to_core(0)
+
+    def x_forward(self):
+        for e, d in enumerate((1, 3)):
+            self.net.wait(f"x{d}")
+            rows = self.out_rows(0, -d, e, 1)
+            self.net.send(
+                f"xx{d}", rows, rows, self.place.rep_dev(0, d, 0), self.out_rows(0, -2 * d, e, 1)
+            )
+            self.to_core(-d)
+
+    def x_last(self):
+        for d in (1, 3):
+            self.net.wait(f"xx{d}")
+        self.to_core(2)
 
     def finish(self):
         self.net.finish()
@@ -282,14 +404,14 @@
     gains,
     attn_grads,
     ffn_grads,
+    core_landed,
     second,
     cot_all,
     branch,
     w_gate,
     w_up,
     w_down,
-    hidden,
-    d_gate,
+    pair,
     d_up,
     part_out,
     part_back,
@@ -298,20 +420,25 @@
     d_value,
     d_qkv,
     staged,
-    o_across,
-    o_near,
-    o_far,
-    o_last,
-    b_across,
-    b_near,
-    b_far,
-    b_last,
+    across,
+    near,
+    far,
+    last,
+    swapped,
+    assembled,
+    gain_sums,
+    gain_landed,
+    free_sem,
+    core_free_sem,
+    landing_free,
+    heads_free,
     local_sems,
-    stage_sems,
     send_sems,
     recv_sems,
 ):
     place = Place()
+    hidden = pair.at[pl.ds(0, 8 * BLOCK)]
+    d_gate = pair.at[pl.ds(8 * BLOCK, 8 * BLOCK)]
     rows_all = 8 * BLOCK
     hid = w_gate.shape[0]
     width = second.shape[1]
@@ -340,12 +467,9 @@
     gather_second = Gather(place, second, *sems(Gather.COPIES))
     gather_cot = Gather(place, cot_all, *sems(Gather.COPIES))
     gather_branch = Gather(place, branch, *sems(Gather.COPIES))
-    scatter_out = Scatter(
-        place, part_out, o_across, o_near, o_far, o_last, *sems(Scatter.COPIES)
-    )
-    scatter_back = Scatter(
-        place, part_back, b_across, b_near, b_far, b_last, *sems(Scatter.COPIES)
-    )
+    landing = (across, near, far, last)
+    scatter_out = Scatter(place, part_out, *landing, *sems(Scatter.COPIES))
+    scatter_back = Scatter(place, part_back, *landing, *sems(Scatter.COPIES))
 
     def feed_forward(dy):
         rows = pl.ds(place.line(dy), LINE)
@@ -386,18 +510,46 @@
                 mm(d_gate[rows, :], w_gate[:, cols]) + mm(d_up[rows, :], w_up[:, cols])
             ).astype(low)
 
-    stores = [None, None]
-
-    def weight_grad(which, left, right):
-        for i in range(hid // 256):
-            slot = (which * (hid // 256) + i) % 2
-            if stores[slot] is not None:
-                stores[slot].wait()
-            staged[slot] = mm_tn(left[:, pl.ds(i * 256, 256)], right[...]).astype(low)
-            stores[slot] = pltpu.make_async_copy(
-                staged.at[slot], ffn_grads.at[which, pl.ds(i * 256, 256)], stage_sems.at[slot]
+    def weight_grad(into, left, right):
+        @pl.loop(0, hid // 256)
+        def _(i):
+            cols = pl.ds(pl.multiple_of(i * 256, 256), 256)
+            into[cols, :] = mm_tn(left[:, cols], right[...]).astype(low)
+
+    unit = hid // 16
+    sums = []
+    for i, whole in enumerate((w_gate, w_up, w_down)):
+        base = i * 7 * unit
+
+        def view(start, count, base=base):
+            return second.at[pl.ds(base + start * unit, count * unit)]
+
+        sums.append(
+            RepSum(
+                place,
+                sems(RepSum.COPIES),
+                whole.at[pl.ds(pl.multiple_of(place.core * 8 * unit, 16), 8 * unit)],
+                whole.at[pl.ds(pl.multiple_of((1 - place.core) * 8 * unit, 16), 8 * unit)],
+                core_landed.at[i],
+                [view(0, 1), view(1, 1)],
+                [view(2, 2), view(4, 2)],
+                view(6, 1),
+                ffn_grads.at[i],
+                unit,
+                unit,
             )
-            stores[slot].start()
+        )
+    sum_gate, sum_up, sum_down = sums
+
+    def load_landed(i):
+        def load():
+            here = staged.at[pl.ds(0, 8 * unit)]
+            copy = pltpu.make_async_copy(core_landed.at[i], here, local_sems.at[3])
+            copy.start()
+            copy.wait()
+            return here
+
+        return load
 
     for step in gather_second.steps():
         step()
@@ -420,12 +572,22 @@
     scatter_back.send_other()
     feed_backward(0)
     scatter_back.send_own()
-    weight_grad(0, d_gate, second)
+    weight_grad(w_gate, d_gate, second)
+    sum_gate.core_send()
     scatter_back.step_one()
-    weight_grad(1, d_up, second)
+    weight_grad(w_up, d_up, second)
+    sum_up.core_send()
+    gather_second.finish()
+    for by in ((0, 1, 0), (0, 3, 0), (1, 0, 0)):
+        pl.semaphore_signal(
+            free_sem, inc=1, device_id=place.rep_dev(*by), device_id_type=MESH
+        )
     scatter_back.step_two()
-    weight_grad(2, hidden, cot_all)
-    gather_second.finish()
+    weight_grad(w_down, hidden, cot_all)
+    sum_down.core_send()
+    pl.semaphore_wait(free_sem, 3)
+    sum_gate.x_first(load_landed(0))
+    sum_up.x_first(load_landed(1))
     gather_cot.finish()
     heads = d_up
     q_cols = 2 * HEAD_DIM
@@ -459,16 +621,28 @@
         grad_tokens[rows, :] = cotangent[rows, :] + back
         gain_part = jnp.sum(gain_part, axis=0, keepdims=True)
         gain_rows = gain_part if gain_rows is None else gain_rows + gain_part
-    gains[...] = jnp.zeros_like(gains)
-    gains[0:1, :] = gain_rows
+    gain_sums[0] = jnp.zeros_like(gain_sums[0])
+
+    def keep_gain(first_row, value):
+        for i in range(value.shape[1] // HEAD_DIM):
+            gain_sums[0, first_row + i : first_row + i + 1, :] = value[
+                :, i * HEAD_DIM : (i + 1) * HEAD_DIM
+            ]
+
+    gain_slots = width // HEAD_DIM
+    keep_gain(gain_slots, gain_rows)
     branch[own, :] = grad_tokens[...].astype(low)
     gather_branch.start()
+    sum_down.x_first(load_landed(2))
+    gather_branch.step_one()
+    sum_gate.x_second()
+    gather_branch.step_two()
     scatter_out.send_other()
     scatter_out.send_own()
-    gather_branch.step_one()
-    gather_branch.step_two()
+    sum_up.x_second()
     gather_branch.step_three()
     gather_branch.step_four()
+    sum_down.x_second()
     gather_branch.own_line()
     for load in loads:
         load.wait()
@@ -518,28 +692,37 @@
             gain_rows = gain_rows + jnp.sum(gain_part, axis=0, keepdims=True)
             d_key[0:seen, :] += mm_tn(d_scores, query[rows, lanes])
             d_value[0:seen, :] += mm_tn(weights.astype(low), d_att[rows, lanes])
+        if part == 0:
+            sum_gate.y_send()
         if part == 1:
             scatter_out.step_two()
+            sum_up.y_send()
+            sum_gate.y_gather(sum_gate.piece(), local_sems.at[3])
         if part == 2:
             scatter_out.step_three()
+            sum_down.y_send()
+            sum_up.y_gather(sum_up.piece(), local_sems.at[3])
+            sum_gate.x_gather()
     d_qkv[:, 3 * HEAD_DIM :] = d_value[...].astype(low)
 
-    gains[2:3, 0:HEAD_DIM] = gain_rows
+    keep_gain(2 * gain_slots, gain_rows)
     lanes = pl.ds(2 * HEAD_DIM, HEAD_DIM)
     back, gain_part = unrotate(pl.ds(0, rows_all), d_key[...] * scale, proj[:, lanes], key_gain[...])
     d_qkv[:, lanes] = back.astype(low)
-    gains[2:3, HEAD_DIM : 2 * HEAD_DIM] = jnp.sum(gain_part, axis=0, keepdims=True)
+    keep_gain(2 * gain_slots + 1, jnp.sum(gain_part, axis=0, keepdims=True))
 
     scatter_back.finish()
-    scatter_first = Scatter(
-        place, part_back, b_across, b_near, b_far, b_last, *sems(Scatter.COPIES)
-    )
+    scatter_first = Scatter(place, part_back, *landing, *sems(Scatter.COPIES))
     for half in (0, 1):
         rows = pl.ds(half * HALF, HALF)
         result[rows, :] = resid[rows, :] + scatter_out.total(half)
     scatter_out.finish()
-    load = pltpu.make_async_copy(first_hbm, second, local_sems.at[0])
+    for by in ((1, 0), (0, 1), (0, 3)):
+        pl.semaphore_signal(landing_free, inc=1, device_id=place.dev(*by), device_id_type=MESH)
+    load = pltpu.make_async_copy(first_hbm, part_out, local_sems.at[0])
     load.start()
+    sum_down.y_gather(sum_down.piece(), local_sems.at[3])
+    sum_up.x_gather()
 
     def into_first(dy):
         rows = pl.ds(place.line(dy), LINE)
@@ -555,30 +738,56 @@
                 ).astype(low)
 
     into_first(1)
+    pl.semaphore_wait(landing_free, 3)
     scatter_first.send_other()
     into_first(0)
     scatter_first.send_own()
+    for by in ((0, 1, 0), (0, 3, 0), (1, 0, 0)):
+        pl.semaphore_signal(
+            heads_free, inc=1, device_id=place.rep_dev(*by), device_id_type=MESH
+        )
+    head_landed = cot_all.at[:, pl.ds(0, 6 * HEAD_DIM)]
     load.wait()
 
-    def attention_grad(index, store):
-        @pl.loop(0, 4)
-        def _(i):
-            cols = pl.ds(pl.multiple_of(index * rows_all + i * 256, 256), 256)
-            rows = pl.ds(pl.multiple_of(i * 256, 256), 256)
-            store[rows, 0 : 4 * HEAD_DIM] = mm_tn(second[:, cols], d_qkv[...]).astype(low)
-            store[rows, 4 * HEAD_DIM :] = mm_tn(branch[:, cols], attended[...]).astype(low)
-
-        copy = pltpu.make_async_copy(
-            store, attn_grads.at[pl.ds(index * rows_all, rows_all)], local_sems.at[1 + index]
-        )
-        copy.start()
-        stores.append(copy)
-
-    attention_grad(0, hidden)
+    sum_attn = RepSum(
+        place,
+        sems(RepSum.COPIES),
+        pair.at[pl.ds(pl.multiple_of(place.core * rows_all, BLOCK), rows_all)],
+        pair.at[pl.ds(pl.multiple_of((1 - place.core) * rows_all, BLOCK), rows_all)],
+        d_up,
+        [head_landed.at[pl.ds(e * BLOCK, BLOCK)] for e in range(2)],
+        [head_landed.at[pl.ds((1 + e) * 2 * BLOCK, 2 * BLOCK)] for e in range(2)],
+        head_landed.at[pl.ds(6 * BLOCK, BLOCK)],
+        attn_grads,
+        BLOCK,
+        16,
+    )
+
+    @pl.loop(0, width // 256)
+    def _(i):
+        cols = pl.ds(pl.multiple_of(i * 256, 256), 256)
+        from_first = mm_tn(part_out[:, cols], d_qkv[...]).astype(low)
+        from_branch = mm_tn(branch[:, cols], attended[...]).astype(low)
+        for piece in range(16):
+            rows = pl.ds(pl.multiple_of(piece * BLOCK + i * 16, 16), 16)
+            pair[rows, 0 : 4 * HEAD_DIM] = from_first[piece * 16 : piece * 16 + 16, :]
+            pair[rows, 4 * HEAD_DIM :] = from_branch[piece * 16 : piece * 16 + 16, :]
+
+    pl.semaphore_signal(
+        core_free_sem, inc=1, device_id=place.rep_dev(0, 0, 1), device_id_type=MESH
+    )
+    pl.semaphore_wait(core_free_sem, 1)
+    sum_attn.core_send()
     scatter_first.step_one()
-    attention_grad(1, d_gate)
+    sum_gate.x_forward()
+    pl.semaphore_wait(heads_free, 3)
+    sum_attn.x_first()
     scatter_first.step_two()
+    sum_down.x_gather()
+    sum_up.x_forward()
     scatter_first.step_three()
+    sum_gate.x_last()
+    sum_attn.x_second()
     gain_rows = None
     for half in (1, 0):
         rows = pl.ds(half * HALF, HALF)
@@ -587,12 +796,78 @@
         grad_tokens[rows, :] += back
         gain_part = jnp.sum(gain_part, axis=0, keepdims=True)
         gain_rows = gain_part if gain_rows is None else gain_rows + gain_part
-    gains[1:2, :] = gain_rows
-
-    for store in stores:
-        store.wait()
+    keep_gain(0, gain_rows)
+
+    gain_net = Net(*sems(9))
+    stages = (
+        [place.dev(0, d) for d in (1, 2, 3)],
+        [place.dev(1, 0)],
+        [place.rep_dev(0, 0, 1)],
+        [place.rep_dev(0, d, 0) for d in (1, 2, 3)],
+        [place.rep_dev(1, 0, 0)],
+    )
+
+    def gain_send(stage):
+        for i, dev in enumerate(stages[stage]):
+            dst = gain_landed.at[3 * stage + i]
+            gain_net.send(f"{stage}.{i}", gain_sums.at[stage], dst, dev, dst)
+
+    def gain_add(stage):
+        total = gain_sums[stage]
+        for i in range(len(stages[stage])):
+            gain_net.wait(f"{stage}.{i}")
+            total = total + gain_landed[3 * stage + i]
+        gain_sums[stage + 1] = total
+
+    gain_send(0)
+    sum_attn.y_send()
+    sum_down.x_forward()
+    gain_add(0)
+    gain_send(1)
+    sum_up.x_last()
+    piece = sum_attn.piece()
+    swap_net = Net(*sems(7))
+    for dy in range(2):
+        for dz in range(4):
+            if dy or dz:
+                to = place.block(dy, dz)
+                src = piece.at[pl.ds(pl.multiple_of(to * 16, 16), 16)]
+                dst = swapped.at[pl.ds(pl.multiple_of(place.shard * 16, 16), 16)]
+                here = place.block(-dy, -dz)
+                here = swapped.at[pl.ds(pl.multiple_of(here * 16, 16), 16)]
+                swap_net.send(f"{dy}{dz}", src, dst, place.dev(dy, dz), here)
+    own_rows = pl.ds(pl.multiple_of(place.shard * 16, 16), 16)
+    swapped[own_rows, :] = piece[own_rows, :]
+    gain_add(1)
+    gain_send(2)
+    sum_down.x_last()
+    swap_net.finish()
+    kv = 8 * HEAD_DIM
+    for j in range(8):
+        rows = pl.ds(j * 16, 16)
+        at = 0
+        for begin, size in ((0, 2), (2, 1), (3, 1), (4, 2)):
+            assembled[:, at + j * size * HEAD_DIM : at + (j + 1) * size * HEAD_DIM] = swapped[
+                rows, begin * HEAD_DIM : (begin + size) * HEAD_DIM
+            ]
+            at += size * kv
+    sum_attn.y_gather(assembled, local_sems.at[3])
+    gain_add(2)
+    gain_send(3)
+    sum_attn.x_gather()
+    gain_add(3)
+    gain_send(4)
+    sum_attn.x_forward()
+    sum_attn.x_last()
+    gain_add(4)
+    gains[...] = gain_sums[5]
+
     gather_branch.finish()
     scatter_first.finish()
+    for one in sums:
+        one.finish()
+    sum_attn.finish()
+    gain_net.finish()
 
 
 def late_call(lengths, *args):
@@ -602,19 +877,21 @@
     vmem = pl.BlockSpec(memory_space=pltpu.VMEM)
     smem = pl.BlockSpec(memory_space=pltpu.SMEM)
     anywhere = pl.BlockSpec(memory_space=pl.ANY)
-    copies = 3 * Gather.COPIES + 3 * Scatter.COPIES
+    copies = 3 * Gather.COPIES + 3 * Scatter.COPIES + 4 * RepSum.COPIES + 9 + 7
+    gain_shape = (2 * width // HEAD_DIM + 8, HEAD_DIM)
     return pl.pallas_call(
         functools.partial(late_kernel, 1.0 / math.sqrt(HEAD_DIM)),
         name="late",
         out_shape=[
             jax.ShapeDtypeStruct((BLOCK, width), f32),
             jax.ShapeDtypeStruct((BLOCK, width), f32),
-            jax.ShapeDtypeStruct((8, width), f32),
-            jax.ShapeDtypeStruct((width, 6 * HEAD_DIM), low),
+            jax.ShapeDtypeStruct(gain_shape, f32),
+            jax.ShapeDtypeStruct((256, 3 * width), low),
             jax.ShapeDtypeStruct((3, hid, width), low),
+            jax.ShapeDtypeStruct((3, hid // 2, width), low),
         ],
         in_specs=[smem] + [vmem] * (len(args) - 6) + [anywhere] * 6,
-        out_specs=[vmem] * 3 + [anywhere] * 2,
+        out_specs=[vmem] * 3 + [pl.BlockSpec(memory_space=pltpu.HBM)] * 3,
         scratch_shapes=[
             pltpu.VMEM((rows, width), low),
             pltpu.VMEM((rows, width), low),
@@ -622,8 +899,7 @@
             pltpu.VMEM((hid, width), low),
             pltpu.VMEM((hid, width), low),
             pltpu.VMEM((hid, width), low),
-            pltpu.VMEM((rows, hid), low),
-            pltpu.VMEM((rows, hid), low),
+            pltpu.VMEM((2 * rows, hid), low),
             pltpu.VMEM((rows, hid), low),
             pltpu.VMEM((rows, width), low),
             pltpu.VMEM((rows, width), low),
@@ -631,13 +907,19 @@
             pltpu.VMEM((rows, HEAD_DIM), f32),
             pltpu.VMEM((rows, HEAD_DIM), f32),
             pltpu.VMEM((rows, 4 * HEAD_DIM), low),
-            pltpu.VMEM((2, 256, width), low),
+            pltpu.VMEM((hid // 2, width), low),
         ]
         + Scatter.scratch(width)
-        + Scatter.scratch(width)
         + [
-            pltpu.SemaphoreType.DMA((3,)),
-            pltpu.SemaphoreType.DMA((2,)),
+            pltpu.VMEM((BLOCK, 6 * HEAD_DIM), low),
+            pltpu.VMEM((16, 3 * width), low),
+            pltpu.VMEM((6,) + gain_shape, f32),
+            pltpu.VMEM((15,) + gain_shape, f32),
+            pltpu.SemaphoreType.REGULAR,
+            pltpu.SemaphoreType.REGULAR,
+            pltpu.SemaphoreType.REGULAR,
+            pltpu.SemaphoreType.REGULAR,
+            pltpu.SemaphoreType.DMA((4,)),
             pltpu.SemaphoreType.DMA((copies,)),
             pltpu.SemaphoreType.DMA((copies,)),
         ],
@@ -795,7 +1077,7 @@
         ],
         axis=1,
     )
-    result, grad_tokens, gain_parts, attn_grads, ffn_grads = late_call(
+    result, grad_tokens, gains, attn_grads, ffn_grads, _ = late_call(
         lengths,
         resid,
         cotangent,
@@ -814,19 +1096,13 @@
         w_up,
         w_down,
     )
-    ffn_grads = lax.psum(ffn_grads, "rep").astype(f32)
-    attn_grads = lax.psum(attn_grads, "rep")
-    attn_grads = lax.all_to_all(
-        attn_grads.reshape(shards, feat, -1), "shard", split_axis=0, concat_axis=1, tiled=True
-    ).reshape(shards, feat, -1).transpose(1, 0, 2).astype(f32)
-    grad_query = attn_grads[:, :, :q_cols].reshape(feat, -1)
-    grad_key = attn_grads[:, :, q_cols : q_cols + k_cols].reshape(feat, -1)
-    grad_value = attn_grads[:, :, q_cols + k_cols : qkv_cols].reshape(feat, -1)
-    grad_out = attn_grads[:, :, qkv_cols:].reshape(feat, -1)
-    gains = lax.psum(
-        jnp.concatenate([gain_parts[1], gain_parts[0], gain_parts[2, : 2 * HEAD_DIM]]),
-        ("rep", "shard"),
-    )
+    ffn_grads = ffn_grads.astype(f32)
+    attn_grads = attn_grads.astype(f32)
+    grad_query = attn_grads[:, :width]
+    grad_key = attn_grads[:, width : width + width // 2]
+    grad_value = attn_grads[:, width + width // 2 : 2 * width]
+    grad_out = attn_grads[:, 2 * width :]
+    gains = gains.reshape(-1)
     head_piece = HEAD_DIM // shards
     gains_first = lax.dynamic_slice_in_dim(gains, my_shard * feat, feat, 0)
     gains_second = lax.dynamic_slice_in_dim(gains, width + my_shard * feat, feat, 0)

time: 735 us -> 531 us (0.72)
  waiting for transfers between devices: 301 us -> 117 us
  blocking collectives: 91.4 us -> 0 us
  Pallas kernels: 192 us -> 270 us
    psum x1 -> x0, waiting for transfers between devices: 184 us -> none  [per_device(): attn_grads = lax.psum(attn_grads, 'rep')]
    psum x1 -> x0, blocking collectives: 91.4 us -> none  [per_device(): lax.psum(jnp.concatenate([gain_parts[1], gain_parts[0], gain_parts[2, :2...]
    pallas_call x1, Pallas kernels: 192 us -> 270 us  [late_call(): pl.pallas_call(functools.partial(late_kernel, 1.0 / math.sqrt(HEAD_DIM)),...]
    convert_element_type x2 -> x1, other arithmetic: 15 us -> 12.5 us  [per_device(): ffn_grads = ffn_grads.astype(f32)]
  transfers between devices with their start and end apart: 5 -> 3, of which waited for: 3 -> 2; matrix products, arithmetic and copies ran while one was open for 9% -> 7% of each run, Pallas kernels for 0% -> 0%
where the time goes in v3:
time: 531 us; the launch traced here: 522 us
  Pallas kernels  270 us (51%)
  waiting for transfers between devices  117 us (22%)
  other arithmetic  50.4 us (9%)
  local copies, waits for them, and re-layouts  42.7 us (8%)
  matrix products  18.2 us (3%)
  between operations  16.2 us (3%)
  starting transfers between devices  7.08 us (1%)
    pallas_call x1, Pallas kernels, late_call(): pl.pallas_call(functools.partial(late_kernel, 1.0 / math.sqrt(HEAD_DIM)),...  270 us
    all_gather x1, waiting for transfers between devices, gather(): return lax.all_gather(x, 'shard', axis=0, tiled=True)  79.7 us
    reduce_scatter x1, waiting for transfers between devices, scatter_sum(): lax.psum_scatter(x.astype(jnp.bfloat16), 'shard', scatter_dimension=0, ti...  37.5 us
    squeeze x1, local copies, waits for them, and re-layouts, per_device(): ffn_grads[2]  13.9 us
    convert_element_type x1, other arithmetic, per_device(): ffn_grads = ffn_grads.astype(f32)  12.5 us
  transfers between devices with their start and end apart: 3, of which 2 were waited for; matrix products, arithmetic and copies ran while one was open for 7% of the time, Pallas kernels for 0%

profile of v3, /device:TPU:1, one launch (start us, length us, event | category | flops | bytes accessed | tf_op | source)
XLA Modules:
  0.0 521.8 jit_solution(16632975650888240435)
XLA Ops:
  7.3 0.8 pad_maximum_fusion.4
  8.1 1.9 pad_maximum_fusion.1
  10.1 1.3 copy_bitcast_fusion.3
  11.6 1.8 pad_maximum_fusion
  13.4 7.0 %all-to-all-start = ((bf16[256,8,768]{2,0,1:T(8,128)(2,1)}), bf16[256,8,768]{2,0,1:T(8,128)(2,1)}, u32[]{:S(2)}, u32[]{:S(2)}) async-start(bf16[256,8,768]{2,0,1:T(8,128)(2,1)} %pad_maximum_fusion), calls=%async_computation | async-start | bytes 6291456 | tf_op jit(solution)/shard_map/all_to_all | solution.py:1025
  20.5 0.6 fusion.33
  22.4 0.7 subtract_convert_fusion
  23.0 3.2 fusion.24
  26.2 0.5 convert_bitcast_fusion
  26.7 1.6 fusion.4
  28.3 79.7 %all-gather.2.cloned.1.call-done = bf16[1152,2048]{1,0:T(8,128)(2,1)} async-done(((bf16[144,2048]{1,0:T(8,128)(2,1)}), bf16[1152,2048]{1,0:T(8,128)(2,1)}) %all-gather.2.cloned.1.call-update) | async-done | bytes 4718608 | tf_op jit(solution)/shard_map/all_gather | solution.py:978
  108.0 3.1 multiply_reduce_fusion
  111.1 0.8 fusion.28
  111.9 3.2 slice_convert_fusion
  115.1 2.8 fusion.1.first_hbm
  117.9 5.2 %fusion.6 = f32[1024,512]{0,1:T(8,128)S(1)} fusion(bf16[1024,2048]{1,0:T(8,128)(2,1)} %fusion.1.first_hbm, bf16[2048,768]{1,0:T(8,128)(2,1)} %bitcast.6.w_attn_hbm), kind=kOutput, calls=%fused_computation.18 | convolution fusion | flops 2147483648 | bytes 8388608 | tf_op jit(solution)/shard_map/dot_general | solution.py:962
  123.1 1.0 slice.109
  124.3 2.5 copy.45
  127.5 2.4 fusion.23
  130.0 1.7 multiply_multiply_fusion
  131.7 1.7 multiply_subtract_fusion
  133.4 2.1 fusion.2
  135.6 2.2 exponential_reduce_fusion
  137.8 1.1 copy-done.3
  139.1 6.3 %fusion.8 = bf16[128,2,1024]{2,0,1:T(8,128)(2,1)S(1)} fusion(f32[1024,1024,2]{1,0,2:T(8,128)} %copy-done.3, f32[2,1024]{1,0:T(2,128)S(1)} %log_add_fusion, pred[1024,1024]{0,1:T(8,128)(4,1)} %fusion.4, bf16[1024,128]{1,0:T(8,128)(2,1)S(1)} %copy.57), kind=kOutput, calls=%fused_computation.21 | convolution fusion | flops 545521664 | bytes 10231808 | tf_op jit(solution)/shard_map/gts,sd->tgd/dot_general | solution.py:1061
  145.4 0.8 copy-done.7
  146.2 4.6 convolution_convert_fusion
  150.9 0.9 copy-done.5
  151.8 1.0 pad_maximum_fusion.2.cosine
  152.8 2.0 pad_maximum_fusion.3.sine
  154.8 2.0 copy.56
  156.9 1.2 slice.114
  158.6 1.9 copy.59
  160.5 0.6 convert.18.gain_two
  161.1 1.5 copy_bitcast_fusion.2
  162.6 3.7 concatenate.46.heads_hbm
  166.3 1.7 maximum_maximum_fusion.proj
  168.0 37.5 %reduce-scatter.2.cloned.1.call-done = bf16[128,2048]{1,0:T(8,128)(2,1)} async-done(((bf16[1024,2048]{1,0:T(8,128)(2,1)}), bf16[128,2048]{1,0:T(8,128)(2,1)}) %reduce-scatter.2.cloned.1.call-update) | async-done | bytes 524304 | tf_op jit(solution)/shard_map/reduce_scatter | solution.py:982
  205.4 2.1 convert_add_fusion.resid
  207.6 270.1 %late.1 = (f32[128,2048]{1,0:T(8,128)}, f32[128,2048]{1,0:T(8,128)}, f32[40,128]{1,0:T(8,128)}, bf16[256,6144]{1,0:T(8,128)(2,1)}, bf16[3,768,2048]{2,1,0:T(8,128)(2,1)}, /*index=5*/bf16[3,384,2048]{2,1,0:T(8,128)(2,1)}) custom-call(s32[1,3]{1,0:T(1,128)} %lengths.1, f32[128,2048]{1,0:T(8,128)} %convert_add_fusion.resid, f32[128,2048]{1,0:T(8,128)} %cotangent.1, ...), custom_call_target="tpu_custom_call" | custom-call | flops 35999997952 | bytes 60000000 | tf_op jit(solution)/shard_map/late/pallas_call | solution.py:882
  477.7 4.2 fusion.29
  481.9 1.6 fusion.30
  483.5 12.5 %convert_element_type.153 = f32[3,768,2048]{2,1,0:T(8,128)} convert(bf16[3,768,2048]{2,1,0:T(8,128)(2,1)} %get-tuple-element.21) | non-fusion elementwise | flops 4718592 | bytes 28311552 | tf_op jit(solution)/shard_map/convert_element_type | solution.py:1099
  496.0 13.9 %slice_bitcast_fusion = (f32[768,2048]{1,0:T(8,128)}, f32[768,2048]{1,0:T(8,128)}, f32[768,2048]{1,0:T(8,128)}) fusion(f32[3,768,2048]{2,1,0:T(8,128)} %convert_element_type.153), kind=kLoop, calls=%fused_computation.8 | loop fusion | bytes 37748736 | tf_op jit(solution)/shard_map/squeeze | solution.py:1122
  509.9 1.3 fusion.32
  511.2 1.3 fusion.31
  512.5 1.0 copy.72
  513.5 1.0 copy.73
  (68 shorter events, 1.9 us)
Async XLA Ops:
  7.2 2.9 copy-start
  7.2 4.2 copy-start.14
  7.2 4.2 copy-start.13
  7.2 100.8 %all-gather.2.cloned.1.call-start = ((), (), s32[]{:S(2)}) async-start(), calls=%async_computation.2 | async-start | bytes 5308416 | tf_op jit(solution)/shard_map/all_gather | solution.py:978
  13.4 7.1 %copy-start.20 = (s32[1,3]{1,0:T(1,128)S(1)}, s32[1,3]{1,0:T(1,128)}, u32[]{:S(2)}) copy-start(s32[1,3]{1,0:T(1,128)} %lengths.1) | copy-start | bytes 40
  13.4 12.8 %copy-start.21 = (bf16[128]{0:T(256)(128)(2,1)S(1)}, bf16[128]{0:T(256)(128)(2,1)}, u32[]{:S(2)}) copy-start(bf16[128]{0:T(256)(128)(2,1)} %param.19) | copy-start | bytes 772
  13.4 12.8 %copy-start.22 = (bf16[128]{0:T(256)(128)(2,1)S(1)}, bf16[128]{0:T(256)(128)(2,1)}, u32[]{:S(2)}) copy-start(bf16[128]{0:T(256)(128)(2,1)} %param.20) | copy-start | bytes 772
  13.4 104.5 %all-to-all-start = ((bf16[256,8,768]{2,0,1:T(8,128)(2,1)}), bf16[256,8,768]{2,0,1:T(8,128)(2,1)}, u32[]{:S(2)}, u32[]{:S(2)}) async-start(bf16[256,8,768]{2,0,1:T(8,128)(2,1)} %pad_maximum_fusion), calls=%async_computation | async-start | bytes 6291456 | tf_op jit(solution)/shard_map/all_to_all | solution.py:1025
  20.4 185.0 %reduce-scatter.2.cloned.1.call-start = ((), (), s32[]{:S(2)}) async-start(), calls=%async_computation.3 | async-start | bytes 4718592 | tf_op jit(solution)/shard_map/reduce_scatter | solution.py:982
  111.8 3.3 copy-start.19
  127.5 5.9 %copy-start.6 = (pred[1024,1024]{0,1:T(8,128)(4,1)S(1)}, pred[1024,1024]{0,1:T(8,128)(4,1)}, u32[]{:S(2)}) copy-start(pred[1024,1024]{0,1:T(8,128)(4,1)} %fusion.4) | copy-start | bytes 3145732
  130.0 5.6 %copy-start.17 = (bf16[1024,64]{1,0:T(8,128)(2,1)}, bf16[1024,64]{1,0:T(8,128)(2,1)S(1)}, u32[]{:S(2)}) copy-start(bf16[1024,64]{1,0:T(8,128)(2,1)S(1)} %get-tuple-element.34) | copy-start | bytes 393220
  130.0 5.6 %copy-start.18 = (bf16[1024,64]{1,0:T(8,128)(2,1)}, bf16[1024,64]{1,0:T(8,128)(2,1)S(1)}, u32[]{:S(2)}) copy-start(bf16[1024,64]{1,0:T(8,128)(2,1)S(1)} %get-tuple-element.35) | copy-start | bytes 393220
  133.4 2.2 copy-start.9
  133.4 2.2 copy-start.10
  135.6 3.3 copy-start.3
  139.1 6.3 %copy-start.15 = (bf16[1024,128]{1,0:T(8,128)(2,1)}, bf16[1024,128]{1,0:T(8,128)(2,1)S(1)}, u32[]{:S(2)}) copy-start(bf16[1024,128]{1,0:T(8,128)(2,1)S(1)} %copy.57) | copy-start | bytes 786436
  145.4 0.8 copy-start.7
  150.7 1.0 copy-start.5
  150.7 2.0 copy-start.4
  156.9 5.7 %copy-start.16 = (bf16[1024,128]{1,0:T(8,128)(2,1)S(1)}, bf16[1024,128]{1,0:T(8,128)(2,1)}, u32[]{:S(2)}) copy-start(bf16[1024,128]{1,0:T(8,128)(2,1)} %copy-done.15) | copy-start | bytes 786436
  166.3 39.2 %copy-start.8 = (bf16[128,2048]{1,0:T(8,128)(2,1)S(1)}, bf16[128,2048]{1,0:T(8,128)(2,1)}, u32[]{:S(2)}) copy-start(bf16[128,2048]{1,0:T(8,128)(2,1)} %tokens.1) | copy-start | bytes 1572868
  477.6 4.2 copy-start.2
  496.0 16.6 %copy-start.12 = (f32[128,2048]{1,0:T(8,128)S(1)}, f32[128,2048]{1,0:T(8,128)}, u32[]{:S(2)}) copy-start(f32[128,2048]{1,0:T(8,128)} %get-tuple-element.74) | copy-start | bytes 3145732
  496.0 17.5 %copy-start.11 = (f32[128,2048]{1,0:T(8,128)S(1)}, f32[128,2048]{1,0:T(8,128)}, u32[]{:S(2)}) copy-start(f32[128,2048]{1,0:T(8,128)} %get-tuple-element.75) | copy-start | bytes 3145732
  496.0 18.5 %copy-start.1 = (bf16[256,1024]{1,0:T(8,128)(2,1)S(1)}, bf16[256,1024]{1,0:T(8,128)(2,1)}, u32[]{:S(2)}) copy-start(bf16[256,1024]{1,0:T(8,128)(2,1)} %param.22) | copy-start | bytes 1572868
Sparse Core Ops, SparseCore 0:
  10.3 97.6 all-gather.1
  150.9 54.5 reduce-scatter.1

commit v4 on v3

--- a/solution.py
+++ b/solution.py
@@ -380,22 +380,19 @@
     return pltpu.roll(value, HEAD_DIM // 2, 1)
 
 
-def late_kernel(
+def layer_kernel(
     scale,
     lengths,
-    resid,
+    tokens,
     cotangent,
-    tokens,
-    gain_one,
-    gain_two,
+    gain_shard,
     query_gain,
     key_gain,
-    proj,
-    cosine,
-    sine,
-    w_attn_hbm,
-    heads_hbm,
-    first_hbm,
+    frequency,
+    w_query_hbm,
+    w_key_hbm,
+    w_value_hbm,
+    w_out_hbm,
     w_gate_hbm,
     w_up_hbm,
     w_down_hbm,
@@ -405,6 +402,15 @@
     attn_grads,
     ffn_grads,
     core_landed,
+    first_hbm,
+    w_attn_hbm,
+    heads_hbm,
+    resid,
+    gain_rows_all,
+    gain_blocks,
+    proj,
+    cosine,
+    sine,
     second,
     cot_all,
     branch,
@@ -428,6 +434,8 @@
     assembled,
     gain_sums,
     gain_landed,
+    swap_sems,
+    sibling_sems,
     free_sem,
     core_free_sem,
     landing_free,
@@ -460,14 +468,212 @@
         return send_sems.at[pl.ds(at, count)], recv_sems.at[pl.ds(at, count)]
 
     own = place.rows(0, 0)
-    root = lax.rsqrt(jnp.mean(resid[...] * resid[...], axis=-1, keepdims=True) + epsilon)
-    second[own, :] = (resid[...] * root * gain_two[...]).astype(low)
+    gain_one = gain_rows_all.at[pl.ds(0, 1)]
+    gain_two = gain_rows_all.at[pl.ds(1, 1)]
     cot_all[own, :] = cotangent[...].astype(low)
+    branch[own, :] = tokens[...]
+    feat = w_query_hbm.shape[0]
+    gain_blocks[place.shard] = gain_shard[...]
     place.greet()
+
+    gain_share = Net(*sems(7))
+    peers = [(dy, dz) for dy in range(2) for dz in range(4) if dy or dz]
+    for by in peers:
+        gain_share.send(
+            str(by),
+            gain_blocks.at[place.shard],
+            gain_blocks.at[place.shard],
+            place.dev(*by),
+            gain_blocks.at[place.block(-by[0], -by[1])],
+        )
+    qkv_parts = (
+        (w_query_hbm, 0, 2 * HEAD_DIM),
+        (w_key_hbm, 2 * HEAD_DIM, HEAD_DIM),
+        (w_value_hbm, 3 * HEAD_DIM, HEAD_DIM),
+    )
+    out_parts = ((w_out_hbm, 4 * HEAD_DIM, 2 * HEAD_DIM),)
+    half_rows = feat // 2
+    qkv_span = pl.ds(0, 4 * HEAD_DIM)
+    out_span = pl.ds(4 * HEAD_DIM, 2 * HEAD_DIM)
+
+    def swap_rows(block):
+        at = block * feat + place.core * half_rows
+        return pl.ds(pl.multiple_of(at, half_rows), half_rows)
+
+    def swap_copy(src, dst, kind, i, dev):
+        return pltpu.make_async_remote_copy(
+            src_ref=src,
+            dst_ref=dst,
+            send_sem=swap_sems.at[0, kind, i],
+            recv_sem=swap_sems.at[1, kind, i],
+            device_id=dev,
+            device_id_type=MESH,
+        )
+
+    def swap_send(parts, kind):
+        for i, by in enumerate(peers):
+            to = place.block(*by)
+            for whole, begin, size in parts:
+                cols = pl.ds(pl.multiple_of(to * size, HEAD_DIM), size)
+                src = whole.at[pl.ds(pl.multiple_of(place.core * half_rows, half_rows), half_rows), cols]
+                dst = pair.at[swap_rows(place.shard), pl.ds(begin, size)]
+                swap_copy(src, dst, kind, i, place.dev(*by)).start()
+        for whole, begin, size in parts:
+            cols = pl.ds(pl.multiple_of(place.shard * size, HEAD_DIM), size)
+            rows = pl.ds(pl.multiple_of(place.shard * feat, feat), feat)
+            copy = pltpu.make_async_copy(
+                whole.at[:, cols], pair.at[rows, pl.ds(begin, size)], sibling_sems.at[2, kind]
+            )
+            copy.start()
+
+    def sibling_copy(ref, kind):
+        return pltpu.make_async_remote_copy(
+            src_ref=ref,
+            dst_ref=ref,
+            send_sem=sibling_sems.at[0, kind],
+            recv_sem=sibling_sems.at[1, kind],
+            device_id=place.rep_dev(0, 0, 1),
+            device_id_type=MESH,
+        )
+
+    def swap_relay(span, kind):
+        for i, by in enumerate(peers):
+            here = pair.at[swap_rows(place.block(-by[0], -by[1])), span]
+            swap_copy(here, here, kind, i, place.dev(*by)).wait_recv()
+            sibling_copy(here, kind).start()
+
+    def swap_done(span, kind):
+        rows = pl.ds(pl.multiple_of(place.shard * feat, feat), feat)
+        mine = pair.at[rows, span]
+        pltpu.make_async_copy(mine, mine, sibling_sems.at[2, kind]).wait()
+        others = pair.at[pl.ds(0, 7 * half_rows), span]
+        sibling_copy(others, kind).wait()
+        for i, by in enumerate(peers):
+            here = pair.at[swap_rows(place.block(-by[0], -by[1])), span]
+            swap_copy(here, here, kind, i, place.dev(*by)).wait_send()
+
+    swap_send(qkv_parts, 0)
+    gather_tokens = Gather(place, branch, *sems(Gather.COPIES))
+    gather_tokens.start()
+
+    start_one = lengths[0, 0]
+    start_two = lengths[0, 0] + lengths[0, 1]
+
+    def begin_of(token):
+        return jnp.where(
+            token >= start_two, start_two, jnp.where(token >= start_one, start_one, 0)
+        )
+
+    token = lax.broadcasted_iota(jnp.int32, (rows_all, 1), 0)
+    angles = (token - begin_of(token)).astype(f32) * frequency[...]
+    lane = lax.broadcasted_iota(jnp.int32, (1, HEAD_DIM), 1)
+    cosine[...] = jnp.cos(angles)
+    sine[...] = jnp.sin(angles) * jnp.where(lane < HEAD_DIM // 2, -1.0, 1.0)
+
+    gather_tokens.step_one()
+    gather_tokens.step_two()
+    gain_share.finish()
+    for j in range(8):
+        span = slice(j * feat, (j + 1) * feat)
+        gain_rows_all[0:2, span] = gain_blocks[j, 0:2, :].astype(f32)
+    swap_relay(qkv_span, 0)
+    swap_send(out_parts, 1)
+    gather_tokens.step_three()
+    gather_tokens.step_four()
+
+    def normalise(dy):
+        line = place.line(dy)
+
+        @pl.loop(0, LINE // BLOCK)
+        def _(i):
+            rows = pl.ds(pl.multiple_of(line + i * BLOCK, BLOCK), BLOCK)
+            x = branch[rows, :].astype(f32)
+            root = lax.rsqrt(jnp.mean(x * x, axis=-1, keepdims=True) + epsilon)
+            second[rows, :] = (x * root * gain_one[...]).astype(low)
+
+    gather_tokens.own_line()
+    normalise(0)
+    gather_tokens.other_line()
+    normalise(1)
+    gather_tokens.finish()
+    keep_first = pltpu.make_async_copy(second, first_hbm, local_sems.at[3])
+    keep_first.start()
+    swap_done(qkv_span, 0)
+    heads = d_up
+    gains_of_head = (query_gain, query_gain, key_gain)
+
+    @pl.loop(0, rows_all // 256)
+    def _(i):
+        rows = pl.ds(pl.multiple_of(i * 256, 256), 256)
+        proj[rows, :] = mm(second[rows, :], pair[:, 0 : 4 * HEAD_DIM])
+        for g in range(3):
+            lanes = pl.ds(g * HEAD_DIM, HEAD_DIM)
+            u = proj[rows, lanes]
+            root = lax.rsqrt(jnp.mean(u * u, axis=-1, keepdims=True) + epsilon)
+            u = u * root * gains_of_head[g][...]
+            heads[rows, lanes] = (u * cosine[rows, :] + swap_halves(u) * sine[rows, :]).astype(low)
+        lanes = pl.ds(3 * HEAD_DIM, HEAD_DIM)
+        heads[rows, lanes] = proj[rows, lanes].astype(low)
+
+    swap_relay(out_span, 1)
+    chunk = 256
+    for part in range(rows_all // chunk):
+        rows = pl.ds(part * chunk, chunk)
+        seen = (part + 1) * chunk
+        token = part * chunk + lax.broadcasted_iota(jnp.int32, (chunk, 1), 0)
+        source = lax.broadcasted_iota(jnp.int32, (1, seen), 1)
+        visible = (source >= begin_of(token)) & (source <= token)
+        for g in range(2):
+            lanes = pl.ds(g * HEAD_DIM, HEAD_DIM)
+            scores = mm_nt(heads[rows, lanes], heads[0:seen, 2 * HEAD_DIM : 3 * HEAD_DIM]) * scale
+            scores = jnp.where(visible, scores, masked_value)
+            top = jnp.max(scores, axis=-1, keepdims=True)
+            raised = jnp.exp(scores - top)
+            total = jnp.sum(raised, axis=-1, keepdims=True)
+            probs = (raised * (1.0 / total)).astype(low)
+            proj[rows, 3 * HEAD_DIM + g : 3 * HEAD_DIM + g + 1] = jnp.log(total) + top
+            heads[rows, pl.ds((4 + g) * HEAD_DIM, HEAD_DIM)] = mm(
+                probs, heads[0:seen, 3 * HEAD_DIM : 4 * HEAD_DIM]
+            ).astype(low)
+    keep_heads = pltpu.make_async_copy(heads, heads_hbm, local_sems.at[4])
+    keep_heads.start()
+    swap_done(out_span, 1)
+    keep_weights = pltpu.make_async_copy(pair, w_attn_hbm, local_sems.at[5])
+    keep_weights.start()
+    landing = (across, near, far, last)
+    scatter_attn = Scatter(place, part_back, *landing, *sems(Scatter.COPIES))
+
+    def attention_out(dy):
+        rows = pl.ds(place.line(dy), LINE)
+
+        @pl.loop(0, width // 256)
+        def _(i):
+            cols = pl.ds(pl.multiple_of(i * 256, 256), 256)
+            part_back[rows, cols] = mm_nt(
+                heads[rows, 4 * HEAD_DIM :], pair[cols, 4 * HEAD_DIM :]
+            ).astype(low)
+
+    attention_out(1)
+    keep_first.wait()
+    scatter_attn.send_other()
+    attention_out(0)
+    scatter_attn.send_own()
+    scatter_attn.step_one()
+    scatter_attn.step_two()
+    scatter_attn.step_three()
+    keep_heads.wait()
+    keep_weights.wait()
+    for half in (1, 0):
+        rows = pl.ds(half * HALF, HALF)
+        x = tokens[rows, :].astype(f32) + scatter_attn.total(half)
+        resid[rows, :] = x
+        root = lax.rsqrt(jnp.mean(x * x, axis=-1, keepdims=True) + epsilon)
+        at = place.rows(0, 0, half * HALF, HALF)
+        second[at, :] = (x * root * gain_two[...]).astype(low)
+    scatter_attn.finish()
     gather_second = Gather(place, second, *sems(Gather.COPIES))
     gather_cot = Gather(place, cot_all, *sems(Gather.COPIES))
     gather_branch = Gather(place, branch, *sems(Gather.COPIES))
-    landing = (across, near, far, last)
     scatter_out = Scatter(place, part_out, *landing, *sems(Scatter.COPIES))
     scatter_back = Scatter(place, part_back, *landing, *sems(Scatter.COPIES))
 
@@ -589,7 +795,6 @@
     sum_gate.x_first(load_landed(0))
     sum_up.x_first(load_landed(1))
     gather_cot.finish()
-    heads = d_up
     q_cols = 2 * HEAD_DIM
     query = heads.at[:, pl.ds(0, q_cols)]
     key = heads.at[:, pl.ds(q_cols, HEAD_DIM)]
@@ -663,21 +868,15 @@
         return rms_backward(projected, gain, turned)
 
     gain_rows = jnp.zeros((1, HEAD_DIM), f32)
-    start_one = lengths[0, 0]
-    start_two = lengths[0, 0] + lengths[0, 1]
     d_key[...] = jnp.zeros_like(d_key)
     d_value[...] = jnp.zeros_like(d_value)
-    chunk = 256
     scatter_out.step_one()
     for part in range(rows_all // chunk):
         rows = pl.ds(part * chunk, chunk)
         seen = (part + 1) * chunk
         token = part * chunk + lax.broadcasted_iota(jnp.int32, (chunk, 1), 0)
         source = lax.broadcasted_iota(jnp.int32, (1, seen), 1)
-        begin = jnp.where(
-            token >= start_two, start_two, jnp.where(token >= start_one, start_one, 0)
-        )
-        visible = (source >= begin) & (source <= token)
+        visible = (source >= begin_of(token)) & (source <= token)
         for g in range(2):
             lanes = pl.ds(g * HEAD_DIM, HEAD_DIM)
             scores = mm_nt(query[rows, lanes], key[0:seen, :]) * scale
@@ -870,18 +1069,19 @@
     gain_net.finish()
 
 
-def late_call(lengths, *args):
-    width = args[0].shape[1]
+def layer_call(lengths, *args):
+    tokens, cotangent = args[:2]
+    width = tokens.shape[1]
     hid = args[-1].shape[0]
     rows = 8 * BLOCK
     vmem = pl.BlockSpec(memory_space=pltpu.VMEM)
     smem = pl.BlockSpec(memory_space=pltpu.SMEM)
-    anywhere = pl.BlockSpec(memory_space=pl.ANY)
-    copies = 3 * Gather.COPIES + 3 * Scatter.COPIES + 4 * RepSum.COPIES + 9 + 7
+    hbm = pl.BlockSpec(memory_space=pltpu.HBM)
+    copies = 4 * Gather.COPIES + 4 * Scatter.COPIES + 4 * RepSum.COPIES + 9 + 7 + 7
     gain_shape = (2 * width // HEAD_DIM + 8, HEAD_DIM)
     return pl.pallas_call(
-        functools.partial(late_kernel, 1.0 / math.sqrt(HEAD_DIM)),
-        name="late",
+        functools.partial(layer_kernel, 1.0 / math.sqrt(HEAD_DIM)),
+        name="layer",
         out_shape=[
             jax.ShapeDtypeStruct((BLOCK, width), f32),
             jax.ShapeDtypeStruct((BLOCK, width), f32),
@@ -889,10 +1089,19 @@
             jax.ShapeDtypeStruct((256, 3 * width), low),
             jax.ShapeDtypeStruct((3, hid, width), low),
             jax.ShapeDtypeStruct((3, hid // 2, width), low),
+            jax.ShapeDtypeStruct((rows, width), low),
+            jax.ShapeDtypeStruct((2 * rows, 6 * HEAD_DIM), low),
+            jax.ShapeDtypeStruct((rows, 6 * HEAD_DIM), low),
         ],
-        in_specs=[smem] + [vmem] * (len(args) - 6) + [anywhere] * 6,
-        out_specs=[vmem] * 3 + [pl.BlockSpec(memory_space=pltpu.HBM)] * 3,
+        in_specs=[smem] + [vmem] * 6 + [hbm] * 7,
+        out_specs=[vmem] * 3 + [hbm] * 6,
         scratch_shapes=[
+            pltpu.VMEM((BLOCK, width), f32),
+            pltpu.VMEM((2, width), f32),
+            pltpu.VMEM((8, 16, 256), low),
+            pltpu.VMEM((rows, 4 * HEAD_DIM), f32),
+            pltpu.VMEM((rows, HEAD_DIM), f32),
+            pltpu.VMEM((rows, HEAD_DIM), f32),
             pltpu.VMEM((rows, width), low),
             pltpu.VMEM((rows, width), low),
             pltpu.VMEM((rows, width), low),
@@ -915,11 +1124,13 @@
             pltpu.VMEM((16, 3 * width), low),
             pltpu.VMEM((6,) + gain_shape, f32),
             pltpu.VMEM((15,) + gain_shape, f32),
+            pltpu.SemaphoreType.DMA((2, 2, 7)),
+            pltpu.SemaphoreType.DMA((3, 2)),
             pltpu.SemaphoreType.REGULAR,
             pltpu.SemaphoreType.REGULAR,
             pltpu.SemaphoreType.REGULAR,
             pltpu.SemaphoreType.REGULAR,
-            pltpu.SemaphoreType.DMA((4,)),
+            pltpu.SemaphoreType.DMA((6,)),
             pltpu.SemaphoreType.DMA((copies,)),
             pltpu.SemaphoreType.DMA((copies,)),
         ],
@@ -930,58 +1141,6 @@
             flops=36_000_000_000, bytes_accessed=60_000_000, transcendentals=4_000_000
         ),
     )(lengths, *args)
-
-
-def rms_scale(values, gain):
-    return values * lax.rsqrt(jnp.mean(values * values, axis=-1, keepdims=True) + epsilon) * gain
-
-
-def rotate(values, positions):
-    half_dim = values.shape[-1] // 2
-    frequency = theta_base ** (-jnp.arange(half_dim, dtype=jnp.float32) * (2.0 / values.shape[-1]))
-    angles = positions.astype(jnp.float32)[:, None] * frequency[None, :]
-    cosine = jnp.cos(angles)[:, None, :]
-    sine = jnp.sin(angles)[:, None, :]
-    first_half = values[..., :half_dim]
-    second_half = values[..., half_dim:]
-    return jnp.concatenate(
-        [first_half * cosine - second_half * sine, second_half * cosine + first_half * sine],
-        axis=-1,
-    )
-
-
-def segment_info(lengths_row, indices):
-    start_one = lengths_row[0]
-    start_two = lengths_row[0] + lengths_row[1]
-    segment = (indices >= start_one).astype(jnp.int32) + (indices >= start_two).astype(jnp.int32)
-    begin = jnp.where(segment == 0, 0, jnp.where(segment == 1, start_one, start_two))
-    return (segment, indices - begin)
-
-
-def dot(left, right):
-    return jnp.dot(left, right, preferred_element_type=jnp.float32)
-
-
-def contract_rows(left, right):
-    return lax.dot_general(
-        left, right, (((1,), (1,)), ((), ())), preferred_element_type=jnp.float32
-    )
-
-
-def contract_first(left, right):
-    return lax.dot_general(
-        left, right, (((0,), (0,)), ((), ())), preferred_element_type=jnp.float32
-    )
-
-
-def gather(x):
-    return lax.all_gather(x, "shard", axis=0, tiled=True)
-
-
-def scatter_sum(x):
-    return lax.psum_scatter(
-        x.astype(jnp.bfloat16), "shard", scatter_dimension=0, tiled=True
-    ).astype(jnp.float32)
 
 
 def per_device(
@@ -1000,98 +1159,26 @@
     w_up,
     w_down,
 ):
-    tok_rows, width = tokens.shape
+    width = tokens.shape[1]
     shards = lax.axis_size("shard")
-    rows = tok_rows * shards
-    group = HEADS // KV_HEADS
     feat = width // shards
-    scale = 1.0 / math.sqrt(HEAD_DIM)
     my_shard = lax.axis_index("shard")
-    index = jnp.arange(rows, dtype=jnp.int32)
-    segment, position = segment_info(lengths[0], index)
-    visible = (segment[:, None] == segment[None, :]) & (index[None, :] <= index[:, None])
-
-    q_cols = w_query.shape[1] // shards
-    k_cols = w_key.shape[1] // shards
-    packed = jnp.concatenate(
-        [
-            w_query.reshape(feat, shards, q_cols),
-            w_key.reshape(feat, shards, k_cols),
-            w_value.reshape(feat, shards, k_cols),
-            w_out.reshape(feat, shards, q_cols),
-        ],
-        axis=2,
-    )
-    mine = lax.all_to_all(packed, "shard", split_axis=1, concat_axis=0, tiled=True).reshape(
-        width, -1
-    )
-    qkv_cols = q_cols + 2 * k_cols
-    w_qkv = mine[:, :qkv_cols]
-    w_o = mine[:, qkv_cols:]
-
-    gains_rows = jnp.concatenate(
-        [attn_gain, mlp_gain, jnp.zeros((width - 2 * feat,), low)]
-    ).reshape(1, width)
-    gathered = gather(
-        jnp.concatenate([tokens, jnp.broadcast_to(gains_rows, (16, width))], axis=0)
-    ).reshape(shards, tok_rows + 16, width)
-    tokens_all = gathered[:, :tok_rows].reshape(rows, width)
-    gain_one = gathered[:, tok_rows, :feat].reshape(width).astype(jnp.float32)
-    gain_two = gathered[:, tok_rows, feat : 2 * feat].reshape(width).astype(jnp.float32)
-
-    inputs = tokens.astype(jnp.float32)
-    first = rms_scale(tokens_all.astype(jnp.float32), gain_one).astype(low)
-    proj = dot(first, w_qkv)
-
-    def prepare(projected, gain, count):
-        return rotate(rms_scale(projected.reshape(rows, count, HEAD_DIM), gain), position)
-
-    q_rot = prepare(proj[:, :q_cols], query_gain.astype(f32), group)
-    k_rot = prepare(proj[:, q_cols : q_cols + k_cols], key_gain.astype(f32), 1)
-    query = q_rot.astype(low)
-    key = k_rot.astype(low)[:, 0]
-    value = proj[:, q_cols + k_cols :].astype(low)
-    scores = jnp.einsum("tgd,sd->gts", query, key, preferred_element_type=jnp.float32) * scale
-    masked = jnp.where(visible[None], scores, masked_value)
-    top = jnp.max(masked, axis=-1, keepdims=True)
-    total = jnp.log(jnp.sum(jnp.exp(masked - top), axis=-1, keepdims=True)) + top
-    weights = jnp.exp(masked - total)
-    probs = weights.astype(low)
-    attended = (
-        jnp.einsum("gts,sd->tgd", probs, value, preferred_element_type=jnp.float32)
-        .reshape(rows, q_cols)
-        .astype(low)
-    )
-    resid = inputs + scatter_sum(contract_rows(attended, w_o))
     half = HEAD_DIM // 2
     frequency = theta_base ** (-jnp.arange(half, dtype=f32) * (2.0 / HEAD_DIM))
-    angles = position.astype(f32)[:, None] * frequency[None, :]
-    cosine = jnp.concatenate([jnp.cos(angles)] * 2, axis=1)
-    sine = jnp.concatenate([-jnp.sin(angles), jnp.sin(angles)], axis=1)
-    kept = jnp.concatenate(
-        [
-            proj[:, : q_cols + k_cols],
-            total[0],
-            total[1],
-            jnp.zeros((rows, HEAD_DIM - 2), f32),
-        ],
-        axis=1,
-    )
-    result, grad_tokens, gains, attn_grads, ffn_grads, _ = late_call(
+    frequency = jnp.concatenate([frequency, frequency])[None]
+    gain_shard = jnp.concatenate([attn_gain[None], mlp_gain[None], jnp.zeros((14, feat), low)])
+    result, grad_tokens, gains, attn_grads, ffn_grads, *_ = layer_call(
         lengths,
-        resid,
+        tokens,
         cotangent,
-        tokens,
-        gain_one[None],
-        gain_two[None],
+        gain_shard,
         query_gain.astype(f32)[None],
         key_gain.astype(f32)[None],
-        kept,
-        cosine,
-        sine,
-        mine,
-        jnp.concatenate([query.reshape(rows, q_cols), key, value, attended], axis=1),
-        first,
+        frequency,
+        w_query,
+        w_key,
+        w_value,
+        w_out,
         w_gate,
         w_up,
         w_down,

time: 531 us -> 404 us (0.76); the launches traced: 522 us -> 401 us
  waiting for transfers between devices: 117 us -> 0 us
  Pallas kernels: 270 us -> 360 us
  other arithmetic: 50.4 us -> 15.1 us
  local copies, waits for them, and re-layouts: 42.7 us -> 24 us
  matrix products: 18.2 us -> 0 us
  between operations: 16.2 us -> 1.11 us
  starting transfers between devices: 7.08 us -> 0 us
    pallas_call x1, Pallas kernels: 270 us -> 360 us  [layer_call(): pl.pallas_call(functools.partial(layer_kernel, 1.0 / math.sqrt(HEAD_DIM))...]
    all_gather x1 -> x0, waiting for transfers between devices: 79.7 us -> none  [gather(): return lax.all_gather(x, 'shard', axis=0, tiled=True)]
    reduce_scatter x1 -> x0, waiting for transfers between devices: 37.5 us -> none  [scatter_sum(): lax.psum_scatter(x.astype(jnp.bfloat16), 'shard', scatter_dimension=0, ti...]
    dot_general x4 -> x0, matrix products: 18.2 us -> none  [the longest x1 6.26 us: per_device(): jnp.einsum('gts,sd->tgd', probs, value, preferred_element_type=jnp.float32)]
    concatenate x7 -> x1, other arithmetic: 11.7 us -> 0.67 us  [per_device(): jnp.concatenate([attn_gain[None], mlp_gain[None], jnp.zeros((14, feat), l...]
    convert_element_type x5 -> x0, other arithmetic: 8.77 us -> none  [the longest x2 6 us: per_device(): first = rms_scale(tokens_all.astype(jnp.float32), gain_one).astype(low)]
    all_to_all x1 -> x0, starting transfers between devices: 7.01 us -> none  [per_device(): lax.all_to_all(packed, 'shard', split_axis=1, concat_axis=0, tiled=True)]
    reduce_sum x4 -> x0, other arithmetic: 5.55 us -> none  [the longest x3 3.39 us: rms_scale(): jnp.mean(values * values, axis=-1, keepdims=True) + epsilon]
  transfers between devices with their start and end apart: 3 -> 0, of which waited for: 2 -> 0; matrix products, arithmetic and copies ran while one was open for 7% -> 0% of each run, Pallas kernels for 0% -> 0%
where the time goes in v4:
time: 404 us; the launch traced here: 401 us
  Pallas kernels  360 us (89%)
  local copies, waits for them, and re-layouts  24 us (6%)
  other arithmetic  15.1 us (4%)
    pallas_call x1, Pallas kernels, layer_call(): pl.pallas_call(functools.partial(layer_kernel, 1.0 / math.sqrt(HEAD_DIM))...  360 us
    squeeze x1, local copies, waits for them, and re-layouts, per_device(): ffn_grads[2]  13.9 us
    convert_element_type x1, other arithmetic, per_device(): ffn_grads = ffn_grads.astype(f32)  12.6 us

profile of v4, /device:TPU:1, one launch (start us, length us, event | category | flops | bytes accessed | tf_op | source)
XLA Modules:
  0.0 400.5 jit_solution(17520794143735985790)
XLA Ops:
  0.7 1.2 bitcast_convert_fusion
  1.8 0.7 broadcast_in_dim.22
  2.5 0.7 broadcast_in_dim.23
  3.2 0.1 pad.4.clone
  3.2 0.7 maximum_maximum_fusion.gain_shard
  3.9 0.6 maximum_bitcast_fusion.frequency
  4.5 360.3 %layer.1 = (f32[128,2048]{1,0:T(8,128)}, f32[128,2048]{1,0:T(8,128)}, f32[40,128]{1,0:T(8,128)}, bf16[256,6144]{1,0:T(8,128)(2,1)}, bf16[3,768,2048]{2,1,0:T(8,1...) custom-call(s32[1,3]{1,0:T(1,128)} %lengths.1, ...), custom_call_target="tpu_custom_call" | custom-call | flops 35999997952 | bytes 60000000 | tf_op jit(solution)/shard_map/layer/pallas_call | solution.py:1082
  364.8 1.3 fusion.3
  366.2 1.3 fusion.2
  367.5 12.6 %convert_element_type.9 = f32[3,768,2048]{2,1,0:T(8,128)} convert(bf16[3,768,2048]{2,1,0:T(8,128)(2,1)} %get-tuple-element.21) | non-fusion elementwise | flops 4718592 | bytes 28311552 | tf_op jit(solution)/shard_map/convert_element_type | solution.py:1186
  380.1 0.0 copy-start
  380.1 13.9 %slice_bitcast_fusion = (f32[768,2048]{1,0:T(8,128)}, f32[768,2048]{1,0:T(8,128)}, f32[768,2048]{1,0:T(8,128)}) fusion(f32[3,768,2048]{2,1,0:T(8,128)} %convert_element_type.9), kind=kLoop, calls=%fused_computation | loop fusion | bytes 37748736 | tf_op jit(solution)/shard_map/squeeze | solution.py:1209
  394.0 0.0 copy-done
  394.0 2.5 fusion
  396.6 0.0 copy-start.2
  396.6 0.0 copy-start.1
  396.6 1.6 fusion.1
  398.1 0.0 copy-done.2
  398.1 1.0 copy.29
  399.1 0.0 copy-done.1
  399.1 1.0 copy.30
  (2 shorter events, 0.0 us)
Async XLA Ops:
  380.1 13.9 %copy-start = (bf16[256,6144]{1,0:T(8,128)(2,1)S(1)}, bf16[256,6144]{1,0:T(8,128)(2,1)}, u32[]{:S(2)}) copy-start(bf16[256,6144]{1,0:T(8,128)(2,1)} %get-tuple-element.20) | copy-start | bytes 9437188
  396.6 1.6 copy-start.2
  396.6 2.5 copy-start.1

commit v5 on v4

--- a/solution.py
+++ b/solution.py
@@ -616,6 +616,8 @@
         heads[rows, lanes] = proj[rows, lanes].astype(low)
 
     swap_relay(out_span, 1)
+    gather_cot = Gather(place, cot_all, *sems(Gather.COPIES))
+    gather_cot.start()
     chunk = 256
     for part in range(rows_all // chunk):
         rows = pl.ds(part * chunk, chunk)
@@ -635,6 +637,8 @@
             heads[rows, pl.ds((4 + g) * HEAD_DIM, HEAD_DIM)] = mm(
                 probs, heads[0:seen, 3 * HEAD_DIM : 4 * HEAD_DIM]
             ).astype(low)
+        if part == 1:
+            gather_cot.step_one()
     keep_heads = pltpu.make_async_copy(heads, heads_hbm, local_sems.at[4])
     keep_heads.start()
     swap_done(out_span, 1)
@@ -672,14 +676,11 @@
         second[at, :] = (x * root * gain_two[...]).astype(low)
     scatter_attn.finish()
     gather_second = Gather(place, second, *sems(Gather.COPIES))
-    gather_cot = Gather(place, cot_all, *sems(Gather.COPIES))
     gather_branch = Gather(place, branch, *sems(Gather.COPIES))
     scatter_out = Scatter(place, part_out, *landing, *sems(Scatter.COPIES))
     scatter_back = Scatter(place, part_back, *landing, *sems(Scatter.COPIES))
 
-    def feed_forward(dy):
-        rows = pl.ds(place.line(dy), LINE)
-
+    def feed_forward(rows):
         @pl.loop(0, hid // 256)
         def _(i):
             cols = pl.ds(pl.multiple_of(i * 256, 256), 256)
@@ -757,19 +758,23 @@
 
         return load
 
-    for step in gather_second.steps():
-        step()
-    gather_second.own_line()
-    gather_cot.start()
+    gather_second.start()
     for load in loads:
         load.wait()
-    feed_forward(0)
-    gather_cot.step_one()
+    feed_forward(own)
+    gather_second.step_one()
+    gather_second.step_two()
+    gather_second.step_three()
+    gather_second.step_four()
     gather_cot.step_two()
+    feed_forward(place.rows(0, 1))
+    feed_forward(place.rows(0, 3))
+    gather_second.own_line()
+    gather_cot.step_three()
+    feed_forward(place.rows(0, 2))
     gather_second.other_line()
-    feed_forward(1)
-    gather_cot.step_three()
     gather_cot.step_four()
+    feed_forward(pl.ds(place.line(1), LINE))
     project_out(1)
     project_out(0)
     gather_cot.own_line()
@@ -842,12 +847,9 @@
     gather_branch.step_one()
     sum_gate.x_second()
     gather_branch.step_two()
-    scatter_out.send_other()
-    scatter_out.send_own()
     sum_up.x_second()
     gather_branch.step_three()
     gather_branch.step_four()
-    sum_down.x_second()
     gather_branch.own_line()
     for load in loads:
         load.wait()
@@ -861,7 +863,13 @@
 
     into_attention(0)
     gather_branch.other_line()
+    scatter_out.send_other()
+    scatter_out.send_own()
     into_attention(1)
+    sum_down.x_second()
+    scatter_back.finish()
+    load = pltpu.make_async_copy(first_hbm, part_back, local_sems.at[0])
+    load.start()
 
     def unrotate(rows, upstream, projected, gain):
         turned = upstream * cosine[rows, :] - swap_halves(upstream) * sine[rows, :]
@@ -870,7 +878,6 @@
     gain_rows = jnp.zeros((1, HEAD_DIM), f32)
     d_key[...] = jnp.zeros_like(d_key)
     d_value[...] = jnp.zeros_like(d_value)
-    scatter_out.step_one()
     for part in range(rows_all // chunk):
         rows = pl.ds(part * chunk, chunk)
         seen = (part + 1) * chunk
@@ -894,11 +901,11 @@
         if part == 0:
             sum_gate.y_send()
         if part == 1:
-            scatter_out.step_two()
+            scatter_out.step_one()
             sum_up.y_send()
             sum_gate.y_gather(sum_gate.piece(), local_sems.at[3])
         if part == 2:
-            scatter_out.step_three()
+            scatter_out.step_two()
             sum_down.y_send()
             sum_up.y_gather(sum_up.piece(), local_sems.at[3])
             sum_gate.x_gather()
@@ -910,44 +917,7 @@
     d_qkv[:, lanes] = back.astype(low)
     keep_gain(2 * gain_slots + 1, jnp.sum(gain_part, axis=0, keepdims=True))
 
-    scatter_back.finish()
-    scatter_first = Scatter(place, part_back, *landing, *sems(Scatter.COPIES))
-    for half in (0, 1):
-        rows = pl.ds(half * HALF, HALF)
-        result[rows, :] = resid[rows, :] + scatter_out.total(half)
-    scatter_out.finish()
-    for by in ((1, 0), (0, 1), (0, 3)):
-        pl.semaphore_signal(landing_free, inc=1, device_id=place.dev(*by), device_id_type=MESH)
-    load = pltpu.make_async_copy(first_hbm, part_out, local_sems.at[0])
-    load.start()
-    sum_down.y_gather(sum_down.piece(), local_sems.at[3])
-    sum_up.x_gather()
-
-    def into_first(dy):
-        rows = pl.ds(place.line(dy), LINE)
-
-        for side in range(2):
-
-            @pl.loop(0, rows_all // 256)
-            def _(i):
-                feats = pl.ds(pl.multiple_of(i * 256, 256), 256)
-                cols = pl.ds(pl.multiple_of(side * rows_all + i * 256, 256), 256)
-                part_back[rows, cols] = mm_nt(
-                    d_qkv[rows, :], w_attn[feats, pl.ds(side * attn_cols, 4 * HEAD_DIM)]
-                ).astype(low)
-
-    into_first(1)
-    pl.semaphore_wait(landing_free, 3)
-    scatter_first.send_other()
-    into_first(0)
-    scatter_first.send_own()
-    for by in ((0, 1, 0), (0, 3, 0), (1, 0, 0)):
-        pl.semaphore_signal(
-            heads_free, inc=1, device_id=place.rep_dev(*by), device_id_type=MESH
-        )
     head_landed = cot_all.at[:, pl.ds(0, 6 * HEAD_DIM)]
-    load.wait()
-
     sum_attn = RepSum(
         place,
         sems(RepSum.COPIES),
@@ -962,10 +932,12 @@
         16,
     )
 
+    load.wait()
+
     @pl.loop(0, width // 256)
     def _(i):
         cols = pl.ds(pl.multiple_of(i * 256, 256), 256)
-        from_first = mm_tn(part_out[:, cols], d_qkv[...]).astype(low)
+        from_first = mm_tn(part_back[:, cols], d_qkv[...]).astype(low)
         from_branch = mm_tn(branch[:, cols], attended[...]).astype(low)
         for piece in range(16):
             rows = pl.ds(pl.multiple_of(piece * BLOCK + i * 16, 16), 16)
@@ -977,16 +949,49 @@
     )
     pl.semaphore_wait(core_free_sem, 1)
     sum_attn.core_send()
+    scatter_out.step_three()
+    for half in (0, 1):
+        rows = pl.ds(half * HALF, HALF)
+        result[rows, :] = resid[rows, :] + scatter_out.total(half)
+    scatter_out.finish()
+    for by in ((1, 0), (0, 1), (0, 3)):
+        pl.semaphore_signal(landing_free, inc=1, device_id=place.dev(*by), device_id_type=MESH)
+    scatter_first = Scatter(place, part_back, *landing, *sems(Scatter.COPIES))
+
+    def into_first(dy):
+        rows = pl.ds(place.line(dy), LINE)
+
+        for side in range(2):
+
+            @pl.loop(0, rows_all // 256)
+            def _(i):
+                feats = pl.ds(pl.multiple_of(i * 256, 256), 256)
+                cols = pl.ds(pl.multiple_of(side * rows_all + i * 256, 256), 256)
+                part_back[rows, cols] = mm_nt(
+                    d_qkv[rows, :], w_attn[feats, pl.ds(side * attn_cols, 4 * HEAD_DIM)]
+                ).astype(low)
+
+    into_first(1)
+    pl.semaphore_wait(landing_free, 3)
+    scatter_first.send_other()
+    into_first(0)
+    scatter_first.send_own()
+    for by in ((0, 1, 0), (0, 3, 0), (1, 0, 0)):
+        pl.semaphore_signal(
+            heads_free, inc=1, device_id=place.rep_dev(*by), device_id_type=MESH
+        )
+    sum_down.y_gather(sum_down.piece(), local_sems.at[3])
+    sum_up.x_gather()
+    pl.semaphore_wait(heads_free, 3)
+    sum_attn.x_first()
     scatter_first.step_one()
     sum_gate.x_forward()
-    pl.semaphore_wait(heads_free, 3)
-    sum_attn.x_first()
     scatter_first.step_two()
+    sum_attn.x_second()
     sum_down.x_gather()
     sum_up.x_forward()
     scatter_first.step_three()
     sum_gate.x_last()
-    sum_attn.x_second()
     gain_rows = None
     for half in (1, 0):
         rows = pl.ds(half * HALF, HALF)
@@ -1143,6 +1148,50 @@
     )(lengths, *args)
 
 
+def widen_kernel(ffn, attn, gate, up, down, query, key, value, out):
+    step = pl.program_id(0)
+    per = pl.num_programs(0) // 3
+    wide = ffn[0].astype(f32)
+    for which, ref in enumerate((gate, up, down)):
+
+        @pl.when(step // per == which)
+        def _(ref=ref):
+            ref[...] = wide
+
+    at = 0
+    for ref in (query, key, value, out):
+        ref[...] = attn[:, at : at + ref.shape[1]].astype(f32)
+        at += ref.shape[1]
+
+
+def widen(ffn, attn):
+    _, hid, width = ffn.shape
+    rows = attn.shape[0]
+    per, tall, some = 3, hid // 3, rows // 8
+
+    def block_of(which):
+        return lambda i: (jnp.clip(i - which * per, 0, per - 1), 0)
+
+    def attn_block(i):
+        return (jnp.minimum(i, 7), 0)
+
+    sizes = (width, width // 2, width // 2, width)
+    return pl.pallas_call(
+        widen_kernel,
+        name="widen",
+        grid=(3 * per,),
+        out_shape=[jax.ShapeDtypeStruct((hid, width), f32)] * 3
+        + [jax.ShapeDtypeStruct((rows, size), f32) for size in sizes],
+        in_specs=[
+            pl.BlockSpec((1, tall, width), lambda i: (i // per, i % per, 0)),
+            pl.BlockSpec((some, 3 * width), attn_block),
+        ],
+        out_specs=[pl.BlockSpec((tall, width), block_of(which)) for which in range(3)]
+        + [pl.BlockSpec((some, size), attn_block) for size in sizes],
+        compiler_params=pltpu.CompilerParams(vmem_limit_bytes=40 << 20),
+    )(ffn, attn)
+
+
 def per_device(
     tokens,
     cotangent,
@@ -1183,12 +1232,9 @@
         w_up,
         w_down,
     )
-    ffn_grads = ffn_grads.astype(f32)
-    attn_grads = attn_grads.astype(f32)
-    grad_query = attn_grads[:, :width]
-    grad_key = attn_grads[:, width : width + width // 2]
-    grad_value = attn_grads[:, width + width // 2 : 2 * width]
-    grad_out = attn_grads[:, 2 * width :]
+    grad_gate, grad_up, grad_down, grad_query, grad_key, grad_value, grad_out = widen(
+        ffn_grads, attn_grads
+    )
     gains = gains.reshape(-1)
     head_piece = HEAD_DIM // shards
     gains_first = lax.dynamic_slice_in_dim(gains, my_shard * feat, feat, 0)
@@ -1204,9 +1250,9 @@
         grad_key,
         grad_value,
         grad_out,
-        ffn_grads[0],
-        ffn_grads[1],
-        ffn_grads[2],
+        grad_gate,
+        grad_up,
+        grad_down,
         gains_first,
         gains_second,
         gains_query,

time: 404 us -> 378 us (0.936)
  other arithmetic: 15.1 us -> 2.46 us
  local copies, waits for them, and re-layouts: 24 us -> 11.6 us
    squeeze x1 -> x0, local copies, waits for them, and re-layouts: 13.9 us -> none  [per_device(): ffn_grads[2]]
    convert_element_type x1 -> x0, other arithmetic: 12.6 us -> none  [per_device(): ffn_grads = ffn_grads.astype(f32)]
    pallas_call x0 -> x1, Pallas kernels: none -> 10.6 us  [widen(): pl.pallas_call(widen_kernel, name='widen', grid=(3 * per,), out_shape=[ja...]
    pallas_call x1, Pallas kernels: 360 us -> 353 us  [layer_call(): pl.pallas_call(functools.partial(layer_kernel, 1.0 / math.sqrt(HEAD_DIM))...]
    unnamed x8 -> x10, local copies, waits for them, and re-layouts: 1.95 us -> 7.52 us
    slice x2 -> x0, local copies, waits for them, and re-layouts: 4.1 us -> none  [the longest x1 2.54 us: per_device(): grad_out = attn_grads[:, 2 * width:]]
where the time goes in v5:
time: 378 us
  Pallas kernels  363 us (96%)
  local copies, waits for them, and re-layouts  11.6 us (3%)
    pallas_call x1, Pallas kernels, layer_call(): pl.pallas_call(functools.partial(layer_kernel, 1.0 / math.sqrt(HEAD_DIM))...  353 us
    pallas_call x1, Pallas kernels, widen(): pl.pallas_call(widen_kernel, name='widen', grid=(3 * per,), out_shape=[ja...  10.6 us

profile of v5, /device:TPU:1, one launch (start us, length us, event | category | flops | bytes accessed | tf_op | source)
XLA Modules:
  0.0 377.9 jit_solution(18209340721779503699)
XLA Ops:
  0.7 0.1 pad.4.clone
  0.8 0.6 maximum_bitcast_fusion.frequency
  1.3 0.7 broadcast_in_dim.22
  2.0 0.7 broadcast_in_dim.23
  2.7 1.2 bitcast_convert_fusion
  3.9 0.7 maximum_maximum_fusion.gain_shard
  4.5 352.5 %layer.1 = (f32[128,2048]{1,0:T(8,128)}, f32[128,2048]{1,0:T(8,128)}, f32[40,128]{1,0:T(8,128)}, bf16[256,6144]{1,0:T(8,128)(2,1)}, bf16[3,768,2048]{2,1,0:T(8,1...) custom-call(s32[1,3]{1,0:T(1,128)} %lengths.1, ...), custom_call_target="tpu_custom_call" | custom-call | flops 35999997952 | bytes 60000000 | tf_op jit(solution)/shard_map/layer/pallas_call | solution.py:1087
  357.1 1.4 fusion
  358.4 1.3 fusion.1
  359.8 0.0 copy-start
  359.8 3.7 copy-done
  363.4 0.0 copy-start.1
  363.4 1.9 copy-done.1
  365.3 0.0 copy-start.3
  365.3 0.0 copy-start.2
  365.3 10.6 %widen.1 = (f32[768,2048]{1,0:T(8,128)}, f32[768,2048]{1,0:T(8,128)}, f32[768,2048]{1,0:T(8,128)}, f32[256,2048]{1,0:T(8,128)}, f32[256,1024]{1,0:T(8,128)}, /*index=5*/f32[256,1024]{1,0:T(8,128)}, f32[256,2048]{1,0:T(8,128)}) custom-call(bf16[3,768,2048]{2,1,0:T(8,128)(2,1)S(1)} %copy-done, bf16[256,6144]{1,0:T(8,128)(2,1)S(1)} %copy-done.1), custom_call_target="tpu_custom_call" | custom-call | tf_op jit(solution)/shard_map/widen/pallas_call | solution.py:1179
  375.9 0.0 copy-done.3
  375.9 1.0 copy.29
  376.9 0.0 copy-done.2
  376.9 1.0 copy.30
  (2 shorter events, 0.0 us)
Async XLA Ops:
  359.8 3.7 copy-start
  363.4 1.9 copy-start.1
  365.3 10.6 %copy-start.3 = (f32[128,2048]{1,0:T(8,128)S(1)}, f32[128,2048]{1,0:T(8,128)}, u32[]{:S(2)}) copy-start(f32[128,2048]{1,0:T(8,128)} %get-tuple-element.56) | copy-start | bytes 3145732
  365.3 11.6 %copy-start.2 = (f32[128,2048]{1,0:T(8,128)S(1)}, f32[128,2048]{1,0:T(8,128)}, u32[]{:S(2)}) copy-start(f32[128,2048]{1,0:T(8,128)} %get-tuple-element.57) | copy-start | bytes 3145732

commit v6 on v5

--- a/solution.py
+++ b/solution.py
@@ -3,6 +3,7 @@
 
 import jax
 import jax.numpy as jnp
+import numpy as np
 from jax import lax
 from jax.experimental import pallas as pl
 from jax.experimental.pallas import tpu as pltpu
@@ -177,6 +178,19 @@
         self.net.finish()
 
 
+class Slots:
+    def __init__(self, ref, base, size):
+        self.ref, self.base, self.size = ref, base, size
+
+    @property
+    def at(self):
+        return self
+
+    def __getitem__(self, i):
+        i = i if isinstance(i, int) else 2 * i[0] + i[1]
+        return self.ref.at[pl.ds(self.base + i * self.size, self.size)]
+
+
 class Scatter:
     COPIES = 17
 
@@ -385,7 +399,8 @@
     lengths,
     tokens,
     cotangent,
-    gain_shard,
+    attn_gain,
+    mlp_gain,
     query_gain,
     key_gain,
     frequency,
@@ -402,6 +417,7 @@
     attn_grads,
     ffn_grads,
     core_landed,
+    head_core_landed,
     first_hbm,
     w_attn_hbm,
     heads_hbm,
@@ -437,7 +453,6 @@
     swap_sems,
     sibling_sems,
     free_sem,
-    core_free_sem,
     landing_free,
     heads_free,
     local_sems,
@@ -473,7 +488,10 @@
     cot_all[own, :] = cotangent[...].astype(low)
     branch[own, :] = tokens[...]
     feat = w_query_hbm.shape[0]
-    gain_blocks[place.shard] = gain_shard[...]
+    at = lax.broadcasted_iota(jnp.int32, (16, attn_gain.shape[1]), 0)
+    gain_blocks[place.shard] = jnp.where(
+        at == 0, attn_gain[...].astype(f32), mlp_gain[...].astype(f32)
+    ).astype(low)
     place.greet()
 
     gain_share = Net(*sems(7))
@@ -492,13 +510,14 @@
         (w_value_hbm, 3 * HEAD_DIM, HEAD_DIM),
     )
     out_parts = ((w_out_hbm, 4 * HEAD_DIM, 2 * HEAD_DIM),)
-    half_rows = feat // 2
+    few = feat // 8
     qkv_span = pl.ds(0, 4 * HEAD_DIM)
     out_span = pl.ds(4 * HEAD_DIM, 2 * HEAD_DIM)
 
-    def swap_rows(block):
-        at = block * feat + place.core * half_rows
-        return pl.ds(pl.multiple_of(at, half_rows), half_rows)
+    def swap_rows(block, dx=0, count=1):
+        first = place.x_at(dx) if count == 1 else 0
+        at = block * feat + (place.core * 4 + first) * few
+        return pl.ds(pl.multiple_of(at, few), count * few)
 
     def swap_copy(src, dst, kind, i, dev):
         return pltpu.make_async_remote_copy(
@@ -511,11 +530,12 @@
         )
 
     def swap_send(parts, kind):
+        own_rows = pl.ds(pl.multiple_of((place.core * 4 + place.x) * few, few), few)
         for i, by in enumerate(peers):
             to = place.block(*by)
             for whole, begin, size in parts:
                 cols = pl.ds(pl.multiple_of(to * size, HEAD_DIM), size)
-                src = whole.at[pl.ds(pl.multiple_of(place.core * half_rows, half_rows), half_rows), cols]
+                src = whole.at[own_rows, cols]
                 dst = pair.at[swap_rows(place.shard), pl.ds(begin, size)]
                 swap_copy(src, dst, kind, i, place.dev(*by)).start()
         for whole, begin, size in parts:
@@ -526,28 +546,32 @@
             )
             copy.start()
 
-    def sibling_copy(ref, kind):
-        return pltpu.make_async_remote_copy(
-            src_ref=ref,
-            dst_ref=ref,
-            send_sem=sibling_sems.at[0, kind],
-            recv_sem=sibling_sems.at[1, kind],
-            device_id=place.rep_dev(0, 0, 1),
-            device_id_type=MESH,
+    def share_copy(ref, kind, i):
+        return swap_copy(
+            ref, ref, kind, 7 + i, place.rep_dev(0, i + 1, 0) if i < 3 else place.rep_dev(0, 0, 1)
         )
 
     def swap_relay(span, kind):
         for i, by in enumerate(peers):
             here = pair.at[swap_rows(place.block(-by[0], -by[1])), span]
             swap_copy(here, here, kind, i, place.dev(*by)).wait_recv()
-            sibling_copy(here, kind).start()
+            for d in range(3):
+                share_copy(here, kind, d).start()
+
+    def swap_share(span, kind):
+        for d in range(3):
+            share_copy(pair.at[pl.ds(0, 7 * few), span], kind, d).wait_recv()
+        for by in peers:
+            here = pair.at[swap_rows(place.block(-by[0], -by[1]), 0, 4), span]
+            share_copy(here, kind, 3).start()
 
     def swap_done(span, kind):
         rows = pl.ds(pl.multiple_of(place.shard * feat, feat), feat)
         mine = pair.at[rows, span]
         pltpu.make_async_copy(mine, mine, sibling_sems.at[2, kind]).wait()
-        others = pair.at[pl.ds(0, 7 * half_rows), span]
-        sibling_copy(others, kind).wait()
+        share_copy(pair.at[pl.ds(0, 7 * 4 * few), span], kind, 3).wait()
+        for d in range(3):
+            share_copy(pair.at[pl.ds(0, 7 * few), span], kind, d).wait_send()
         for i, by in enumerate(peers):
             here = pair.at[swap_rows(place.block(-by[0], -by[1])), span]
             swap_copy(here, here, kind, i, place.dev(*by)).wait_send()
@@ -571,14 +595,15 @@
     sine[...] = jnp.sin(angles) * jnp.where(lane < HEAD_DIM // 2, -1.0, 1.0)
 
     gather_tokens.step_one()
+    swap_relay(qkv_span, 0)
     gather_tokens.step_two()
     gain_share.finish()
     for j in range(8):
         span = slice(j * feat, (j + 1) * feat)
         gain_rows_all[0:2, span] = gain_blocks[j, 0:2, :].astype(f32)
-    swap_relay(qkv_span, 0)
+    gather_tokens.step_three()
+    swap_share(qkv_span, 0)
     swap_send(out_parts, 1)
-    gather_tokens.step_three()
     gather_tokens.step_four()
 
     def normalise(dy):
@@ -598,6 +623,9 @@
     gather_tokens.finish()
     keep_first = pltpu.make_async_copy(second, first_hbm, local_sems.at[3])
     keep_first.start()
+    gather_cot = Gather(place, cot_all, *sems(Gather.COPIES))
+    gather_cot.start()
+    swap_relay(out_span, 1)
     swap_done(qkv_span, 0)
     heads = d_up
     gains_of_head = (query_gain, query_gain, key_gain)
@@ -610,14 +638,12 @@
             lanes = pl.ds(g * HEAD_DIM, HEAD_DIM)
             u = proj[rows, lanes]
             root = lax.rsqrt(jnp.mean(u * u, axis=-1, keepdims=True) + epsilon)
-            u = u * root * gains_of_head[g][...]
+            u = u * root * gains_of_head[g][...].astype(f32)
             heads[rows, lanes] = (u * cosine[rows, :] + swap_halves(u) * sine[rows, :]).astype(low)
         lanes = pl.ds(3 * HEAD_DIM, HEAD_DIM)
         heads[rows, lanes] = proj[rows, lanes].astype(low)
 
-    swap_relay(out_span, 1)
-    gather_cot = Gather(place, cot_all, *sems(Gather.COPIES))
-    gather_cot.start()
+    swap_share(out_span, 1)
     chunk = 256
     for part in range(rows_all // chunk):
         rows = pl.ds(part * chunk, chunk)
@@ -637,7 +663,7 @@
             heads[rows, pl.ds((4 + g) * HEAD_DIM, HEAD_DIM)] = mm(
                 probs, heads[0:seen, 3 * HEAD_DIM : 4 * HEAD_DIM]
             ).astype(low)
-        if part == 1:
+        if part == 2:
             gather_cot.step_one()
     keep_heads = pltpu.make_async_copy(heads, heads_hbm, local_sems.at[4])
     keep_heads.start()
@@ -758,31 +784,25 @@
 
         return load
 
-    gather_second.start()
+    for step in gather_second.steps():
+        step()
+    gather_cot.step_two()
     for load in loads:
         load.wait()
-    feed_forward(own)
-    gather_second.step_one()
-    gather_second.step_two()
-    gather_second.step_three()
-    gather_second.step_four()
-    gather_cot.step_two()
-    feed_forward(place.rows(0, 1))
-    feed_forward(place.rows(0, 3))
     gather_second.own_line()
     gather_cot.step_three()
-    feed_forward(place.rows(0, 2))
+    feed_forward(pl.ds(place.line(0), LINE))
     gather_second.other_line()
     gather_cot.step_four()
     feed_forward(pl.ds(place.line(1), LINE))
-    project_out(1)
-    project_out(0)
     gather_cot.own_line()
     gather_cot.other_line()
     feed_backward(1)
     scatter_back.send_other()
     feed_backward(0)
     scatter_back.send_own()
+    project_out(1)
+    project_out(0)
     weight_grad(w_gate, d_gate, second)
     sum_gate.core_send()
     scatter_back.step_one()
@@ -849,7 +869,10 @@
     gather_branch.step_two()
     sum_up.x_second()
     gather_branch.step_three()
+    sum_down.x_second()
+    sum_gate.y_send()
     gather_branch.step_four()
+    sum_up.y_send()
     gather_branch.own_line()
     for load in loads:
         load.wait()
@@ -863,10 +886,8 @@
 
     into_attention(0)
     gather_branch.other_line()
-    scatter_out.send_other()
-    scatter_out.send_own()
     into_attention(1)
-    sum_down.x_second()
+    sum_down.y_send()
     scatter_back.finish()
     load = pltpu.make_async_copy(first_hbm, part_back, local_sems.at[0])
     load.start()
@@ -892,28 +913,25 @@
             inner = jnp.sum(weights * d_probs, axis=-1, keepdims=True)
             d_scores = (weights * (d_probs - inner)).astype(low)
             back, gain_part = unrotate(
-                rows, mm(d_scores, key[0:seen, :]) * scale, proj[rows, lanes], query_gain[...]
+                rows, mm(d_scores, key[0:seen, :]) * scale, proj[rows, lanes], query_gain[...].astype(f32)
             )
             d_qkv[rows, lanes] = back.astype(low)
             gain_rows = gain_rows + jnp.sum(gain_part, axis=0, keepdims=True)
             d_key[0:seen, :] += mm_tn(d_scores, query[rows, lanes])
             d_value[0:seen, :] += mm_tn(weights.astype(low), d_att[rows, lanes])
         if part == 0:
-            sum_gate.y_send()
+            sum_gate.y_gather(sum_gate.piece(), local_sems.at[3])
         if part == 1:
-            scatter_out.step_one()
-            sum_up.y_send()
-            sum_gate.y_gather(sum_gate.piece(), local_sems.at[3])
+            sum_up.y_gather(sum_up.piece(), local_sems.at[3])
         if part == 2:
-            scatter_out.step_two()
-            sum_down.y_send()
-            sum_up.y_gather(sum_up.piece(), local_sems.at[3])
-            sum_gate.x_gather()
+            sum_down.y_gather(sum_down.piece(), local_sems.at[3])
+            scatter_out.send_other()
+            scatter_out.send_own()
     d_qkv[:, 3 * HEAD_DIM :] = d_value[...].astype(low)
 
     keep_gain(2 * gain_slots, gain_rows)
     lanes = pl.ds(2 * HEAD_DIM, HEAD_DIM)
-    back, gain_part = unrotate(pl.ds(0, rows_all), d_key[...] * scale, proj[:, lanes], key_gain[...])
+    back, gain_part = unrotate(pl.ds(0, rows_all), d_key[...] * scale, proj[:, lanes], key_gain[...].astype(f32))
     d_qkv[:, lanes] = back.astype(low)
     keep_gain(2 * gain_slots + 1, jnp.sum(gain_part, axis=0, keepdims=True))
 
@@ -923,7 +941,7 @@
         sems(RepSum.COPIES),
         pair.at[pl.ds(pl.multiple_of(place.core * rows_all, BLOCK), rows_all)],
         pair.at[pl.ds(pl.multiple_of((1 - place.core) * rows_all, BLOCK), rows_all)],
-        d_up,
+        head_core_landed,
         [head_landed.at[pl.ds(e * BLOCK, BLOCK)] for e in range(2)],
         [head_landed.at[pl.ds((1 + e) * 2 * BLOCK, 2 * BLOCK)] for e in range(2)],
         head_landed.at[pl.ds(6 * BLOCK, BLOCK)],
@@ -944,19 +962,27 @@
             pair[rows, 0 : 4 * HEAD_DIM] = from_first[piece * 16 : piece * 16 + 16, :]
             pair[rows, 4 * HEAD_DIM :] = from_branch[piece * 16 : piece * 16 + 16, :]
 
-    pl.semaphore_signal(
-        core_free_sem, inc=1, device_id=place.rep_dev(0, 0, 1), device_id_type=MESH
-    )
-    pl.semaphore_wait(core_free_sem, 1)
-    sum_attn.core_send()
-    scatter_out.step_three()
-    for half in (0, 1):
-        rows = pl.ds(half * HALF, HALF)
-        result[rows, :] = resid[rows, :] + scatter_out.total(half)
-    scatter_out.finish()
+    gather_branch.finish()
     for by in ((1, 0), (0, 1), (0, 3)):
         pl.semaphore_signal(landing_free, inc=1, device_id=place.dev(*by), device_id_type=MESH)
-    scatter_first = Scatter(place, part_back, *landing, *sems(Scatter.COPIES))
+    sum_attn.core_send()
+    sum_gate.x_gather()
+    sum_up.x_gather()
+    scatter_first = Scatter(
+        place,
+        part_back,
+        Slots(branch, 0, HALF),
+        Slots(branch, 4 * HALF, 32),
+        Slots(branch, 7 * HALF, HALF),
+        branch.at[pl.ds(13 * HALF, HALF)],
+        *sems(Scatter.COPIES),
+    )
+
+    def load_heads():
+        copy = pltpu.make_async_copy(head_core_landed, d_up, local_sems.at[3])
+        copy.start()
+        copy.wait()
+        return d_up
 
     def into_first(dy):
         rows = pl.ds(place.line(dy), LINE)
@@ -980,55 +1006,19 @@
         pl.semaphore_signal(
             heads_free, inc=1, device_id=place.rep_dev(*by), device_id_type=MESH
         )
-    sum_down.y_gather(sum_down.piece(), local_sems.at[3])
-    sum_up.x_gather()
     pl.semaphore_wait(heads_free, 3)
-    sum_attn.x_first()
+    sum_attn.x_first(load_heads)
+    scatter_out.step_one()
     scatter_first.step_one()
+    sum_attn.x_second()
     sum_gate.x_forward()
+    scatter_out.step_two()
+    sum_attn.y_send()
+    sum_down.x_gather()
     scatter_first.step_two()
-    sum_attn.x_second()
-    sum_down.x_gather()
+    scatter_out.step_three()
+    scatter_first.step_three()
     sum_up.x_forward()
-    scatter_first.step_three()
-    sum_gate.x_last()
-    gain_rows = None
-    for half in (1, 0):
-        rows = pl.ds(half * HALF, HALF)
-        d_first = scatter_first.total(half)
-        back, gain_part = rms_backward(tokens[rows, :].astype(f32), gain_one[...], d_first)
-        grad_tokens[rows, :] += back
-        gain_part = jnp.sum(gain_part, axis=0, keepdims=True)
-        gain_rows = gain_part if gain_rows is None else gain_rows + gain_part
-    keep_gain(0, gain_rows)
-
-    gain_net = Net(*sems(9))
-    stages = (
-        [place.dev(0, d) for d in (1, 2, 3)],
-        [place.dev(1, 0)],
-        [place.rep_dev(0, 0, 1)],
-        [place.rep_dev(0, d, 0) for d in (1, 2, 3)],
-        [place.rep_dev(1, 0, 0)],
-    )
-
-    def gain_send(stage):
-        for i, dev in enumerate(stages[stage]):
-            dst = gain_landed.at[3 * stage + i]
-            gain_net.send(f"{stage}.{i}", gain_sums.at[stage], dst, dev, dst)
-
-    def gain_add(stage):
-        total = gain_sums[stage]
-        for i in range(len(stages[stage])):
-            gain_net.wait(f"{stage}.{i}")
-            total = total + gain_landed[3 * stage + i]
-        gain_sums[stage + 1] = total
-
-    gain_send(0)
-    sum_attn.y_send()
-    sum_down.x_forward()
-    gain_add(0)
-    gain_send(1)
-    sum_up.x_last()
     piece = sum_attn.piece()
     swap_net = Net(*sems(7))
     for dy in range(2):
@@ -1042,9 +1032,38 @@
                 swap_net.send(f"{dy}{dz}", src, dst, place.dev(dy, dz), here)
     own_rows = pl.ds(pl.multiple_of(place.shard * 16, 16), 16)
     swapped[own_rows, :] = piece[own_rows, :]
-    gain_add(1)
-    gain_send(2)
-    sum_down.x_last()
+    gain_rows = None
+    for half in (1, 0):
+        rows = pl.ds(half * HALF, HALF)
+        d_first = scatter_first.total(half)
+        back, gain_part = rms_backward(tokens[rows, :].astype(f32), gain_one[...], d_first)
+        grad_tokens[rows, :] += back
+        gain_part = jnp.sum(gain_part, axis=0, keepdims=True)
+        gain_rows = gain_part if gain_rows is None else gain_rows + gain_part
+    keep_gain(0, gain_rows)
+
+    gain_net = Net(*sems(9))
+    stages = (
+        [place.dev(0, d) for d in (1, 2, 3)],
+        [place.dev(1, 0)],
+        [place.rep_dev(0, 0, 1)],
+        [place.rep_dev(0, d, 0) for d in (1, 2, 3)],
+        [place.rep_dev(1, 0, 0)],
+    )
+
+    def gain_send(stage):
+        for i, dev in enumerate(stages[stage]):
+            dst = gain_landed.at[3 * stage + i]
+            gain_net.send(f"{stage}.{i}", gain_sums.at[stage], dst, dev, dst)
+
+    def gain_add(stage):
+        total = gain_sums[stage]
+        for i in range(len(stages[stage])):
+            gain_net.wait(f"{stage}.{i}")
+            total = total + gain_landed[3 * stage + i]
+        gain_sums[stage + 1] = total
+
+    gain_send(0)
     swap_net.finish()
     kv = 8 * HEAD_DIM
     for j in range(8):
@@ -1056,18 +1075,29 @@
             ]
             at += size * kv
     sum_attn.y_gather(assembled, local_sems.at[3])
+    gain_add(0)
+    gain_send(1)
+    for half in (0, 1):
+        rows = pl.ds(half * HALF, HALF)
+        result[rows, :] = resid[rows, :] + scatter_out.total(half)
+    sum_down.x_forward()
+    sum_attn.x_gather()
+    gain_add(1)
+    gain_send(2)
+    sum_gate.x_last()
     gain_add(2)
     gain_send(3)
-    sum_attn.x_gather()
+    sum_up.x_last()
+    sum_attn.x_forward()
     gain_add(3)
     gain_send(4)
-    sum_attn.x_forward()
+    sum_down.x_last()
     sum_attn.x_last()
     gain_add(4)
     gains[...] = gain_sums[5]
 
-    gather_branch.finish()
     scatter_first.finish()
+    scatter_out.finish()
     for one in sums:
         one.finish()
     sum_attn.finish()
@@ -1094,12 +1124,13 @@
             jax.ShapeDtypeStruct((256, 3 * width), low),
             jax.ShapeDtypeStruct((3, hid, width), low),
             jax.ShapeDtypeStruct((3, hid // 2, width), low),
+            jax.ShapeDtypeStruct((rows, 6 * HEAD_DIM), low),
             jax.ShapeDtypeStruct((rows, width), low),
             jax.ShapeDtypeStruct((2 * rows, 6 * HEAD_DIM), low),
             jax.ShapeDtypeStruct((rows, 6 * HEAD_DIM), low),
         ],
-        in_specs=[smem] + [vmem] * 6 + [hbm] * 7,
-        out_specs=[vmem] * 3 + [hbm] * 6,
+        in_specs=[smem] + [vmem] * 7 + [hbm] * 7,
+        out_specs=[vmem] * 3 + [hbm] * 7,
         scratch_shapes=[
             pltpu.VMEM((BLOCK, width), f32),
             pltpu.VMEM((2, width), f32),
@@ -1129,9 +1160,8 @@
             pltpu.VMEM((16, 3 * width), low),
             pltpu.VMEM((6,) + gain_shape, f32),
             pltpu.VMEM((15,) + gain_shape, f32),
-            pltpu.SemaphoreType.DMA((2, 2, 7)),
+            pltpu.SemaphoreType.DMA((2, 2, 11)),
             pltpu.SemaphoreType.DMA((3, 2)),
-            pltpu.SemaphoreType.REGULAR,
             pltpu.SemaphoreType.REGULAR,
             pltpu.SemaphoreType.REGULAR,
             pltpu.SemaphoreType.REGULAR,
@@ -1188,7 +1218,7 @@
         ],
         out_specs=[pl.BlockSpec((tall, width), block_of(which)) for which in range(3)]
         + [pl.BlockSpec((some, size), attn_block) for size in sizes],
-        compiler_params=pltpu.CompilerParams(vmem_limit_bytes=40 << 20),
+        compiler_params=pltpu.CompilerParams(vmem_limit_bytes=60 << 20),
     )(ffn, attn)
 
 
@@ -1212,17 +1242,16 @@
     shards = lax.axis_size("shard")
     feat = width // shards
     my_shard = lax.axis_index("shard")
-    half = HEAD_DIM // 2
-    frequency = theta_base ** (-jnp.arange(half, dtype=f32) * (2.0 / HEAD_DIM))
-    frequency = jnp.concatenate([frequency, frequency])[None]
-    gain_shard = jnp.concatenate([attn_gain[None], mlp_gain[None], jnp.zeros((14, feat), low)])
+    half = np.arange(HEAD_DIM, dtype=np.float64) % (HEAD_DIM // 2)
+    frequency = jnp.asarray(theta_base ** (-half * (2.0 / HEAD_DIM)), f32)[None]
     result, grad_tokens, gains, attn_grads, ffn_grads, *_ = layer_call(
         lengths,
         tokens,
         cotangent,
-        gain_shard,
-        query_gain.astype(f32)[None],
-        key_gain.astype(f32)[None],
+        attn_gain[None],
+        mlp_gain[None],
+        query_gain[None],
+        key_gain[None],
         frequency,
         w_query,
         w_key,

time: 378 us -> 342 us (0.905)
  Pallas kernels: 363 us -> 333 us
  local copies, waits for them, and re-layouts: 11.6 us -> 7.05 us
    pallas_call x1, Pallas kernels: 353 us -> 318 us  [layer_call(): pl.pallas_call(functools.partial(layer_kernel, 1.0 / math.sqrt(HEAD_DIM))...]
    unnamed x10 -> x6, local copies, waits for them, and re-layouts: 7.52 us -> 1.95 us
    pallas_call x1, Pallas kernels: 10.6 us -> 15.8 us  [widen(): pl.pallas_call(widen_kernel, name='widen', grid=(3 * per,), out_shape=[ja...]
where the time goes in v6:
time: 342 us; the launch traced here: 341 us
  Pallas kernels  333 us (97%)
  local copies, waits for them, and re-layouts  7.05 us (2%)
    pallas_call x1, Pallas kernels, layer_call(): pl.pallas_call(functools.partial(layer_kernel, 1.0 / math.sqrt(HEAD_DIM))...  318 us
    pallas_call x1, Pallas kernels, widen(): pl.pallas_call(widen_kernel, name='widen', grid=(3 * per,), out_shape=[ja...  15.8 us

profile of v6, /device:TPU:1, one launch (start us, length us, event | category | flops | bytes accessed | tf_op | source)
XLA Modules:
  0.0 341.2 jit_solution(13748300655413565716)
XLA Ops:
  0.7 1.2 broadcast_in_dim.15.attn_gain
  1.9 1.2 broadcast_in_dim.16.mlp_gain
  3.1 317.6 %layer.1 = (f32[128,2048]{1,0:T(8,128)}, f32[128,2048]{1,0:T(8,128)}, f32[40,128]{1,0:T(8,128)}, bf16[256,6144]{1,0:T(8,128)(2,1)}, bf16[3,768,2048]{2,1,0:T(8,1...) custom-call(s32[1,3]{1,0:T(1,128)} %lengths.1, ...), custom_call_target="tpu_custom_call" | custom-call | flops 35999997952 | bytes 60000000 | tf_op jit(solution)/shard_map/layer/pallas_call | solution.py:1117
  320.7 1.3 fusion
  322.0 1.3 fusion.1
  323.4 0.0 copy-start.1
  323.4 0.0 copy-start
  323.4 15.8 %widen.1 = (f32[768,2048]{1,0:T(8,128)}, f32[768,2048]{1,0:T(8,128)}, f32[768,2048]{1,0:T(8,128)}, f32[256,2048]{1,0:T(8,128)}, f32[256,1024]{1,0:T(8,128)}, /*index=5*/f32[256,1024]{1,0:T(8,128)}, f32[256,2048]{1,0:T(8,128)}) custom-call(bf16[3,768,2048]{2,1,0:T(8,128)(2,1)} %get-tuple-element.27.ffn, bf16[256,6144]{1,0:T(8,128)(2,1)} %get-tuple-element.28.attn), custom_call_target="tpu_custom_call" | custom-call | tf_op jit(solution)/shard_map/widen/pallas_call | solution.py:1209
  339.2 0.0 copy-done.1
  339.2 1.0 copy.30
  340.2 0.0 copy-done
  340.2 1.0 copy.31
Async XLA Ops:
  323.4 15.9 %copy-start.1 = (f32[128,2048]{1,0:T(8,128)S(1)}, f32[128,2048]{1,0:T(8,128)}, u32[]{:S(2)}) copy-start(f32[128,2048]{1,0:T(8,128)} %get-tuple-element.54) | copy-start | bytes 3145732
  323.4 16.8 %copy-start = (f32[128,2048]{1,0:T(8,128)S(1)}, f32[128,2048]{1,0:T(8,128)}, u32[]{:S(2)}) copy-start(f32[128,2048]{1,0:T(8,128)} %get-tuple-element.55) | copy-start | bytes 3145732

commit v7 on v6

--- a/solution.py
+++ b/solution.py
@@ -399,8 +399,7 @@
     lengths,
     tokens,
     cotangent,
-    attn_gain,
-    mlp_gain,
+    gain_shard,
     query_gain,
     key_gain,
     frequency,
@@ -488,10 +487,7 @@
     cot_all[own, :] = cotangent[...].astype(low)
     branch[own, :] = tokens[...]
     feat = w_query_hbm.shape[0]
-    at = lax.broadcasted_iota(jnp.int32, (16, attn_gain.shape[1]), 0)
-    gain_blocks[place.shard] = jnp.where(
-        at == 0, attn_gain[...].astype(f32), mlp_gain[...].astype(f32)
-    ).astype(low)
+    gain_blocks[place.shard] = gain_shard[...]
     place.greet()
 
     gain_share = Net(*sems(7))
@@ -703,7 +699,19 @@
     scatter_attn.finish()
     gather_second = Gather(place, second, *sems(Gather.COPIES))
     gather_branch = Gather(place, branch, *sems(Gather.COPIES))
-    scatter_out = Scatter(place, part_out, *landing, *sems(Scatter.COPIES))
+    left, right = (pl.ds(side * (width // 2), width // 2) for side in range(2))
+    scatter_left, scatter_right = (
+        Scatter(
+            place,
+            part_out.at[:, cols],
+            across.at[:, :, cols],
+            near.at[:, :, :, cols],
+            far.at[:, :, :, cols],
+            last.at[:, cols],
+            *sems(Scatter.COPIES),
+        )
+        for cols in (left, right)
+    )
     scatter_back = Scatter(place, part_back, *landing, *sems(Scatter.COPIES))
 
     def feed_forward(rows):
@@ -888,6 +896,8 @@
     gather_branch.other_line()
     into_attention(1)
     sum_down.y_send()
+    scatter_left.send_other()
+    scatter_left.send_own()
     scatter_back.finish()
     load = pltpu.make_async_copy(first_hbm, part_back, local_sems.at[0])
     load.start()
@@ -919,14 +929,10 @@
             gain_rows = gain_rows + jnp.sum(gain_part, axis=0, keepdims=True)
             d_key[0:seen, :] += mm_tn(d_scores, query[rows, lanes])
             d_value[0:seen, :] += mm_tn(weights.astype(low), d_att[rows, lanes])
-        if part == 0:
+        if part == 1:
             sum_gate.y_gather(sum_gate.piece(), local_sems.at[3])
-        if part == 1:
+        if part == 3:
             sum_up.y_gather(sum_up.piece(), local_sems.at[3])
-        if part == 2:
-            sum_down.y_gather(sum_down.piece(), local_sems.at[3])
-            scatter_out.send_other()
-            scatter_out.send_own()
     d_qkv[:, 3 * HEAD_DIM :] = d_value[...].astype(low)
 
     keep_gain(2 * gain_slots, gain_rows)
@@ -966,8 +972,6 @@
     for by in ((1, 0), (0, 1), (0, 3)):
         pl.semaphore_signal(landing_free, inc=1, device_id=place.dev(*by), device_id_type=MESH)
     sum_attn.core_send()
-    sum_gate.x_gather()
-    sum_up.x_gather()
     scatter_first = Scatter(
         place,
         part_back,
@@ -1006,19 +1010,19 @@
         pl.semaphore_signal(
             heads_free, inc=1, device_id=place.rep_dev(*by), device_id_type=MESH
         )
+    sum_down.y_gather(sum_down.piece(), local_sems.at[3])
+    sum_gate.x_gather()
     pl.semaphore_wait(heads_free, 3)
     sum_attn.x_first(load_heads)
-    scatter_out.step_one()
+    scatter_left.step_one()
+    sum_attn.x_second()
+    scatter_left.step_two()
     scatter_first.step_one()
-    sum_attn.x_second()
+    sum_up.x_gather()
     sum_gate.x_forward()
-    scatter_out.step_two()
     sum_attn.y_send()
-    sum_down.x_gather()
+    scatter_left.step_three()
     scatter_first.step_two()
-    scatter_out.step_three()
-    scatter_first.step_three()
-    sum_up.x_forward()
     piece = sum_attn.piece()
     swap_net = Net(*sems(7))
     for dy in range(2):
@@ -1032,6 +1036,8 @@
                 swap_net.send(f"{dy}{dz}", src, dst, place.dev(dy, dz), here)
     own_rows = pl.ds(pl.multiple_of(place.shard * 16, 16), 16)
     swapped[own_rows, :] = piece[own_rows, :]
+    scatter_first.step_three()
+    sum_down.x_gather()
     gain_rows = None
     for half in (1, 0):
         rows = pl.ds(half * HALF, HALF)
@@ -1046,9 +1052,9 @@
     stages = (
         [place.dev(0, d) for d in (1, 2, 3)],
         [place.dev(1, 0)],
+        [place.rep_dev(1, 0, 0)],
         [place.rep_dev(0, 0, 1)],
         [place.rep_dev(0, d, 0) for d in (1, 2, 3)],
-        [place.rep_dev(1, 0, 0)],
     )
 
     def gain_send(stage):
@@ -1079,25 +1085,34 @@
     gain_send(1)
     for half in (0, 1):
         rows = pl.ds(half * HALF, HALF)
-        result[rows, :] = resid[rows, :] + scatter_out.total(half)
-    sum_down.x_forward()
-    sum_attn.x_gather()
+        result[rows, left] = resid[rows, left] + scatter_left.total(half)
+    sum_up.x_forward()
     gain_add(1)
     gain_send(2)
+    scatter_right.send_other()
+    scatter_right.send_own()
+    sum_attn.x_gather()
     sum_gate.x_last()
     gain_add(2)
     gain_send(3)
-    sum_up.x_last()
+    sum_down.x_forward()
+    scatter_right.step_one()
     sum_attn.x_forward()
     gain_add(3)
     gain_send(4)
+    sum_up.x_last()
+    scatter_right.step_two()
     sum_down.x_last()
     sum_attn.x_last()
+    scatter_right.step_three()
     gain_add(4)
+    for half in (0, 1):
+        rows = pl.ds(half * HALF, HALF)
+        result[rows, right] = resid[rows, right] + scatter_right.total(half)
     gains[...] = gain_sums[5]
 
-    scatter_first.finish()
-    scatter_out.finish()
+    for one in (scatter_first, scatter_left, scatter_right):
+        one.finish()
     for one in sums:
         one.finish()
     sum_attn.finish()
@@ -1112,7 +1127,7 @@
     vmem = pl.BlockSpec(memory_space=pltpu.VMEM)
     smem = pl.BlockSpec(memory_space=pltpu.SMEM)
     hbm = pl.BlockSpec(memory_space=pltpu.HBM)
-    copies = 4 * Gather.COPIES + 4 * Scatter.COPIES + 4 * RepSum.COPIES + 9 + 7 + 7
+    copies = 4 * Gather.COPIES + 5 * Scatter.COPIES + 4 * RepSum.COPIES + 9 + 7 + 7
     gain_shape = (2 * width // HEAD_DIM + 8, HEAD_DIM)
     return pl.pallas_call(
         functools.partial(layer_kernel, 1.0 / math.sqrt(HEAD_DIM)),
@@ -1129,7 +1144,7 @@
             jax.ShapeDtypeStruct((2 * rows, 6 * HEAD_DIM), low),
             jax.ShapeDtypeStruct((rows, 6 * HEAD_DIM), low),
         ],
-        in_specs=[smem] + [vmem] * 7 + [hbm] * 7,
+        in_specs=[smem] + [vmem] * 6 + [hbm] * 7,
         out_specs=[vmem] * 3 + [hbm] * 7,
         scratch_shapes=[
             pltpu.VMEM((BLOCK, width), f32),
@@ -1178,46 +1193,69 @@
     )(lengths, *args)
 
 
-def widen_kernel(ffn, attn, gate, up, down, query, key, value, out):
-    step = pl.program_id(0)
-    per = pl.num_programs(0) // 3
-    wide = ffn[0].astype(f32)
-    for which, ref in enumerate((gate, up, down)):
-
-        @pl.when(step // per == which)
-        def _(ref=ref):
-            ref[...] = wide
-
-    at = 0
-    for ref in (query, key, value, out):
-        ref[...] = attn[:, at : at + ref.shape[1]].astype(f32)
-        at += ref.shape[1]
+def widen_kernel(ffn, attn, *refs):
+    outs, (narrow, narrow_attn, wide, wide_attn, load_sems, store_sems, attn_sems) = refs[:7], refs[7:]
+    slots, tall, _ = wide.shape
+    count = narrow.shape[0] // tall
+    per = count // 3
+    loads = []
+    for i in range(count):
+        rows = pl.ds(i % per * tall, tall)
+        loads.append(
+            pltpu.make_async_copy(
+                ffn.at[i // per, rows], narrow.at[pl.ds(i * tall, tall)], load_sems.at[i]
+            )
+        )
+    first = pltpu.make_async_copy(attn, narrow_attn, load_sems.at[count])
+    first.start()
+    for load in loads:
+        load.start()
+    first.wait()
+    wide_attn[...] = narrow_attn[...].astype(f32)
+    stores, at = [], 0
+    for j, ref in enumerate(outs[3:]):
+        size = ref.shape[1]
+        stores.append(
+            pltpu.make_async_copy(wide_attn.at[:, pl.ds(at, size)], ref, attn_sems.at[j])
+        )
+        stores[-1].start()
+        at += size
+    busy = [None] * slots
+    for i in range(count):
+        loads[i].wait()
+        slot = i % slots
+        if busy[slot] is not None:
+            busy[slot].wait()
+        wide[slot] = narrow[pl.ds(i * tall, tall), :].astype(f32)
+        rows = pl.ds(i % per * tall, tall)
+        busy[slot] = pltpu.make_async_copy(wide.at[slot], outs[i // per].at[rows], store_sems.at[slot])
+        busy[slot].start()
+    for copy in busy + stores:
+        copy.wait()
 
 
 def widen(ffn, attn):
     _, hid, width = ffn.shape
     rows = attn.shape[0]
-    per, tall, some = 3, hid // 3, rows // 8
-
-    def block_of(which):
-        return lambda i: (jnp.clip(i - which * per, 0, per - 1), 0)
-
-    def attn_block(i):
-        return (jnp.minimum(i, 7), 0)
-
+    tall, slots = hid // 3, 6
     sizes = (width, width // 2, width // 2, width)
+    hbm = pl.BlockSpec(memory_space=pltpu.HBM)
     return pl.pallas_call(
         widen_kernel,
         name="widen",
-        grid=(3 * per,),
         out_shape=[jax.ShapeDtypeStruct((hid, width), f32)] * 3
         + [jax.ShapeDtypeStruct((rows, size), f32) for size in sizes],
-        in_specs=[
-            pl.BlockSpec((1, tall, width), lambda i: (i // per, i % per, 0)),
-            pl.BlockSpec((some, 3 * width), attn_block),
+        in_specs=[hbm, hbm],
+        out_specs=[hbm] * 7,
+        scratch_shapes=[
+            pltpu.VMEM((3 * hid, width), low),
+            pltpu.VMEM((rows, 3 * width), low),
+            pltpu.VMEM((slots, tall, width), f32),
+            pltpu.VMEM((rows, 3 * width), f32),
+            pltpu.SemaphoreType.DMA((10,)),
+            pltpu.SemaphoreType.DMA((slots,)),
+            pltpu.SemaphoreType.DMA((4,)),
         ],
-        out_specs=[pl.BlockSpec((tall, width), block_of(which)) for which in range(3)]
-        + [pl.BlockSpec((some, size), attn_block) for size in sizes],
         compiler_params=pltpu.CompilerParams(vmem_limit_bytes=60 << 20),
     )(ffn, attn)
 
@@ -1248,8 +1286,7 @@
         lengths,
         tokens,
         cotangent,
-        attn_gain[None],
-        mlp_gain[None],
+        jnp.concatenate([attn_gain[None], mlp_gain[None], jnp.zeros((14, feat), low)]),
         query_gain[None],
         key_gain[None],
         frequency,

time: 342 us -> 327 us (0.956)
  Pallas kernels: 333 us -> 318 us
    pallas_call x1, Pallas kernels: 318 us -> 306 us  [layer_call(): pl.pallas_call(functools.partial(layer_kernel, 1.0 / math.sqrt(HEAD_DIM))...]
where the time goes in v7:
time: 327 us; the launch traced here: 326 us
  Pallas kernels  318 us (97%)
  local copies, waits for them, and re-layouts  6.01 us (2%)
    pallas_call x1, Pallas kernels, layer_call(): pl.pallas_call(functools.partial(layer_kernel, 1.0 / math.sqrt(HEAD_DIM))...  306 us
    pallas_call x1, Pallas kernels, widen(): pl.pallas_call(widen_kernel, name='widen', out_shape=[jax.ShapeDtypeStruc...  12.6 us

profile of v7, /device:TPU:1, one launch (start us, length us, event | category | flops | bytes accessed | tf_op | source)
XLA Modules:
  0.0 325.8 jit_solution(15758280486817376630)
XLA Ops:
  0.7 0.1 pad.2.clone
  0.7 0.7 broadcast_in_dim.18
  1.4 0.7 broadcast_in_dim.19
  2.1 0.7 maximum_maximum_fusion.gain_shard
  2.7 305.8 %layer.1 = (f32[128,2048]{1,0:T(8,128)}, f32[128,2048]{1,0:T(8,128)}, f32[40,128]{1,0:T(8,128)}, bf16[256,6144]{1,0:T(8,128)(2,1)}, bf16[3,768,2048]{2,1,0:T(8,1...) custom-call(s32[1,3]{1,0:T(1,128)} %lengths.1, ...), custom_call_target="tpu_custom_call" | custom-call | flops 35999997952 | bytes 60000000 | tf_op jit(solution)/shard_map/layer/pallas_call | solution.py:1132
  308.6 1.3 fusion
  309.9 1.3 fusion.1
  311.2 0.0 copy-start.1
  311.2 0.0 copy-start
  311.2 12.6 %widen.1 = (f32[768,2048]{1,0:T(8,128)}, f32[768,2048]{1,0:T(8,128)}, f32[768,2048]{1,0:T(8,128)}, f32[256,2048]{1,0:T(8,128)}, f32[256,1024]{1,0:T(8,128)}, /*index=5*/f32[256,1024]{1,0:T(8,128)}, f32[256,2048]{1,0:T(8,128)}) custom-call(bf16[3,768,2048]{2,1,0:T(8,128)(2,1)} %get-tuple-element.27.ffn, bf16[256,6144]{1,0:T(8,128)(2,1)} %get-tuple-element.28.attn), custom_call_target="tpu_custom_call" | custom-call | tf_op jit(solution)/shard_map/widen/pallas_call | solution.py:1243
  323.8 0.0 copy-done.1
  323.8 1.0 copy.30
  324.8 0.0 copy-done
  324.8 1.0 copy.31
  (1 shorter events, 0.0 us)
Async XLA Ops:
  311.2 12.6 %copy-start.1 = (f32[128,2048]{1,0:T(8,128)S(1)}, f32[128,2048]{1,0:T(8,128)}, u32[]{:S(2)}) copy-start(f32[128,2048]{1,0:T(8,128)} %get-tuple-element.54) | copy-start | bytes 3145732
  311.2 13.6 %copy-start = (f32[128,2048]{1,0:T(8,128)S(1)}, f32[128,2048]{1,0:T(8,128)}, u32[]{:S(2)}) copy-start(f32[128,2048]{1,0:T(8,128)} %get-tuple-element.55) | copy-start | bytes 3145732

commit v8 on v7

--- a/solution.py
+++ b/solution.py
@@ -896,8 +896,6 @@
     gather_branch.other_line()
     into_attention(1)
     sum_down.y_send()
-    scatter_left.send_other()
-    scatter_left.send_own()
     scatter_back.finish()
     load = pltpu.make_async_copy(first_hbm, part_back, local_sems.at[0])
     load.start()
@@ -931,6 +929,8 @@
             d_value[0:seen, :] += mm_tn(weights.astype(low), d_att[rows, lanes])
         if part == 1:
             sum_gate.y_gather(sum_gate.piece(), local_sems.at[3])
+            scatter_left.send_other()
+            scatter_left.send_own()
         if part == 3:
             sum_up.y_gather(sum_up.piece(), local_sems.at[3])
     d_qkv[:, 3 * HEAD_DIM :] = d_value[...].astype(low)
@@ -972,6 +972,8 @@
     for by in ((1, 0), (0, 1), (0, 3)):
         pl.semaphore_signal(landing_free, inc=1, device_id=place.dev(*by), device_id_type=MESH)
     sum_attn.core_send()
+    sum_gate.x_gather()
+    scatter_left.step_one()
     scatter_first = Scatter(
         place,
         part_back,
@@ -1011,18 +1013,49 @@
             heads_free, inc=1, device_id=place.rep_dev(*by), device_id_type=MESH
         )
     sum_down.y_gather(sum_down.piece(), local_sems.at[3])
-    sum_gate.x_gather()
     pl.semaphore_wait(heads_free, 3)
     sum_attn.x_first(load_heads)
-    scatter_left.step_one()
+    scatter_first.step_one()
+    scatter_left.step_two()
     sum_attn.x_second()
-    scatter_left.step_two()
-    scatter_first.step_one()
+    sum_gate.x_forward()
     sum_up.x_gather()
-    sum_gate.x_forward()
-    sum_attn.y_send()
     scatter_left.step_three()
     scatter_first.step_two()
+    scatter_first.step_three()
+    sum_attn.y_send()
+    gain_rows = None
+    for half in (1, 0):
+        rows = pl.ds(half * HALF, HALF)
+        d_first = scatter_first.total(half)
+        back, gain_part = rms_backward(tokens[rows, :].astype(f32), gain_one[...], d_first)
+        grad_tokens[rows, :] += back
+        gain_part = jnp.sum(gain_part, axis=0, keepdims=True)
+        gain_rows = gain_part if gain_rows is None else gain_rows + gain_part
+    keep_gain(0, gain_rows)
+
+    gain_net = Net(*sems(9))
+    stages = (
+        [place.dev(0, d) for d in (1, 2, 3)],
+        [place.dev(1, 0)],
+        [place.rep_dev(1, 0, 0)],
+        [place.rep_dev(0, 0, 1)],
+        [place.rep_dev(0, d, 0) for d in (1, 2, 3)],
+    )
+
+    def gain_send(stage):
+        for i, dev in enumerate(stages[stage]):
+            dst = gain_landed.at[3 * stage + i]
+            gain_net.send(f"{stage}.{i}", gain_sums.at[stage], dst, dev, dst)
+
+    def gain_add(stage):
+        total = gain_sums[stage]
+        for i in range(len(stages[stage])):
+            gain_net.wait(f"{stage}.{i}")
+            total = total + gain_landed[3 * stage + i]
+        gain_sums[stage + 1] = total
+
+    gain_send(0)
     piece = sum_attn.piece()
     swap_net = Net(*sems(7))
     for dy in range(2):
@@ -1036,40 +1069,10 @@
                 swap_net.send(f"{dy}{dz}", src, dst, place.dev(dy, dz), here)
     own_rows = pl.ds(pl.multiple_of(place.shard * 16, 16), 16)
     swapped[own_rows, :] = piece[own_rows, :]
-    scatter_first.step_three()
+    sum_up.x_forward()
     sum_down.x_gather()
-    gain_rows = None
-    for half in (1, 0):
-        rows = pl.ds(half * HALF, HALF)
-        d_first = scatter_first.total(half)
-        back, gain_part = rms_backward(tokens[rows, :].astype(f32), gain_one[...], d_first)
-        grad_tokens[rows, :] += back
-        gain_part = jnp.sum(gain_part, axis=0, keepdims=True)
-        gain_rows = gain_part if gain_rows is None else gain_rows + gain_part
-    keep_gain(0, gain_rows)
-
-    gain_net = Net(*sems(9))
-    stages = (
-        [place.dev(0, d) for d in (1, 2, 3)],
-        [place.dev(1, 0)],
-        [place.rep_dev(1, 0, 0)],
-        [place.rep_dev(0, 0, 1)],
-        [place.rep_dev(0, d, 0) for d in (1, 2, 3)],
-    )
-
-    def gain_send(stage):
-        for i, dev in enumerate(stages[stage]):
-            dst = gain_landed.at[3 * stage + i]
-            gain_net.send(f"{stage}.{i}", gain_sums.at[stage], dst, dev, dst)
-
-    def gain_add(stage):
-        total = gain_sums[stage]
-        for i in range(len(stages[stage])):
-            gain_net.wait(f"{stage}.{i}")
-            total = total + gain_landed[3 * stage + i]
-        gain_sums[stage + 1] = total
-
-    gain_send(0)
+    gain_add(0)
+    gain_send(1)
     swap_net.finish()
     kv = 8 * HEAD_DIM
     for j in range(8):
@@ -1081,30 +1084,27 @@
             ]
             at += size * kv
     sum_attn.y_gather(assembled, local_sems.at[3])
-    gain_add(0)
-    gain_send(1)
-    for half in (0, 1):
-        rows = pl.ds(half * HALF, HALF)
-        result[rows, left] = resid[rows, left] + scatter_left.total(half)
-    sum_up.x_forward()
     gain_add(1)
     gain_send(2)
     scatter_right.send_other()
     scatter_right.send_own()
+    for half in (0, 1):
+        rows = pl.ds(half * HALF, HALF)
+        result[rows, left] = resid[rows, left] + scatter_left.total(half)
+    sum_gate.x_last()
     sum_attn.x_gather()
-    sum_gate.x_last()
     gain_add(2)
     gain_send(3)
     sum_down.x_forward()
     scatter_right.step_one()
+    sum_up.x_last()
     sum_attn.x_forward()
     gain_add(3)
     gain_send(4)
-    sum_up.x_last()
     scatter_right.step_two()
     sum_down.x_last()
+    scatter_right.step_three()
     sum_attn.x_last()
-    scatter_right.step_three()
     gain_add(4)
     for half in (0, 1):
         rows = pl.ds(half * HALF, HALF)

time: 327 us -> 329 us (level)
  no operation moved by 1% of the time
where the time goes in v8:
time: 329 us; the launch traced here: 328 us
  Pallas kernels  321 us (98%)
  local copies, waits for them, and re-layouts  6.01 us (2%)
    pallas_call x1, Pallas kernels, layer_call(): pl.pallas_call(functools.partial(layer_kernel, 1.0 / math.sqrt(HEAD_DIM))...  308 us
    pallas_call x1, Pallas kernels, widen(): pl.pallas_call(widen_kernel, name='widen', out_shape=[jax.ShapeDtypeStruc...  12.6 us

profile of v8, /device:TPU:1, one launch (start us, length us, event | category | flops | bytes accessed | tf_op | source)
XLA Modules:
  0.0 328.2 jit_solution(6901466514095391883)
XLA Ops:
  0.7 0.1 pad.2.clone
  0.7 0.7 broadcast_in_dim.18
  1.4 0.7 broadcast_in_dim.19
  2.1 0.7 maximum_maximum_fusion.gain_shard
  2.7 308.3 %layer.1 = (f32[128,2048]{1,0:T(8,128)}, f32[128,2048]{1,0:T(8,128)}, f32[40,128]{1,0:T(8,128)}, bf16[256,6144]{1,0:T(8,128)(2,1)}, bf16[3,768,2048]{2,1,0:T(8,1...) custom-call(s32[1,3]{1,0:T(1,128)} %lengths.1, ...), custom_call_target="tpu_custom_call" | custom-call | flops 35999997952 | bytes 60000000 | tf_op jit(solution)/shard_map/layer/pallas_call | solution.py:1132
  311.0 1.3 fusion
  312.4 1.3 fusion.1
  313.7 0.0 copy-start.1
  313.7 0.0 copy-start
  313.7 12.6 %widen.1 = (f32[768,2048]{1,0:T(8,128)}, f32[768,2048]{1,0:T(8,128)}, f32[768,2048]{1,0:T(8,128)}, f32[256,2048]{1,0:T(8,128)}, f32[256,1024]{1,0:T(8,128)}, /*index=5*/f32[256,1024]{1,0:T(8,128)}, f32[256,2048]{1,0:T(8,128)}) custom-call(bf16[3,768,2048]{2,1,0:T(8,128)(2,1)} %get-tuple-element.27.ffn, bf16[256,6144]{1,0:T(8,128)(2,1)} %get-tuple-element.28.attn), custom_call_target="tpu_custom_call" | custom-call | tf_op jit(solution)/shard_map/widen/pallas_call | solution.py:1243
  326.3 0.0 copy-done.1
  326.3 1.0 copy.30
  327.3 0.0 copy-done
  327.3 1.0 copy.31
  (1 shorter events, 0.0 us)
Async XLA Ops:
  313.7 12.6 %copy-start.1 = (f32[128,2048]{1,0:T(8,128)S(1)}, f32[128,2048]{1,0:T(8,128)}, u32[]{:S(2)}) copy-start(f32[128,2048]{1,0:T(8,128)} %get-tuple-element.54) | copy-start | bytes 3145732
  313.7 13.6 %copy-start = (f32[128,2048]{1,0:T(8,128)S(1)}, f32[128,2048]{1,0:T(8,128)}, u32[]{:S(2)}) copy-start(f32[128,2048]{1,0:T(8,128)} %get-tuple-element.55) | copy-start | bytes 3145732

commit v9 on v8

--- a/solution.py
+++ b/solution.py
@@ -1024,38 +1024,6 @@
     scatter_first.step_two()
     scatter_first.step_three()
     sum_attn.y_send()
-    gain_rows = None
-    for half in (1, 0):
-        rows = pl.ds(half * HALF, HALF)
-        d_first = scatter_first.total(half)
-        back, gain_part = rms_backward(tokens[rows, :].astype(f32), gain_one[...], d_first)
-        grad_tokens[rows, :] += back
-        gain_part = jnp.sum(gain_part, axis=0, keepdims=True)
-        gain_rows = gain_part if gain_rows is None else gain_rows + gain_part
-    keep_gain(0, gain_rows)
-
-    gain_net = Net(*sems(9))
-    stages = (
-        [place.dev(0, d) for d in (1, 2, 3)],
-        [place.dev(1, 0)],
-        [place.rep_dev(1, 0, 0)],
-        [place.rep_dev(0, 0, 1)],
-        [place.rep_dev(0, d, 0) for d in (1, 2, 3)],
-    )
-
-    def gain_send(stage):
-        for i, dev in enumerate(stages[stage]):
-            dst = gain_landed.at[3 * stage + i]
-            gain_net.send(f"{stage}.{i}", gain_sums.at[stage], dst, dev, dst)
-
-    def gain_add(stage):
-        total = gain_sums[stage]
-        for i in range(len(stages[stage])):
-            gain_net.wait(f"{stage}.{i}")
-            total = total + gain_landed[3 * stage + i]
-        gain_sums[stage + 1] = total
-
-    gain_send(0)
     piece = sum_attn.piece()
     swap_net = Net(*sems(7))
     for dy in range(2):
@@ -1071,8 +1039,6 @@
     swapped[own_rows, :] = piece[own_rows, :]
     sum_up.x_forward()
     sum_down.x_gather()
-    gain_add(0)
-    gain_send(1)
     swap_net.finish()
     kv = 8 * HEAD_DIM
     for j in range(8):
@@ -1084,6 +1050,41 @@
             ]
             at += size * kv
     sum_attn.y_gather(assembled, local_sems.at[3])
+    gain_rows = None
+    for half in (1, 0):
+        rows = pl.ds(half * HALF, HALF)
+        d_first = scatter_first.total(half)
+        back, gain_part = rms_backward(tokens[rows, :].astype(f32), gain_one[...], d_first)
+        grad_tokens[rows, :] += back
+        gain_part = jnp.sum(gain_part, axis=0, keepdims=True)
+        gain_rows = gain_part if gain_rows is None else gain_rows + gain_part
+    keep_gain(0, gain_rows)
+
+    gain_net = Net(*sems(9))
+    stages = (
+        [place.dev(0, d) for d in (1, 2, 3)],
+        [place.dev(1, 0)],
+        [place.rep_dev(1, 0, 0)],
+        [place.rep_dev(0, 0, 1)],
+        [place.rep_dev(0, d, 0) for d in (1, 2, 3)],
+    )
+
+    def gain_send(stage):
+        for i, dev in enumerate(stages[stage]):
+            dst = gain_landed.at[3 * stage + i]
+            gain_net.send(f"{stage}.{i}", gain_sums.at[stage], dst, dev, dst)
+
+    def gain_add(stage):
+        total = gain_sums[stage]
+        for i in range(len(stages[stage])):
+            gain_net.wait(f"{stage}.{i}")
+            total = total + gain_landed[3 * stage + i]
+        gain_sums[stage + 1] = total
+
+    gain_send(0)
+    gain_add(0)
+    gain_send(1)
+    sum_attn.x_gather()
     gain_add(1)
     gain_send(2)
     scatter_right.send_other()
@@ -1092,7 +1093,6 @@
         rows = pl.ds(half * HALF, HALF)
         result[rows, left] = resid[rows, left] + scatter_left.total(half)
     sum_gate.x_last()
-    sum_attn.x_gather()
     gain_add(2)
     gain_send(3)
     sum_down.x_forward()

time: 329 us -> 328 us (level)
  no operation moved by 1% of the time
where the time goes in v9:
time: 328 us
  Pallas kernels  321 us (98%)
  local copies, waits for them, and re-layouts  6.01 us (2%)
    pallas_call x1, Pallas kernels, layer_call(): pl.pallas_call(functools.partial(layer_kernel, 1.0 / math.sqrt(HEAD_DIM))...  308 us
    pallas_call x1, Pallas kernels, widen(): pl.pallas_call(widen_kernel, name='widen', out_shape=[jax.ShapeDtypeStruc...  12.6 us

profile of v9, /device:TPU:1, one launch (start us, length us, event | category | flops | bytes accessed | tf_op | source)
XLA Modules:
  0.0 328.0 jit_solution(11293874302082903364)
XLA Ops:
  0.7 0.1 pad.2.clone
  0.7 0.7 broadcast_in_dim.18
  1.4 0.7 broadcast_in_dim.19
  2.1 0.7 maximum_maximum_fusion.gain_shard
  2.7 308.1 %layer.1 = (f32[128,2048]{1,0:T(8,128)}, f32[128,2048]{1,0:T(8,128)}, f32[40,128]{1,0:T(8,128)}, bf16[256,6144]{1,0:T(8,128)(2,1)}, bf16[3,768,2048]{2,1,0:T(8,1...) custom-call(s32[1,3]{1,0:T(1,128)} %lengths.1, ...), custom_call_target="tpu_custom_call" | custom-call | flops 35999997952 | bytes 60000000 | tf_op jit(solution)/shard_map/layer/pallas_call | solution.py:1132
  310.8 1.3 fusion
  312.2 1.3 fusion.1
  313.5 0.0 copy-start.1
  313.5 0.0 copy-start
  313.5 12.6 %widen.1 = (f32[768,2048]{1,0:T(8,128)}, f32[768,2048]{1,0:T(8,128)}, f32[768,2048]{1,0:T(8,128)}, f32[256,2048]{1,0:T(8,128)}, f32[256,1024]{1,0:T(8,128)}, /*index=5*/f32[256,1024]{1,0:T(8,128)}, f32[256,2048]{1,0:T(8,128)}) custom-call(bf16[3,768,2048]{2,1,0:T(8,128)(2,1)} %get-tuple-element.27.ffn, bf16[256,6144]{1,0:T(8,128)(2,1)} %get-tuple-element.28.attn), custom_call_target="tpu_custom_call" | custom-call | tf_op jit(solution)/shard_map/widen/pallas_call | solution.py:1243
  326.1 0.0 copy-done.1
  326.1 1.0 copy.30
  327.0 0.0 copy-done
  327.0 1.0 copy.31
  (1 shorter events, 0.0 us)
Async XLA Ops:
  313.5 12.6 %copy-start.1 = (f32[128,2048]{1,0:T(8,128)S(1)}, f32[128,2048]{1,0:T(8,128)}, u32[]{:S(2)}) copy-start(f32[128,2048]{1,0:T(8,128)} %get-tuple-element.54) | copy-start | bytes 3145732
  313.5 13.6 %copy-start = (f32[128,2048]{1,0:T(8,128)S(1)}, f32[128,2048]{1,0:T(8,128)}, u32[]{:S(2)}) copy-start(f32[128,2048]{1,0:T(8,128)} %get-tuple-element.55) | copy-start | bytes 3145732

commit v10 on v9

--- a/solution.py
+++ b/solution.py
@@ -1024,6 +1024,8 @@
     scatter_first.step_two()
     scatter_first.step_three()
     sum_attn.y_send()
+    sum_up.x_forward()
+    sum_down.x_gather()
     piece = sum_attn.piece()
     swap_net = Net(*sems(7))
     for dy in range(2):
@@ -1037,8 +1039,6 @@
                 swap_net.send(f"{dy}{dz}", src, dst, place.dev(dy, dz), here)
     own_rows = pl.ds(pl.multiple_of(place.shard * 16, 16), 16)
     swapped[own_rows, :] = piece[own_rows, :]
-    sum_up.x_forward()
-    sum_down.x_gather()
     swap_net.finish()
     kv = 8 * HEAD_DIM
     for j in range(8):

time: 328 us -> 326 us (level)
  no operation moved by 1% of the time
where the time goes in v10:
time: 326 us
  Pallas kernels  318 us (98%)
  local copies, waits for them, and re-layouts  6.01 us (2%)
    pallas_call x1, Pallas kernels, layer_call(): pl.pallas_call(functools.partial(layer_kernel, 1.0 / math.sqrt(HEAD_DIM))...  306 us
    pallas_call x1, Pallas kernels, widen(): pl.pallas_call(widen_kernel, name='widen', out_shape=[jax.ShapeDtypeStruc...  12.6 us

profile of v10, /device:TPU:1, one launch (start us, length us, event | category | flops | bytes accessed | tf_op | source)
XLA Modules:
  0.0 325.6 jit_solution(18412967617377428100)
XLA Ops:
  0.7 0.1 pad.2.clone
  0.7 0.7 broadcast_in_dim.18
  1.4 0.7 broadcast_in_dim.19
  2.1 0.7 maximum_maximum_fusion.gain_shard
  2.7 305.7 %layer.1 = (f32[128,2048]{1,0:T(8,128)}, f32[128,2048]{1,0:T(8,128)}, f32[40,128]{1,0:T(8,128)}, bf16[256,6144]{1,0:T(8,128)(2,1)}, bf16[3,768,2048]{2,1,0:T(8,1...) custom-call(s32[1,3]{1,0:T(1,128)} %lengths.1, ...), custom_call_target="tpu_custom_call" | custom-call | flops 35999997952 | bytes 60000000 | tf_op jit(solution)/shard_map/layer/pallas_call | solution.py:1132
  308.4 1.3 fusion
  309.8 1.3 fusion.1
  311.1 0.0 copy-start.1
  311.1 0.0 copy-start
  311.1 12.6 %widen.1 = (f32[768,2048]{1,0:T(8,128)}, f32[768,2048]{1,0:T(8,128)}, f32[768,2048]{1,0:T(8,128)}, f32[256,2048]{1,0:T(8,128)}, f32[256,1024]{1,0:T(8,128)}, /*index=5*/f32[256,1024]{1,0:T(8,128)}, f32[256,2048]{1,0:T(8,128)}) custom-call(bf16[3,768,2048]{2,1,0:T(8,128)(2,1)} %get-tuple-element.27.ffn, bf16[256,6144]{1,0:T(8,128)(2,1)} %get-tuple-element.28.attn), custom_call_target="tpu_custom_call" | custom-call | tf_op jit(solution)/shard_map/widen/pallas_call | solution.py:1243
  323.7 0.0 copy-done.1
  323.7 1.0 copy.30
  324.7 0.0 copy-done
  324.7 1.0 copy.31
  (1 shorter events, 0.0 us)
Async XLA Ops:
  311.1 12.6 %copy-start.1 = (f32[128,2048]{1,0:T(8,128)S(1)}, f32[128,2048]{1,0:T(8,128)}, u32[]{:S(2)}) copy-start(f32[128,2048]{1,0:T(8,128)} %get-tuple-element.54) | copy-start | bytes 3145732
  311.1 13.6 %copy-start = (f32[128,2048]{1,0:T(8,128)S(1)}, f32[128,2048]{1,0:T(8,128)}, u32[]{:S(2)}) copy-start(f32[128,2048]{1,0:T(8,128)} %get-tuple-element.55) | copy-start | bytes 3145732
